TPU v7x, 256 devices: a whole 4x4x8 slice. The times are simulated.
256 devices in a mesh: grp: 8 (over y, x_lo), blk: 32 (over z, x_hi, core).
Axes of the slice: x: 4 (x_hi: 2, x_lo: 2; x = x_hi * 2 + x_lo), y: 4, z: 8, core: 2. Of those that a mesh axis runs over, the one named last changes fastest.
Arguments:
- sources: bfloat16 [32768, 768], P('blk'), may hold values from -1 to 1
- targets: bfloat16 [16384, 768], P(('grp', 'blk')), may hold values from -1 to 1
- potential_in: float32 [16384], P(('grp', 'blk')), may hold values from -6 to 6
- source_logw: float32 [32768], P('blk'), may hold values from -12 to 12
- target_logw: float32 [16384], P(('grp', 'blk')), may hold values from -12 to 12
Outputs:
- source_potential: float32 [32768], P('blk')
- potential_out: float32 [16384], P(('grp', 'blk'))
All inputs are finite; a program needn't handle non-finite values.
Results may differ from a plain program's by a relative error of at most 0.0003.
Values may be sent and summed in bfloat16 or wider, within the bound.
No kernel may reach another device: no remote copies, remote signals or barrier semaphores. Data moves between devices by JAX's collectives and lax.ppermute only.
A program may use at most 64 MiB of HBM per device.

v0:
```python
import jax
import jax.numpy as jnp
from jax import lax
from jax.sharding import PartitionSpec as P

EPSILON = 0.05


def from_behind(value, axis, steps):
    count = lax.axis_size(axis)
    pairs = [(source, (source + steps) % count) for source in range(count)]
    return lax.ppermute(value, axis, pairs)


def combine(first, second):
    peak = jnp.maximum(first[0], second[0])
    total = first[1] * jnp.exp(first[0] - peak) + second[1] * jnp.exp(second[0] - peak)
    return (peak, total)


def row_terms(sources, src_sq, group, group_pot, group_logw):
    cross = lax.dot_general(
        sources, group, (((1,), (1,)), ((), ())), preferred_element_type=jnp.float32
    )
    group_sq = jnp.sum(jnp.square(group.astype(jnp.float32)), axis=1)
    scores = (
        group_logw[None, :]
        + (group_pot[None, :] - group_sq[None, :] + 2.0 * cross - src_sq[:, None]) / EPSILON
    )
    peak = jnp.max(scores, axis=1)
    return (peak, jnp.sum(jnp.exp(scores - peak[:, None]), axis=1))


def column_terms(sources, src_sq, source_pot, source_logw, group):
    cross = lax.dot_general(
        group, sources, (((1,), (1,)), ((), ())), preferred_element_type=jnp.float32
    )
    group_sq = jnp.sum(jnp.square(group.astype(jnp.float32)), axis=1)
    scores = (
        source_logw[None, :]
        + (source_pot[None, :] - src_sq[None, :] + 2.0 * cross - group_sq[:, None]) / EPSILON
    )
    peak = jnp.max(scores, axis=1)
    return (peak, jnp.sum(jnp.exp(scores - peak[:, None]), axis=1))


def advance(group):
    return from_behind(group, "blk", 1)


def on_device(sources, targets, potential_in, source_logw, target_logw):
    src_sq = jnp.sum(jnp.square(sources.astype(jnp.float32)), axis=1)
    cycle_size = lax.axis_size("blk")

    def first_step(index, carry):
        acc, group, group_pot, group_logw = carry
        group = advance(group)
        group_pot, group_logw = from_behind((group_pot, group_logw), "blk", 1)
        acc = combine(acc, row_terms(sources, src_sq, group, group_pot, group_logw))
        return (acc, group, group_pot, group_logw)

    start = row_terms(sources, src_sq, targets, potential_in, target_logw)
    acc = lax.fori_loop(0, cycle_size - 1, first_step, (start, targets, potential_in, target_logw))[
        0
    ]
    peak, total = acc
    highest = lax.pmax(peak, "grp")
    total = lax.psum(total * jnp.exp(peak - highest), "grp")
    peak = highest
    source_potential = -EPSILON * (peak + jnp.log(total))

    def second_step(index, carry):
        totals, group = carry
        group = advance(group)
        totals = from_behind((totals[0], totals[1]), "blk", 1)
        totals = combine(
            totals, column_terms(sources, src_sq, source_potential, source_logw, group)
        )
        return (totals, group)

    begin = column_terms(sources, src_sq, source_potential, source_logw, targets)
    totals = lax.fori_loop(0, cycle_size - 1, second_step, (begin, targets))[0]
    col_peak, col_total = from_behind((totals[0], totals[1]), "blk", 1)
    potential_out = -EPSILON * (col_peak + jnp.log(col_total))
    return (source_potential, potential_out)


def solution(mesh):
    in_specs = (
        P("blk", None),
        P(("grp", "blk"), None),
        P(("grp", "blk")),
        P("blk"),
        P(("grp", "blk")),
    )
    out_specs = (P("blk"), P(("grp", "blk")))
    return jax.shard_map(
        on_device, mesh=mesh, in_specs=in_specs, out_specs=out_specs, check_vma=False
    )
```

profile of v0, /device:TPU:1, one launch (start us, length us, event | category | flops | bytes accessed | tf_op | source)
XLA Modules:
  0.0 593.9 jit_solution(1503230873738883433)
XLA Ops:
  5.6 272.8 %while.34 = (s32[]{:T(128)}, f32[1024]{0:T(1024)S(1)}, f32[1024]{0:T(1024)S(1)}, bf16[64,768]{1,0:T(8,128)(2,1)S(1)}, f32[64]{0:T(128)S(1)}, /*index=5*/f32[64]{...) while((s32[]{:T(128)}, f32[1024]{0:T(1024)S(1)}, f32[1024]{0:T(1024)S(1)}, ...), condition=%wide.region_8.0_spmd, body=%wide.region_4.0_spmd.sunk | while | flops 101601280 | bytes 2933973 | solution.py:63
  5.6 4.2 collective-permute-start.1
  13.5 3.8 collective-permute-start.1
  17.4 3.9 collective-permute-start.2
  30.6 3.8 collective-permute-start.1
  34.5 3.9 collective-permute-start.2
  40.1 3.8 collective-permute-start.1
  47.8 3.8 collective-permute-start.1
  57.2 3.8 collective-permute-start.1
  65.9 3.8 collective-permute-start.1
  70.3 4.6 collective-permute-start.2
  85.4 3.8 collective-permute-start.1
  94.2 3.8 collective-permute-start.1
  103.0 3.8 collective-permute-start.1
  111.7 3.8 collective-permute-start.1
  120.5 3.8 collective-permute-start.1
  138.0 3.8 collective-permute-start.1
  146.8 3.8 collective-permute-start.1
  155.6 3.8 collective-permute-start.1
  164.4 3.8 collective-permute-start.1
  278.4 15.3 %pmax.7 = f32[1024]{0:T(1024)S(1)} all-reduce(f32[1024]{0:T(1024)S(1)} %get-tuple-element.137), channel_id=1, replica_groups=mesh['grp'=8,'blk'=32] {'grp'}, use_global_device_ids=true, to_apply=%region_9.0 | all-reduce | flops 1024 | bytes 8192 | tf_op jit(solution)/shard_map/pmax | solution.py:67
  293.7 12.6 %psum.7 = f32[1024]{0:T(1024)S(1)} all-reduce(f32[1024]{0:T(1024)S(1)} %exponential_multiply_fusion), channel_id=1, replica_groups=mesh['grp'=8,'blk'=32] {'grp'}, use_global_device_ids=true, to_apply=%region_10.0 | all-reduce | flops 1024 | bytes 8192 | tf_op jit(solution)/shard_map/psum | solution.py:68
  307.8 277.9 %while.35 = (s32[]{:T(128)}, f32[64]{0:T(128)S(1)}, f32[64]{0:T(128)S(1)}, bf16[64,768]{1,0:T(8,128)(2,1)S(1)}, f32[1024]{0:T(1024)S(1)}, /*index=5*/f32[1,1024]...) while((s32[]{:T(128)}, f32[64]{0:T(128)S(1)}, f32[64]{0:T(128)S(1)}, bf16[64,768]{1,0:T(8,128)(2,1)S(1)}, ...), condition=%wide.region_17.18_spmd, body=%wide.region_13.17_spmd.sunk | while | flops 101335232 | bytes 2896845 | solution.py:82
  307.8 11.7 %collective-permute-start.3 = (bf16[64,768]{1,0:T(8,128)(2,1)S(1)}, bf16[64,768]{1,0:T(8,128)(2,1)S(1)}, u32[]{:S(2)}, u32[]{:S(2)}) collective-permute-start(bf16[64,768]{1,0:T(8,128)(2,1)S(1)} %get-tuple-element.331), channel_id=1, source_target_pairs={{0,1},{1,2},{2,3},{3,4},{4,5},{5,6},{6,7},{7,8},{8,9},{9,10},{10,1... | collective-permute-start | bytes 294920 | tf_op jit(solution)/shard_map/while/body/eval_jaxpr/ppermute | solution.py:12
  382.6 4.2 collective-permute-start.5
  391.5 4.2 collective-permute-start.5
  400.3 4.2 collective-permute-start.5
  409.2 4.2 collective-permute-start.5
  418.0 4.2 collective-permute-start.5
  426.9 4.2 collective-permute-start.5
  435.7 4.2 collective-permute-start.5
  444.6 4.2 collective-permute-start.5
  453.4 4.2 collective-permute-start.5
  462.3 4.2 collective-permute-start.5
  471.1 4.2 collective-permute-start.5
  480.0 4.2 collective-permute-start.5
  488.8 4.2 collective-permute-start.5
  497.7 4.2 collective-permute-start.5
  506.5 4.2 collective-permute-start.5
  515.4 4.2 collective-permute-start.5
  524.2 4.2 collective-permute-start.5
  533.1 4.2 collective-permute-start.5
  541.9 4.2 collective-permute-start.5
  550.8 4.2 collective-permute-start.5
  559.6 4.2 collective-permute-start.5
  568.5 4.2 collective-permute-start.5
  577.3 4.2 collective-permute-start.5
  586.2 7.2 %collective-permute-done.6 = f32[64]{0:T(128)S(1)} collective-permute-done((f32[64]{0:T(128)S(1)}, f32[64]{0:T(128)S(1)}, u32[]{:S(2)}, u32[]{:S(2)}) %collective-permute-start.6) | collective-permute-done | bytes 288 | tf_op jit(solution)/shard_map/ppermute | solution.py:12
  (753 shorter events, 373.0 us)
Async XLA Ops:
  13.5 8.6 %collective-permute-start.1 = (bf16[64,768]{1,0:T(8,128)(2,1)S(1)}, bf16[64,768]{1,0:T(8,128)(2,1)S(1)}, u32[]{:S(2)}, u32[]{:S(2)}) collective-permute-start(bf16[64,768]{1,0:T(8,128)(2,1)S(1)} %get-tuple-element.305), channel_id=1, source_target_pairs={{0,1},{1,2},{2,3},{3,4},{4,5},{5,6},{6,7},{7,8},{8,9},{9,10},{10,1... | collective-permute-start | bytes 294920 | tf_op jit(solution)/shard_map/while/body/eval_jaxpr/ppermute | solution.py:12
  30.6 8.5 %collective-permute-start.1 = (bf16[64,768]{1,0:T(8,128)(2,1)S(1)}, bf16[64,768]{1,0:T(8,128)(2,1)S(1)}, u32[]{:S(2)}, u32[]{:S(2)}) collective-permute-start(bf16[64,768]{1,0:T(8,128)(2,1)S(1)} %get-tuple-element.305), channel_id=1, source_target_pairs={{0,1},{1,2},{2,3},{3,4},{4,5},{5,6},{6,7},{7,8},{8,9},{9,10},{10,1... | collective-permute-start | bytes 294920 | tf_op jit(solution)/shard_map/while/body/eval_jaxpr/ppermute | solution.py:12
  47.8 8.4 %collective-permute-start.1 = (bf16[64,768]{1,0:T(8,128)(2,1)S(1)}, bf16[64,768]{1,0:T(8,128)(2,1)S(1)}, u32[]{:S(2)}, u32[]{:S(2)}) collective-permute-start(bf16[64,768]{1,0:T(8,128)(2,1)S(1)} %get-tuple-element.305), channel_id=1, source_target_pairs={{0,1},{1,2},{2,3},{3,4},{4,5},{5,6},{6,7},{7,8},{8,9},{9,10},{10,1... | collective-permute-start | bytes 294920 | tf_op jit(solution)/shard_map/while/body/eval_jaxpr/ppermute | solution.py:12
  65.9 9.8 %collective-permute-start.1 = (bf16[64,768]{1,0:T(8,128)(2,1)S(1)}, bf16[64,768]{1,0:T(8,128)(2,1)S(1)}, u32[]{:S(2)}, u32[]{:S(2)}) collective-permute-start(bf16[64,768]{1,0:T(8,128)(2,1)S(1)} %get-tuple-element.305), channel_id=1, source_target_pairs={{0,1},{1,2},{2,3},{3,4},{4,5},{5,6},{6,7},{7,8},{8,9},{9,10},{10,1... | collective-permute-start | bytes 294920 | tf_op jit(solution)/shard_map/while/body/eval_jaxpr/ppermute | solution.py:12
  307.8 14.3 %collective-permute-start.3 = (bf16[64,768]{1,0:T(8,128)(2,1)S(1)}, bf16[64,768]{1,0:T(8,128)(2,1)S(1)}, u32[]{:S(2)}, u32[]{:S(2)}) collective-permute-start(bf16[64,768]{1,0:T(8,128)(2,1)S(1)} %get-tuple-element.331), channel_id=1, source_target_pairs={{0,1},{1,2},{2,3},{3,4},{4,5},{5,6},{6,7},{7,8},{8,9},{9,10},{10,1... | collective-permute-start | bytes 294920 | tf_op jit(solution)/shard_map/while/body/eval_jaxpr/ppermute | solution.py:12
  382.5 8.5 %collective-permute-start.4 = (f32[64]{0:T(128)S(1)}, f32[64]{0:T(128)S(1)}, u32[]{:S(2)}, u32[]{:S(2)}) collective-permute-start(f32[64]{0:T(128)S(1)} %get-tuple-element.330), channel_id=1, source_target_pairs={{0,1},{1,2},{2,3},{3,4},{4,5},{5,6},{6,7},{7,8},{8,9},{9,10},{10,1... | collective-permute-start | bytes 776 | tf_op jit(solution)/shard_map/while/body/eval_jaxpr/ppermute | solution.py:12
  382.6 8.4 %collective-permute-start.5 = (f32[64]{0:T(128)S(1)}, f32[64]{0:T(128)S(1)}, u32[]{:S(2)}, u32[]{:S(2)}) collective-permute-start(f32[64]{0:T(128)S(1)} %get-tuple-element.329), channel_id=1, source_target_pairs={{0,1},{1,2},{2,3},{3,4},{4,5},{5,6},{6,7},{7,8},{8,9},{9,10},{10,1... | collective-permute-start | bytes 776 | tf_op jit(solution)/shard_map/while/body/eval_jaxpr/ppermute | solution.py:12
  391.4 8.5 %collective-permute-start.4 = (f32[64]{0:T(128)S(1)}, f32[64]{0:T(128)S(1)}, u32[]{:S(2)}, u32[]{:S(2)}) collective-permute-start(f32[64]{0:T(128)S(1)} %get-tuple-element.330), channel_id=1, source_target_pairs={{0,1},{1,2},{2,3},{3,4},{4,5},{5,6},{6,7},{7,8},{8,9},{9,10},{10,1... | collective-permute-start | bytes 776 | tf_op jit(solution)/shard_map/while/body/eval_jaxpr/ppermute | solution.py:12
  391.5 8.4 %collective-permute-start.5 = (f32[64]{0:T(128)S(1)}, f32[64]{0:T(128)S(1)}, u32[]{:S(2)}, u32[]{:S(2)}) collective-permute-start(f32[64]{0:T(128)S(1)} %get-tuple-element.329), channel_id=1, source_target_pairs={{0,1},{1,2},{2,3},{3,4},{4,5},{5,6},{6,7},{7,8},{8,9},{9,10},{10,1... | collective-permute-start | bytes 776 | tf_op jit(solution)/shard_map/while/body/eval_jaxpr/ppermute | solution.py:12
  400.2 8.5 %collective-permute-start.4 = (f32[64]{0:T(128)S(1)}, f32[64]{0:T(128)S(1)}, u32[]{:S(2)}, u32[]{:S(2)}) collective-permute-start(f32[64]{0:T(128)S(1)} %get-tuple-element.330), channel_id=1, source_target_pairs={{0,1},{1,2},{2,3},{3,4},{4,5},{5,6},{6,7},{7,8},{8,9},{9,10},{10,1... | collective-permute-start | bytes 776 | tf_op jit(solution)/shard_map/while/body/eval_jaxpr/ppermute | solution.py:12
  400.3 8.4 %collective-permute-start.5 = (f32[64]{0:T(128)S(1)}, f32[64]{0:T(128)S(1)}, u32[]{:S(2)}, u32[]{:S(2)}) collective-permute-start(f32[64]{0:T(128)S(1)} %get-tuple-element.329), channel_id=1, source_target_pairs={{0,1},{1,2},{2,3},{3,4},{4,5},{5,6},{6,7},{7,8},{8,9},{9,10},{10,1... | collective-permute-start | bytes 776 | tf_op jit(solution)/shard_map/while/body/eval_jaxpr/ppermute | solution.py:12
  409.1 8.5 %collective-permute-start.4 = (f32[64]{0:T(128)S(1)}, f32[64]{0:T(128)S(1)}, u32[]{:S(2)}, u32[]{:S(2)}) collective-permute-start(f32[64]{0:T(128)S(1)} %get-tuple-element.330), channel_id=1, source_target_pairs={{0,1},{1,2},{2,3},{3,4},{4,5},{5,6},{6,7},{7,8},{8,9},{9,10},{10,1... | collective-permute-start | bytes 776 | tf_op jit(solution)/shard_map/while/body/eval_jaxpr/ppermute | solution.py:12
  409.2 8.4 %collective-permute-start.5 = (f32[64]{0:T(128)S(1)}, f32[64]{0:T(128)S(1)}, u32[]{:S(2)}, u32[]{:S(2)}) collective-permute-start(f32[64]{0:T(128)S(1)} %get-tuple-element.329), channel_id=1, source_target_pairs={{0,1},{1,2},{2,3},{3,4},{4,5},{5,6},{6,7},{7,8},{8,9},{9,10},{10,1... | collective-permute-start | bytes 776 | tf_op jit(solution)/shard_map/while/body/eval_jaxpr/ppermute | solution.py:12
  417.9 8.5 %collective-permute-start.4 = (f32[64]{0:T(128)S(1)}, f32[64]{0:T(128)S(1)}, u32[]{:S(2)}, u32[]{:S(2)}) collective-permute-start(f32[64]{0:T(128)S(1)} %get-tuple-element.330), channel_id=1, source_target_pairs={{0,1},{1,2},{2,3},{3,4},{4,5},{5,6},{6,7},{7,8},{8,9},{9,10},{10,1... | collective-permute-start | bytes 776 | tf_op jit(solution)/shard_map/while/body/eval_jaxpr/ppermute | solution.py:12
  418.0 8.4 %collective-permute-start.5 = (f32[64]{0:T(128)S(1)}, f32[64]{0:T(128)S(1)}, u32[]{:S(2)}, u32[]{:S(2)}) collective-permute-start(f32[64]{0:T(128)S(1)} %get-tuple-element.329), channel_id=1, source_target_pairs={{0,1},{1,2},{2,3},{3,4},{4,5},{5,6},{6,7},{7,8},{8,9},{9,10},{10,1... | collective-permute-start | bytes 776 | tf_op jit(solution)/shard_map/while/body/eval_jaxpr/ppermute | solution.py:12
  426.8 8.5 %collective-permute-start.4 = (f32[64]{0:T(128)S(1)}, f32[64]{0:T(128)S(1)}, u32[]{:S(2)}, u32[]{:S(2)}) collective-permute-start(f32[64]{0:T(128)S(1)} %get-tuple-element.330), channel_id=1, source_target_pairs={{0,1},{1,2},{2,3},{3,4},{4,5},{5,6},{6,7},{7,8},{8,9},{9,10},{10,1... | collective-permute-start | bytes 776 | tf_op jit(solution)/shard_map/while/body/eval_jaxpr/ppermute | solution.py:12
  426.9 8.4 %collective-permute-start.5 = (f32[64]{0:T(128)S(1)}, f32[64]{0:T(128)S(1)}, u32[]{:S(2)}, u32[]{:S(2)}) collective-permute-start(f32[64]{0:T(128)S(1)} %get-tuple-element.329), channel_id=1, source_target_pairs={{0,1},{1,2},{2,3},{3,4},{4,5},{5,6},{6,7},{7,8},{8,9},{9,10},{10,1... | collective-permute-start | bytes 776 | tf_op jit(solution)/shard_map/while/body/eval_jaxpr/ppermute | solution.py:12
  435.6 8.5 %collective-permute-start.4 = (f32[64]{0:T(128)S(1)}, f32[64]{0:T(128)S(1)}, u32[]{:S(2)}, u32[]{:S(2)}) collective-permute-start(f32[64]{0:T(128)S(1)} %get-tuple-element.330), channel_id=1, source_target_pairs={{0,1},{1,2},{2,3},{3,4},{4,5},{5,6},{6,7},{7,8},{8,9},{9,10},{10,1... | collective-permute-start | bytes 776 | tf_op jit(solution)/shard_map/while/body/eval_jaxpr/ppermute | solution.py:12
  435.7 8.4 %collective-permute-start.5 = (f32[64]{0:T(128)S(1)}, f32[64]{0:T(128)S(1)}, u32[]{:S(2)}, u32[]{:S(2)}) collective-permute-start(f32[64]{0:T(128)S(1)} %get-tuple-element.329), channel_id=1, source_target_pairs={{0,1},{1,2},{2,3},{3,4},{4,5},{5,6},{6,7},{7,8},{8,9},{9,10},{10,1... | collective-permute-start | bytes 776 | tf_op jit(solution)/shard_map/while/body/eval_jaxpr/ppermute | solution.py:12
  444.5 8.5 %collective-permute-start.4 = (f32[64]{0:T(128)S(1)}, f32[64]{0:T(128)S(1)}, u32[]{:S(2)}, u32[]{:S(2)}) collective-permute-start(f32[64]{0:T(128)S(1)} %get-tuple-element.330), channel_id=1, source_target_pairs={{0,1},{1,2},{2,3},{3,4},{4,5},{5,6},{6,7},{7,8},{8,9},{9,10},{10,1... | collective-permute-start | bytes 776 | tf_op jit(solution)/shard_map/while/body/eval_jaxpr/ppermute | solution.py:12
  444.6 8.4 %collective-permute-start.5 = (f32[64]{0:T(128)S(1)}, f32[64]{0:T(128)S(1)}, u32[]{:S(2)}, u32[]{:S(2)}) collective-permute-start(f32[64]{0:T(128)S(1)} %get-tuple-element.329), channel_id=1, source_target_pairs={{0,1},{1,2},{2,3},{3,4},{4,5},{5,6},{6,7},{7,8},{8,9},{9,10},{10,1... | collective-permute-start | bytes 776 | tf_op jit(solution)/shard_map/while/body/eval_jaxpr/ppermute | solution.py:12
  453.3 8.5 %collective-permute-start.4 = (f32[64]{0:T(128)S(1)}, f32[64]{0:T(128)S(1)}, u32[]{:S(2)}, u32[]{:S(2)}) collective-permute-start(f32[64]{0:T(128)S(1)} %get-tuple-element.330), channel_id=1, source_target_pairs={{0,1},{1,2},{2,3},{3,4},{4,5},{5,6},{6,7},{7,8},{8,9},{9,10},{10,1... | collective-permute-start | bytes 776 | tf_op jit(solution)/shard_map/while/body/eval_jaxpr/ppermute | solution.py:12
  453.4 8.4 %collective-permute-start.5 = (f32[64]{0:T(128)S(1)}, f32[64]{0:T(128)S(1)}, u32[]{:S(2)}, u32[]{:S(2)}) collective-permute-start(f32[64]{0:T(128)S(1)} %get-tuple-element.329), channel_id=1, source_target_pairs={{0,1},{1,2},{2,3},{3,4},{4,5},{5,6},{6,7},{7,8},{8,9},{9,10},{10,1... | collective-permute-start | bytes 776 | tf_op jit(solution)/shard_map/while/body/eval_jaxpr/ppermute | solution.py:12
  462.2 8.5 %collective-permute-start.4 = (f32[64]{0:T(128)S(1)}, f32[64]{0:T(128)S(1)}, u32[]{:S(2)}, u32[]{:S(2)}) collective-permute-start(f32[64]{0:T(128)S(1)} %get-tuple-element.330), channel_id=1, source_target_pairs={{0,1},{1,2},{2,3},{3,4},{4,5},{5,6},{6,7},{7,8},{8,9},{9,10},{10,1... | collective-permute-start | bytes 776 | tf_op jit(solution)/shard_map/while/body/eval_jaxpr/ppermute | solution.py:12
  462.3 8.4 %collective-permute-start.5 = (f32[64]{0:T(128)S(1)}, f32[64]{0:T(128)S(1)}, u32[]{:S(2)}, u32[]{:S(2)}) collective-permute-start(f32[64]{0:T(128)S(1)} %get-tuple-element.329), channel_id=1, source_target_pairs={{0,1},{1,2},{2,3},{3,4},{4,5},{5,6},{6,7},{7,8},{8,9},{9,10},{10,1... | collective-permute-start | bytes 776 | tf_op jit(solution)/shard_map/while/body/eval_jaxpr/ppermute | solution.py:12
  471.0 8.5 %collective-permute-start.4 = (f32[64]{0:T(128)S(1)}, f32[64]{0:T(128)S(1)}, u32[]{:S(2)}, u32[]{:S(2)}) collective-permute-start(f32[64]{0:T(128)S(1)} %get-tuple-element.330), channel_id=1, source_target_pairs={{0,1},{1,2},{2,3},{3,4},{4,5},{5,6},{6,7},{7,8},{8,9},{9,10},{10,1... | collective-permute-start | bytes 776 | tf_op jit(solution)/shard_map/while/body/eval_jaxpr/ppermute | solution.py:12
  471.1 8.4 %collective-permute-start.5 = (f32[64]{0:T(128)S(1)}, f32[64]{0:T(128)S(1)}, u32[]{:S(2)}, u32[]{:S(2)}) collective-permute-start(f32[64]{0:T(128)S(1)} %get-tuple-element.329), channel_id=1, source_target_pairs={{0,1},{1,2},{2,3},{3,4},{4,5},{5,6},{6,7},{7,8},{8,9},{9,10},{10,1... | collective-permute-start | bytes 776 | tf_op jit(solution)/shard_map/while/body/eval_jaxpr/ppermute | solution.py:12
  479.9 8.5 %collective-permute-start.4 = (f32[64]{0:T(128)S(1)}, f32[64]{0:T(128)S(1)}, u32[]{:S(2)}, u32[]{:S(2)}) collective-permute-start(f32[64]{0:T(128)S(1)} %get-tuple-element.330), channel_id=1, source_target_pairs={{0,1},{1,2},{2,3},{3,4},{4,5},{5,6},{6,7},{7,8},{8,9},{9,10},{10,1... | collective-permute-start | bytes 776 | tf_op jit(solution)/shard_map/while/body/eval_jaxpr/ppermute | solution.py:12
  480.0 8.4 %collective-permute-start.5 = (f32[64]{0:T(128)S(1)}, f32[64]{0:T(128)S(1)}, u32[]{:S(2)}, u32[]{:S(2)}) collective-permute-start(f32[64]{0:T(128)S(1)} %get-tuple-element.329), channel_id=1, source_target_pairs={{0,1},{1,2},{2,3},{3,4},{4,5},{5,6},{6,7},{7,8},{8,9},{9,10},{10,1... | collective-permute-start | bytes 776 | tf_op jit(solution)/shard_map/while/body/eval_jaxpr/ppermute | solution.py:12
  488.7 8.5 %collective-permute-start.4 = (f32[64]{0:T(128)S(1)}, f32[64]{0:T(128)S(1)}, u32[]{:S(2)}, u32[]{:S(2)}) collective-permute-start(f32[64]{0:T(128)S(1)} %get-tuple-element.330), channel_id=1, source_target_pairs={{0,1},{1,2},{2,3},{3,4},{4,5},{5,6},{6,7},{7,8},{8,9},{9,10},{10,1... | collective-permute-start | bytes 776 | tf_op jit(solution)/shard_map/while/body/eval_jaxpr/ppermute | solution.py:12
  488.8 8.4 %collective-permute-start.5 = (f32[64]{0:T(128)S(1)}, f32[64]{0:T(128)S(1)}, u32[]{:S(2)}, u32[]{:S(2)}) collective-permute-start(f32[64]{0:T(128)S(1)} %get-tuple-element.329), channel_id=1, source_target_pairs={{0,1},{1,2},{2,3},{3,4},{4,5},{5,6},{6,7},{7,8},{8,9},{9,10},{10,1... | collective-permute-start | bytes 776 | tf_op jit(solution)/shard_map/while/body/eval_jaxpr/ppermute | solution.py:12
  497.6 8.5 %collective-permute-start.4 = (f32[64]{0:T(128)S(1)}, f32[64]{0:T(128)S(1)}, u32[]{:S(2)}, u32[]{:S(2)}) collective-permute-start(f32[64]{0:T(128)S(1)} %get-tuple-element.330), channel_id=1, source_target_pairs={{0,1},{1,2},{2,3},{3,4},{4,5},{5,6},{6,7},{7,8},{8,9},{9,10},{10,1... | collective-permute-start | bytes 776 | tf_op jit(solution)/shard_map/while/body/eval_jaxpr/ppermute | solution.py:12
  497.7 8.4 %collective-permute-start.5 = (f32[64]{0:T(128)S(1)}, f32[64]{0:T(128)S(1)}, u32[]{:S(2)}, u32[]{:S(2)}) collective-permute-start(f32[64]{0:T(128)S(1)} %get-tuple-element.329), channel_id=1, source_target_pairs={{0,1},{1,2},{2,3},{3,4},{4,5},{5,6},{6,7},{7,8},{8,9},{9,10},{10,1... | collective-permute-start | bytes 776 | tf_op jit(solution)/shard_map/while/body/eval_jaxpr/ppermute | solution.py:12
  506.4 8.5 %collective-permute-start.4 = (f32[64]{0:T(128)S(1)}, f32[64]{0:T(128)S(1)}, u32[]{:S(2)}, u32[]{:S(2)}) collective-permute-start(f32[64]{0:T(128)S(1)} %get-tuple-element.330), channel_id=1, source_target_pairs={{0,1},{1,2},{2,3},{3,4},{4,5},{5,6},{6,7},{7,8},{8,9},{9,10},{10,1... | collective-permute-start | bytes 776 | tf_op jit(solution)/shard_map/while/body/eval_jaxpr/ppermute | solution.py:12
  515.3 8.5 %collective-permute-start.4 = (f32[64]{0:T(128)S(1)}, f32[64]{0:T(128)S(1)}, u32[]{:S(2)}, u32[]{:S(2)}) collective-permute-start(f32[64]{0:T(128)S(1)} %get-tuple-element.330), channel_id=1, source_target_pairs={{0,1},{1,2},{2,3},{3,4},{4,5},{5,6},{6,7},{7,8},{8,9},{9,10},{10,1... | collective-permute-start | bytes 776 | tf_op jit(solution)/shard_map/while/body/eval_jaxpr/ppermute | solution.py:12
  515.4 8.4 %collective-permute-start.5 = (f32[64]{0:T(128)S(1)}, f32[64]{0:T(128)S(1)}, u32[]{:S(2)}, u32[]{:S(2)}) collective-permute-start(f32[64]{0:T(128)S(1)} %get-tuple-element.329), channel_id=1, source_target_pairs={{0,1},{1,2},{2,3},{3,4},{4,5},{5,6},{6,7},{7,8},{8,9},{9,10},{10,1... | collective-permute-start | bytes 776 | tf_op jit(solution)/shard_map/while/body/eval_jaxpr/ppermute | solution.py:12
  524.1 8.5 %collective-permute-start.4 = (f32[64]{0:T(128)S(1)}, f32[64]{0:T(128)S(1)}, u32[]{:S(2)}, u32[]{:S(2)}) collective-permute-start(f32[64]{0:T(128)S(1)} %get-tuple-element.330), channel_id=1, source_target_pairs={{0,1},{1,2},{2,3},{3,4},{4,5},{5,6},{6,7},{7,8},{8,9},{9,10},{10,1... | collective-permute-start | bytes 776 | tf_op jit(solution)/shard_map/while/body/eval_jaxpr/ppermute | solution.py:12
  524.2 8.4 %collective-permute-start.5 = (f32[64]{0:T(128)S(1)}, f32[64]{0:T(128)S(1)}, u32[]{:S(2)}, u32[]{:S(2)}) collective-permute-start(f32[64]{0:T(128)S(1)} %get-tuple-element.329), channel_id=1, source_target_pairs={{0,1},{1,2},{2,3},{3,4},{4,5},{5,6},{6,7},{7,8},{8,9},{9,10},{10,1... | collective-permute-start | bytes 776 | tf_op jit(solution)/shard_map/while/body/eval_jaxpr/ppermute | solution.py:12
  533.0 8.5 %collective-permute-start.4 = (f32[64]{0:T(128)S(1)}, f32[64]{0:T(128)S(1)}, u32[]{:S(2)}, u32[]{:S(2)}) collective-permute-start(f32[64]{0:T(128)S(1)} %get-tuple-element.330), channel_id=1, source_target_pairs={{0,1},{1,2},{2,3},{3,4},{4,5},{5,6},{6,7},{7,8},{8,9},{9,10},{10,1... | collective-permute-start | bytes 776 | tf_op jit(solution)/shard_map/while/body/eval_jaxpr/ppermute | solution.py:12
  541.8 8.5 %collective-permute-start.4 = (f32[64]{0:T(128)S(1)}, f32[64]{0:T(128)S(1)}, u32[]{:S(2)}, u32[]{:S(2)}) collective-permute-start(f32[64]{0:T(128)S(1)} %get-tuple-element.330), channel_id=1, source_target_pairs={{0,1},{1,2},{2,3},{3,4},{4,5},{5,6},{6,7},{7,8},{8,9},{9,10},{10,1... | collective-permute-start | bytes 776 | tf_op jit(solution)/shard_map/while/body/eval_jaxpr/ppermute | solution.py:12
  541.9 8.4 %collective-permute-start.5 = (f32[64]{0:T(128)S(1)}, f32[64]{0:T(128)S(1)}, u32[]{:S(2)}, u32[]{:S(2)}) collective-permute-start(f32[64]{0:T(128)S(1)} %get-tuple-element.329), channel_id=1, source_target_pairs={{0,1},{1,2},{2,3},{3,4},{4,5},{5,6},{6,7},{7,8},{8,9},{9,10},{10,1... | collective-permute-start | bytes 776 | tf_op jit(solution)/shard_map/while/body/eval_jaxpr/ppermute | solution.py:12
  550.7 8.5 %collective-permute-start.4 = (f32[64]{0:T(128)S(1)}, f32[64]{0:T(128)S(1)}, u32[]{:S(2)}, u32[]{:S(2)}) collective-permute-start(f32[64]{0:T(128)S(1)} %get-tuple-element.330), channel_id=1, source_target_pairs={{0,1},{1,2},{2,3},{3,4},{4,5},{5,6},{6,7},{7,8},{8,9},{9,10},{10,1... | collective-permute-start | bytes 776 | tf_op jit(solution)/shard_map/while/body/eval_jaxpr/ppermute | solution.py:12
  550.8 8.4 %collective-permute-start.5 = (f32[64]{0:T(128)S(1)}, f32[64]{0:T(128)S(1)}, u32[]{:S(2)}, u32[]{:S(2)}) collective-permute-start(f32[64]{0:T(128)S(1)} %get-tuple-element.329), channel_id=1, source_target_pairs={{0,1},{1,2},{2,3},{3,4},{4,5},{5,6},{6,7},{7,8},{8,9},{9,10},{10,1... | collective-permute-start | bytes 776 | tf_op jit(solution)/shard_map/while/body/eval_jaxpr/ppermute | solution.py:12
  559.5 8.5 %collective-permute-start.4 = (f32[64]{0:T(128)S(1)}, f32[64]{0:T(128)S(1)}, u32[]{:S(2)}, u32[]{:S(2)}) collective-permute-start(f32[64]{0:T(128)S(1)} %get-tuple-element.330), channel_id=1, source_target_pairs={{0,1},{1,2},{2,3},{3,4},{4,5},{5,6},{6,7},{7,8},{8,9},{9,10},{10,1... | collective-permute-start | bytes 776 | tf_op jit(solution)/shard_map/while/body/eval_jaxpr/ppermute | solution.py:12
  568.4 8.5 %collective-permute-start.4 = (f32[64]{0:T(128)S(1)}, f32[64]{0:T(128)S(1)}, u32[]{:S(2)}, u32[]{:S(2)}) collective-permute-start(f32[64]{0:T(128)S(1)} %get-tuple-element.330), channel_id=1, source_target_pairs={{0,1},{1,2},{2,3},{3,4},{4,5},{5,6},{6,7},{7,8},{8,9},{9,10},{10,1... | collective-permute-start | bytes 776 | tf_op jit(solution)/shard_map/while/body/eval_jaxpr/ppermute | solution.py:12
  568.5 8.4 %collective-permute-start.5 = (f32[64]{0:T(128)S(1)}, f32[64]{0:T(128)S(1)}, u32[]{:S(2)}, u32[]{:S(2)}) collective-permute-start(f32[64]{0:T(128)S(1)} %get-tuple-element.329), channel_id=1, source_target_pairs={{0,1},{1,2},{2,3},{3,4},{4,5},{5,6},{6,7},{7,8},{8,9},{9,10},{10,1... | collective-permute-start | bytes 776 | tf_op jit(solution)/shard_map/while/body/eval_jaxpr/ppermute | solution.py:12
  577.2 8.5 %collective-permute-start.4 = (f32[64]{0:T(128)S(1)}, f32[64]{0:T(128)S(1)}, u32[]{:S(2)}, u32[]{:S(2)}) collective-permute-start(f32[64]{0:T(128)S(1)} %get-tuple-element.330), channel_id=1, source_target_pairs={{0,1},{1,2},{2,3},{3,4},{4,5},{5,6},{6,7},{7,8},{8,9},{9,10},{10,1... | collective-permute-start | bytes 776 | tf_op jit(solution)/shard_map/while/body/eval_jaxpr/ppermute | solution.py:12
  577.3 8.4 %collective-permute-start.5 = (f32[64]{0:T(128)S(1)}, f32[64]{0:T(128)S(1)}, u32[]{:S(2)}, u32[]{:S(2)}) collective-permute-start(f32[64]{0:T(128)S(1)} %get-tuple-element.329), channel_id=1, source_target_pairs={{0,1},{1,2},{2,3},{3,4},{4,5},{5,6},{6,7},{7,8},{8,9},{9,10},{10,1... | collective-permute-start | bytes 776 | tf_op jit(solution)/shard_map/while/body/eval_jaxpr/ppermute | solution.py:12
  (142 other events, 1111.9 us)
where the time goes:
time: 599 us; the launch traced here: 594 us
  starting transfers between devices  383 us (64%)
  waiting for transfers between devices  110 us (18%)
  matrix products  42.4 us (7%)
  blocking collectives  27.9 us (5%)
  other arithmetic  23 us (4%)
    ppermute x188, starting transfers between devices, from_behind(): return lax.ppermute(value, axis, pairs)  383 us
    ppermute x188, waiting for transfers between devices, from_behind(): return lax.ppermute(value, axis, pairs)  110 us
    dot_general x32, matrix products, column_terms(): lax.dot_general(group, sources, (((1,), (1,)), ((), ())), preferred_eleme...  22.6 us
    dot_general x32, matrix products, row_terms(): lax.dot_general(sources, group, (((1,), (1,)), ((), ())), preferred_eleme...  19.8 us
    pmax x1, blocking collectives, on_device(): highest = lax.pmax(peak, 'grp')  15.3 us
    psum x1, blocking collectives, on_device(): total = lax.psum(total * jnp.exp(peak - highest), 'grp')  12.6 us
  transfers between devices with their start and end apart: 188, of which 60 were waited for; matrix products, arithmetic and copies ran while one was open for 6% of the time, Pallas kernels for 0%

commit v1 on v0

v1 whole, which is shorter than its diff:
```python
import math

import jax
import jax.numpy as jnp
from jax import lax
from jax.experimental import pallas as pl
from jax.experimental.pallas import tpu as pltpu
from jax.sharding import Mesh, PartitionSpec as P

EPSILON = 0.05
LOG2E = math.log2(math.e)
SCALE = 2.0 / EPSILON * LOG2E
BACK = EPSILON * math.log(2.0)

D = 768
PAD = 128
UNIT = 128
UNITS = 8
ROWS = UNIT * UNITS
SRC = 2048
BLOCK = 512
PLANE = 16
OFFSETS = (1, -1, 2, -2, 3, -3, 0, 4)
VMEM = 48 * 1024 * 1024


def ring(value, step):
    count = lax.axis_size("z")
    return lax.ppermute(value, "z", [(i, (i + step) % count) for i in range(count)])


def other_core(value):
    return lax.ppermute(value, "core", [(0, 1), (1, 0)])


def facing(value):
    return lax.ppermute(value, ("x_lo", "x_hi"), [(0, 3), (3, 0), (1, 2), (2, 1)])


def log_sum2(values):
    peak = jnp.max(values, axis=0, keepdims=True)
    return peak + jnp.log2(jnp.sum(jnp.exp2(values - peak), axis=0, keepdims=True))


def row_kernel(units, last, *refs):
    group_refs = refs[:units]
    src_ref = refs[units]
    rest = refs[units + 1 :]
    cross_ref, lse_ref = rest[-2:]
    parts = []
    for at, group_ref in enumerate(group_refs):
        cross = lax.dot_general(
            group_ref[:, :D],
            src_ref[...],
            (((1,), (1,)), ((), ())),
            preferred_element_type=jnp.float32,
        )
        cross = cross * SCALE
        cross_ref[at * UNIT : (at + 1) * UNIT, :] = cross
        pieces = group_ref[:, D : D + PAD].astype(jnp.float32)
        bias = pieces[:, 0:1] + pieces[:, 1:2] + pieces[:, 2:3]
        parts.append(cross + bias)
    scores = parts[0] if units == 1 else jnp.concatenate(parts, axis=0)
    total = log_sum2(scores)
    if last:
        earlier = [ref[...] for ref in rest[1:-2]]
        total = log_sum2(jnp.concatenate([total, *earlier], axis=0))
        total = jnp.broadcast_to(total, (PLANE, BLOCK))
    lse_ref[...] = total


def row_pass(groups, sources, buffer, place, earlier=()):
    units = len(groups)
    last = len(earlier) > 0
    rows = units * UNIT
    in_specs = [pl.BlockSpec((UNIT, D + PAD), lambda i: (0, 0))] * units
    in_specs.append(pl.BlockSpec((BLOCK, D), lambda i: (i, 0)))
    operands = [*groups, sources]
    aliases = {}
    if buffer is not None:
        aliases = {len(operands): 0}
        operands.append(buffer)
        in_specs.append(pl.BlockSpec(memory_space=pl.ANY))
    elif last:
        raise ValueError("no buffer")
    for value in earlier:
        operands.append(value)
        in_specs.append(pl.BlockSpec((1, BLOCK), lambda i: (0, i)))
    height = PLANE if last else 1

    def body(*refs):
        row_kernel(units, last, *refs)

    return pl.pallas_call(
        body,
        grid=(SRC // BLOCK,),
        in_specs=in_specs,
        out_specs=[
            pl.BlockSpec((rows, BLOCK), lambda i: (place, i)),
            pl.BlockSpec((height, BLOCK), lambda i: (0, i)),
        ],
        out_shape=[
            jax.ShapeDtypeStruct((ROWS, SRC), jnp.float32),
            jax.ShapeDtypeStruct((height, SRC), jnp.float32),
        ],
        input_output_aliases=aliases,
        compiler_params=pltpu.CompilerParams(vmem_limit_bytes=VMEM),
        cost_estimate=pl.CostEstimate(
            flops=2 * rows * SRC * D,
            bytes_accessed=SRC * D * 2 + rows * SRC * 4,
            transcendentals=rows * SRC,
        ),
        name="rows",
    )(*operands)


def column_kernel(z_ref, cross_ref, partial_ref, logw_ref, out_ref, row_ref, bias_ref):
    step = pl.program_id(0)

    @pl.when(step == 0)
    def _():
        row = log_sum2(partial_ref[...])
        row_ref[...] = row
        bias_ref[...] = logw_ref[...] * LOG2E - row

    scores = cross_ref[...] + bias_ref[...]
    peak = jnp.max(scores, axis=1, keepdims=True)
    total = jnp.sum(jnp.exp2(scores - peak), axis=1, keepdims=True)
    lse = jnp.broadcast_to(peak + jnp.log2(total), (UNIT, UNIT)).T
    half = step // 2 + 1
    offset = jnp.where(step % 2 == 0, half, UNITS - half)
    offset = jnp.where(step == 6, 0, offset)
    place = lax.rem(z_ref[0] + offset, UNITS)
    out_ref[pl.ds(place, 1), :] = lse[0:1, :]


def column_pass(z, cross, partial, logw):
    return pl.pallas_call(
        column_kernel,
        grid=(UNITS,),
        in_specs=[
            pl.BlockSpec(memory_space=pltpu.SMEM),
            pl.BlockSpec((UNIT, SRC), lambda i: (i, 0)),
            pl.BlockSpec((PLANE, SRC), lambda i: (0, 0)),
            pl.BlockSpec((1, SRC), lambda i: (0, 0)),
        ],
        out_specs=[
            pl.BlockSpec((UNITS, UNIT), lambda i: (0, 0)),
            pl.BlockSpec((1, SRC), lambda i: (0, 0)),
        ],
        out_shape=[
            jax.ShapeDtypeStruct((UNITS, UNIT), jnp.float32),
            jax.ShapeDtypeStruct((1, SRC), jnp.float32),
        ],
        scratch_shapes=[pltpu.VMEM((1, SRC), jnp.float32)],
        compiler_params=pltpu.CompilerParams(vmem_limit_bytes=VMEM),
        cost_estimate=pl.CostEstimate(
            flops=6 * ROWS * SRC, bytes_accessed=ROWS * SRC * 4, transcendentals=ROWS * SRC
        ),
        name="columns",
    )(z, cross, partial, logw)


def on_device(sources, targets, potential_in, source_logw, target_logw):
    core = lax.axis_index("core")
    z = lax.axis_index("z").astype(jnp.int32).reshape(1)

    tgt_sq = jnp.sum(jnp.square(targets.astype(jnp.float32)), axis=1)
    bias = (target_logw + (potential_in - tgt_sq) / EPSILON) * LOG2E
    high = lax.reduce_precision(bias, 8, 7)
    middle = lax.reduce_precision(bias - high, 8, 7)
    low = bias - high - middle
    pieces = jnp.stack([high, middle, low], axis=1).astype(jnp.bfloat16)
    own = jnp.concatenate([targets, jnp.pad(pieces, ((0, 0), (0, PAD - 3)))], axis=1)

    pair = jnp.concatenate([own, facing(own)], axis=0)

    def both(value):
        other = other_core(value)
        first = core == 0
        return jnp.concatenate(
            [jnp.where(first, value, other), jnp.where(first, other, value)], axis=0
        )

    all_sources = both(sources)
    logw = both(source_logw).reshape(1, SRC)
    src_sq = jnp.sum(jnp.square(sources.astype(jnp.float32)), axis=1)

    lses = []
    buffer, lse = row_pass([pair], all_sources, None, 6)
    lses.append(lse)
    below = above = pair
    for step in range(3):
        below, above = ring(below, 1), ring(above, -1)
        buffer, lse = row_pass([above, below], all_sources, buffer, step)
        lses.append(lse)
    opposite = ring(below, 1)
    buffer, shared = row_pass([opposite], all_sources, buffer, 7, lses)

    partial = lax.all_to_all(shared, ("y", "x_lo", "core"), 0, 0, tiled=True)
    columns, rows = column_pass(z, buffer, partial, logw)
    mine = lax.dynamic_slice(rows.reshape(SRC), (core * (SRC // 2),), (SRC // 2,))
    source_potential = src_sq - BACK * mine

    gathered = lax.all_to_all(columns, "z", 0, 0, tiled=True)
    summed = log_sum2(gathered).reshape(UNIT)
    arrived = facing(summed[UNIT // 2 :])
    final = log_sum2(jnp.stack([summed[: UNIT // 2], arrived], axis=0)).reshape(UNIT // 2)
    potential_out = tgt_sq - BACK * final
    return (source_potential, potential_out)


def solution(mesh):
    fine = Mesh(mesh.devices.reshape(4, 2, 8, 2, 2), ("y", "x_lo", "z", "x_hi", "core"))
    blk = ("z", "x_hi", "core")
    every = ("y", "x_lo", "z", "x_hi", "core")
    in_specs = (P(blk, None), P(every, None), P(every), P(blk), P(every))
    out_specs = (P(blk), P(every))
    return jax.shard_map(
        on_device, mesh=fine, in_specs=in_specs, out_specs=out_specs, check_vma=False
    )
```

time: 599 us -> 95.6 us (0.16)
  the two profiles are of different devices: /device:TPU:1 before, /device:TPU:6 now
where the time goes in v1:
time: 95.6 us; the launch traced here: 95.2 us
  waiting for transfers between devices  34.5 us (36%)
  starting transfers between devices  27.2 us (28%)
  Pallas kernels  24.7 us (26%)
  other arithmetic  6.97 us (7%)
  local copies, waits for them, and re-layouts  1.04 us (1%)
    pallas_call x5, Pallas kernels, row_pass(): pl.pallas_call(body, grid=(SRC // BLOCK,), in_specs=in_specs, out_specs=[...  16.9 us
    ppermute x7, waiting for transfers between devices, ring(): lax.ppermute(value, 'z', [(i, (i + step) % count) for i in range(count)])  14 us
    ppermute x7, starting transfers between devices, ring(): lax.ppermute(value, 'z', [(i, (i + step) % count) for i in range(count)])  12.5 us
    ppermute x2, waiting for transfers between devices, facing(): lax.ppermute(value, ('x_lo', 'x_hi'), [(0, 3), (3, 0), (1, 2), (2, 1)])  8.11 us
    pallas_call x1, Pallas kernels, column_pass(): pl.pallas_call(column_kernel, grid=(UNITS,), in_specs=[pl.BlockSpec(memor...  7.76 us
    all_to_all x1, waiting for transfers between devices, on_device(): gathered = lax.all_to_all(columns, 'z', 0, 0, tiled=True)  7.22 us
    all_to_all x1, starting transfers between devices, on_device(): partial = lax.all_to_all(shared, ('y', 'x_lo', 'core'), 0, 0, tiled=True)  5.94 us
    all_to_all x1, starting transfers between devices, on_device(): gathered = lax.all_to_all(columns, 'z', 0, 0, tiled=True)  5.82 us
  transfers between devices with their start and end apart: 13, of which 7 were waited for; matrix products, arithmetic and copies ran while one was open for 8% of the time, Pallas kernels for 18%

profile of v1, /device:TPU:6, one launch (start us, length us, event | category | flops | bytes accessed | tf_op | source)
XLA Modules:
  0.0 95.2 jit_solution(4677098296090975696)
XLA Ops:
  0.6 0.1 collective-permute-start.5
  0.7 1.0 %multiply_reduce_fusion.1 = f32[64]{0:T(128)S(1)} fusion(bf16[64,768]{1,0:T(8,128)(2,1)} %param.6), kind=kLoop, calls=%fused_computation.5 | loop fusion | flops 147392 | bytes 98560 | tf_op jit(solution)/shard_map/reduce_sum | solution.py:168
  1.7 0.7 fusion.3
  2.5 0.1 copy.14
  2.6 0.9 pad_maximum_fusion.2
  3.5 2.3 %collective-permute-start = (bf16[64,896]{1,0:T(8,128)(2,1)S(1)}, bf16[64,896]{1,0:T(8,128)(2,1)S(1)}, u32[]{:S(2)}, u32[]{:S(2)}) collective-permute-start(bf16[64,896]{1,0:T(8,128)(2,1)S(1)} %pad_maximum_fusion.2), channel_id=1, source_target_pairs={{0,34},{34,0},{2,32},{32,2},{1,35},{35,1},{3,33},{33,3},{4,38},{38... | collective-permute-start | bytes 344072 | tf_op jit(solution)/shard_map/ppermute | solution.py:37
  5.8 4.5 %collective-permute-done = bf16[64,896]{1,0:T(8,128)(2,1)S(1)} collective-permute-done((bf16[64,896]{1,0:T(8,128)(2,1)S(1)}, bf16[64,896]{1,0:T(8,128)(2,1)S(1)}, u32[]{:S(2)}, u32[]{:S(2)}) %collective-permute-start) | collective-permute-done | bytes 114720 | tf_op jit(solution)/shard_map/ppermute | solution.py:37
  10.3 0.9 pad_maximum_fusion.1.refs_0_
  11.2 2.0 %collective-permute-start.1 = (bf16[128,896]{1,0:T(8,128)(2,1)S(1)}, bf16[128,896]{1,0:T(8,128)(2,1)S(1)}, u32[]{:S(2)}, u32[]{:S(2)}) collective-permute-start(bf16[128,896]{1,0:T(8,128)(2,1)S(1)} %pad_maximum_fusion.1.refs_0_), channel_id=1, source_target_pairs={{0,4},{4,8},{8,12},{12,16},{16,20},{20,24},{24,28},{28,0},{1,5},{5... | collective-permute-start | bytes 688136 | tf_op jit(solution)/shard_map/ppermute | solution.py:29
  13.2 4.0 %collective-permute-start.6 = (bf16[128,896]{1,0:T(8,128)(2,1)S(1)}, bf16[128,896]{1,0:T(8,128)(2,1)S(1)}, u32[]{:S(2)}, u32[]{:S(2)}) collective-permute-start(bf16[128,896]{1,0:T(8,128)(2,1)S(1)} %pad_maximum_fusion.1.refs_0_), channel_id=1, source_target_pairs={{0,28},{4,0},{8,4},{12,8},{16,12},{20,16},{24,20},{28,24},{1,29},{... | collective-permute-start | bytes 688136 | tf_op jit(solution)/shard_map/ppermute | solution.py:29
  17.3 5.4 %collective-permute-done.1.refs_1_ = bf16[128,896]{1,0:T(8,128)(2,1)S(1)} collective-permute-done((bf16[128,896]{1,0:T(8,128)(2,1)S(1)}, bf16[128,896]{1,0:T(8,128)(2,1)S(1)}, u32[]{:S(2)}, u32[]{:S(2)}) %collective-permute-start.1) | collective-permute-done | bytes 229408 | tf_op jit(solution)/shard_map/ppermute | solution.py:29
  22.7 0.0 collective-permute-start.2
  22.7 0.0 collective-permute-done.6.refs_0_
  22.7 3.2 %collective-permute-start.7 = (bf16[128,896]{1,0:T(8,128)(2,1)S(1)}, bf16[128,896]{1,0:T(8,128)(2,1)S(1)}, u32[]{:S(2)}, u32[]{:S(2)}) collective-permute-start(bf16[128,896]{1,0:T(8,128)(2,1)S(1)} %collective-permute-done.6.refs_0_), channel_id=1, source_target_pairs={{0,28},{4,0},{8,4},{12,8},{16,12},{20,16},{24,20},{28,24},{1,29},{... | collective-permute-start | bytes 688136 | tf_op jit(solution)/shard_map/ppermute | solution.py:29
  25.9 4.6 %collective-permute-done.2.refs_1_ = bf16[128,896]{1,0:T(8,128)(2,1)S(1)} collective-permute-done((bf16[128,896]{1,0:T(8,128)(2,1)S(1)}, bf16[128,896]{1,0:T(8,128)(2,1)S(1)}, u32[]{:S(2)}, u32[]{:S(2)}) %collective-permute-start.2) | collective-permute-done | bytes 229408 | tf_op jit(solution)/shard_map/ppermute | solution.py:29
  30.5 0.0 collective-permute-start.3
  30.5 0.0 collective-permute-start.9
  30.5 0.0 collective-permute-done.7.refs_0_
  30.5 3.2 %collective-permute-start.8 = (bf16[128,896]{1,0:T(8,128)(2,1)S(1)}, bf16[128,896]{1,0:T(8,128)(2,1)S(1)}, u32[]{:S(2)}, u32[]{:S(2)}) collective-permute-start(bf16[128,896]{1,0:T(8,128)(2,1)S(1)} %collective-permute-done.7.refs_0_), channel_id=1, source_target_pairs={{0,28},{4,0},{8,4},{12,8},{16,12},{20,16},{24,20},{28,24},{1,29},{... | collective-permute-start | bytes 688136 | tf_op jit(solution)/shard_map/ppermute | solution.py:29
  33.8 4.0 %collective-permute-done.3.refs_1_ = bf16[128,896]{1,0:T(8,128)(2,1)S(1)} collective-permute-done((bf16[128,896]{1,0:T(8,128)(2,1)S(1)}, bf16[128,896]{1,0:T(8,128)(2,1)S(1)}, u32[]{:S(2)}, u32[]{:S(2)}) %collective-permute-start.3) | collective-permute-done | bytes 229408 | tf_op jit(solution)/shard_map/ppermute | solution.py:29
  37.7 0.0 collective-permute-start.4
  37.8 0.0 collective-permute-done.5
  37.8 1.6 %broadcast_select_fusion.1 = (bf16[1024,768]{1,0:T(8,128)(2,1)S(1)}, bf16[1024,768]{1,0:T(8,128)(2,1)S(1)}) fusion(bf16[1024,768]{1,0:T(8,128)(2,1)} %param.5, bf16[1024,768]{1,0:T(8,128)(2,1)S(1)} %collective-permute-done.5, pred[]{:T(512)S(6)} %eq.4), kind=kLoop, calls=%fused_computation.3 | loop fusion | flops 1572864 | bytes 6291457 | tf_op jit(solution)/shard_map/jit(_where)/select_n | solution.py:182
  39.4 0.2 pad_maximum_fusion.refs_1_.refs_2_
  39.6 2.8 %rows.5 = (f32[1024,2048]{1,0:T(8,128)}, f32[1,2048]{1,0:T(1,128)S(1)}) custom-call(bf16[128,896]{1,0:T(8,128)(2,1)S(1)} %pad_maximum_fusion.1.refs_0_, bf16[2048,768]{1,0:T(8,128)(2,1)S(1)} %pad_maximum_fusion.refs_1_.refs_2_), custom_call_target="tpu_custom_call" | custom-call | flops 402653184 | bytes 4194304 | tf_op jit(solution)/shard_map/rows/pallas_call | solution.py:94
  42.4 3.8 %rows.6 = (f32[1024,2048]{1,0:T(8,128)}, f32[1,2048]{1,0:T(1,128)S(1)}) custom-call(bf16[128,896]{1,0:T(8,128)(2,1)S(1)} %collective-permute-done.6.refs_0_, bf16[128,896]{1,0:T(8,128)(2,1)S(1)} %collective-permute-done.1.refs_1_, bf16[2048,768]{1,0:T(8,128)(2,1)S(1)} %pad_maximum_fusion.refs_1_.refs_2_, ...), custom_call_target="tpu_custom_call", output_to_operand_aliasing={{0}: (3, {})} | custom-call | flops 805306368 | bytes 5242880 | tf_op jit(solution)/shard_map/rows/pallas_call | solution.py:94
  46.1 3.8 %rows.7 = (f32[1024,2048]{1,0:T(8,128)}, f32[1,2048]{1,0:T(1,128)S(1)}) custom-call(bf16[128,896]{1,0:T(8,128)(2,1)S(1)} %collective-permute-done.7.refs_0_, bf16[128,896]{1,0:T(8,128)(2,1)S(1)} %collective-permute-done.2.refs_1_, bf16[2048,768]{1,0:T(8,128)(2,1)S(1)} %pad_maximum_fusion.refs_1_.refs_2_, ...), custom_call_target="tpu_custom_call", output_to_operand_aliasing={{0}: (3, {})} | custom-call | flops 805306368 | bytes 5242880 | tf_op jit(solution)/shard_map/rows/pallas_call | solution.py:94
  49.9 0.0 collective-permute-done.8.refs_0_
  50.0 3.8 %rows.8 = (f32[1024,2048]{1,0:T(8,128)}, f32[1,2048]{1,0:T(1,128)S(1)}) custom-call(bf16[128,896]{1,0:T(8,128)(2,1)S(1)} %collective-permute-done.8.refs_0_, bf16[128,896]{1,0:T(8,128)(2,1)S(1)} %collective-permute-done.3.refs_1_, bf16[2048,768]{1,0:T(8,128)(2,1)S(1)} %pad_maximum_fusion.refs_1_.refs_2_, ...), custom_call_target="tpu_custom_call", output_to_operand_aliasing={{0}: (3, {})} | custom-call | flops 805306368 | bytes 5242880 | tf_op jit(solution)/shard_map/rows/pallas_call | solution.py:94
  53.7 0.0 collective-permute-done.4.refs_0_
  53.7 0.0 copy-start.1
  53.7 2.8 %rows.9 = (f32[1024,2048]{1,0:T(8,128)}, f32[16,2048]{1,0:T(8,128)S(1)}) custom-call(bf16[128,896]{1,0:T(8,128)(2,1)S(1)} %collective-permute-done.4.refs_0_, bf16[2048,768]{1,0:T(8,128)(2,1)S(1)} %pad_maximum_fusion.refs_1_.refs_2_, f32[1024,2048]{1,0:T(8,128)} %get-tuple-element.17.refs_2_, ...), custom_call_target="tpu_custom_call", output_to_operand_aliasing={{0}: (2, {})} | custom-call | flops 402653184 | bytes 4194304 | tf_op jit(solution)/shard_map/rows/pallas_call | solution.py:94
  56.5 0.8 copy.15
  57.3 5.9 %all-to-all-start = ((f32[16,1,2048]{2,1,0:T(1,128)}), f32[16,1,2048]{2,1,0:T(1,128)S(1)}, u32[]{:S(2)}, u32[]{:S(2)}) async-start(f32[16,1,2048]{2,1,0:T(1,128)} %copy.15), calls=%async_computation | async-start | bytes 262144 | tf_op jit(solution)/shard_map/all_to_all | solution.py:200
  63.2 0.0 collective-permute-done.9
  63.2 0.0 copy-done.1
  63.3 5.2 %all-to-all-done = f32[16,1,2048]{2,1,0:T(1,128)S(1)} async-done(((f32[16,1,2048]{2,1,0:T(1,128)}), f32[16,1,2048]{2,1,0:T(1,128)S(1)}, u32[]{:S(2)}, u32[]{:S(2)}) %all-to-all-start) | async-done | bytes 131104 | tf_op jit(solution)/shard_map/all_to_all | solution.py:200
  68.5 0.0 copy-start
  68.5 7.8 %columns.1 = (f32[8,128]{1,0:T(8,128)}, f32[1,2048]{1,0:T(1,128)S(1)}) custom-call(s32[1]{0:T(128)} %bitcast.z_ref, f32[1024,2048]{1,0:T(8,128)} %get-tuple-element.22.cross_ref, f32[16,2048]{1,0:T(8,128)S(1)} %bitcast.33, f32[1,2048]{1,0:T(1,128)S(1)} %bitcast.35), custom_call_target="tpu_custom_call" | custom-call | flops 12582912 | bytes 8388608 | tf_op jit(solution)/shard_map/columns/pallas_call | solution.py:138
  76.3 5.8 %all-to-all-start.1 = ((f32[8,1,128]{2,1,0:T(1,128)}), f32[8,1,128]{2,1,0:T(1,128)S(1)}, u32[]{:S(2)}, u32[]{:S(2)}) async-start(f32[8,1,128]{2,1,0:T(1,128)} %bitcast.8), calls=%async_computation.1 | async-start | bytes 8192 | tf_op jit(solution)/shard_map/all_to_all | solution.py:205
  82.1 0.0 copy-done
  82.1 0.4 multiply_reduce_fusion
  82.5 7.2 %all-to-all-done.1 = f32[8,1,128]{2,1,0:T(1,128)S(1)} async-done(((f32[8,1,128]{2,1,0:T(1,128)}), f32[8,1,128]{2,1,0:T(1,128)S(1)}, u32[]{:S(2)}, u32[]{:S(2)}) %all-to-all-start.1) | async-done | bytes 4128 | tf_op jit(solution)/shard_map/all_to_all | solution.py:205
  89.8 0.1 slice_bitcast_fusion
  89.8 0.6 collective-permute-start.10
  90.4 0.6 sub.37
  91.0 3.6 %collective-permute-done.10 = f32[64]{0:T(128)S(1)} collective-permute-done((f32[64]{0:T(128)S(1)}, f32[64]{0:T(128)S(1)}, u32[]{:S(2)}, u32[]{:S(2)}) %collective-permute-start.10) | collective-permute-done | bytes 288 | tf_op jit(solution)/shard_map/ppermute | solution.py:37
  94.6 0.5 fusion.9
  (12 shorter events, 0.2 us)
Async XLA Ops:
  0.6 37.1 %collective-permute-start.5 = (bf16[1024,768]{1,0:T(8,128)(2,1)}, bf16[1024,768]{1,0:T(8,128)(2,1)S(1)}, u32[]{:S(2)}, u32[]{:S(2)}) collective-permute-start(bf16[1024,768]{1,0:T(8,128)(2,1)} %param.5), channel_id=1, source_target_pairs={{0,1},{1,0},{2,3},{3,2},{4,5},{5,4},{6,7},{7,6},{8,9},{9,8},{10,11... | collective-permute-start | bytes 4718600 | tf_op jit(solution)/shard_map/ppermute | solution.py:33
  3.5 6.8 %collective-permute-start = (bf16[64,896]{1,0:T(8,128)(2,1)S(1)}, bf16[64,896]{1,0:T(8,128)(2,1)S(1)}, u32[]{:S(2)}, u32[]{:S(2)}) collective-permute-start(bf16[64,896]{1,0:T(8,128)(2,1)S(1)} %pad_maximum_fusion.2), channel_id=1, source_target_pairs={{0,34},{34,0},{2,32},{32,2},{1,35},{35,1},{3,33},{33,3},{4,38},{38... | collective-permute-start | bytes 344072 | tf_op jit(solution)/shard_map/ppermute | solution.py:37
  11.2 11.4 %collective-permute-start.1 = (bf16[128,896]{1,0:T(8,128)(2,1)S(1)}, bf16[128,896]{1,0:T(8,128)(2,1)S(1)}, u32[]{:S(2)}, u32[]{:S(2)}) collective-permute-start(bf16[128,896]{1,0:T(8,128)(2,1)S(1)} %pad_maximum_fusion.1.refs_0_), channel_id=1, source_target_pairs={{0,4},{4,8},{8,12},{12,16},{16,20},{20,24},{24,28},{28,0},{1,5},{5... | collective-permute-start | bytes 688136 | tf_op jit(solution)/shard_map/ppermute | solution.py:29
  13.2 9.4 %collective-permute-start.6 = (bf16[128,896]{1,0:T(8,128)(2,1)S(1)}, bf16[128,896]{1,0:T(8,128)(2,1)S(1)}, u32[]{:S(2)}, u32[]{:S(2)}) collective-permute-start(bf16[128,896]{1,0:T(8,128)(2,1)S(1)} %pad_maximum_fusion.1.refs_0_), channel_id=1, source_target_pairs={{0,28},{4,0},{8,4},{12,8},{16,12},{20,16},{24,20},{28,24},{1,29},{... | collective-permute-start | bytes 688136 | tf_op jit(solution)/shard_map/ppermute | solution.py:29
  22.7 7.9 %collective-permute-start.2 = (bf16[128,896]{1,0:T(8,128)(2,1)S(1)}, bf16[128,896]{1,0:T(8,128)(2,1)S(1)}, u32[]{:S(2)}, u32[]{:S(2)}) collective-permute-start(bf16[128,896]{1,0:T(8,128)(2,1)S(1)} %collective-permute-done.1.refs_1_), channel_id=1, source_target_pairs={{0,4},{4,8},{8,12},{12,16},{16,20},{20,24},{24,28},{28,0},{1,5},{5... | collective-permute-start | bytes 688136 | tf_op jit(solution)/shard_map/ppermute | solution.py:29
  22.7 7.9 %collective-permute-start.7 = (bf16[128,896]{1,0:T(8,128)(2,1)S(1)}, bf16[128,896]{1,0:T(8,128)(2,1)S(1)}, u32[]{:S(2)}, u32[]{:S(2)}) collective-permute-start(bf16[128,896]{1,0:T(8,128)(2,1)S(1)} %collective-permute-done.6.refs_0_), channel_id=1, source_target_pairs={{0,28},{4,0},{8,4},{12,8},{16,12},{20,16},{24,20},{28,24},{1,29},{... | collective-permute-start | bytes 688136 | tf_op jit(solution)/shard_map/ppermute | solution.py:29
  30.5 7.2 %collective-permute-start.3 = (bf16[128,896]{1,0:T(8,128)(2,1)S(1)}, bf16[128,896]{1,0:T(8,128)(2,1)S(1)}, u32[]{:S(2)}, u32[]{:S(2)}) collective-permute-start(bf16[128,896]{1,0:T(8,128)(2,1)S(1)} %collective-permute-done.2.refs_1_), channel_id=1, source_target_pairs={{0,4},{4,8},{8,12},{12,16},{16,20},{20,24},{24,28},{28,0},{1,5},{5... | collective-permute-start | bytes 688136 | tf_op jit(solution)/shard_map/ppermute | solution.py:29
  30.5 32.7 %collective-permute-start.9 = (f32[1024]{0:T(1024)}, f32[1024]{0:T(1024)S(1)}, u32[]{:S(2)}, u32[]{:S(2)}) collective-permute-start(f32[1024]{0:T(1024)} %param.8), channel_id=1, source_target_pairs={{0,1},{1,0},{2,3},{3,2},{4,5},{5,4},{6,7},{7,6},{8,9},{9,8},{10,11... | collective-permute-start | bytes 12296 | tf_op jit(solution)/shard_map/ppermute | solution.py:33
  30.5 19.4 %collective-permute-start.8 = (bf16[128,896]{1,0:T(8,128)(2,1)S(1)}, bf16[128,896]{1,0:T(8,128)(2,1)S(1)}, u32[]{:S(2)}, u32[]{:S(2)}) collective-permute-start(bf16[128,896]{1,0:T(8,128)(2,1)S(1)} %collective-permute-done.7.refs_0_), channel_id=1, source_target_pairs={{0,28},{4,0},{8,4},{12,8},{16,12},{20,16},{24,20},{28,24},{1,29},{... | collective-permute-start | bytes 688136 | tf_op jit(solution)/shard_map/ppermute | solution.py:29
  37.7 16.0 %collective-permute-start.4 = (bf16[128,896]{1,0:T(8,128)(2,1)S(1)}, bf16[128,896]{1,0:T(8,128)(2,1)S(1)}, u32[]{:S(2)}, u32[]{:S(2)}) collective-permute-start(bf16[128,896]{1,0:T(8,128)(2,1)S(1)} %collective-permute-done.3.refs_1_), channel_id=1, source_target_pairs={{0,4},{4,8},{8,12},{12,16},{16,20},{20,24},{24,28},{28,0},{1,5},{5... | collective-permute-start | bytes 688136 | tf_op jit(solution)/shard_map/ppermute | solution.py:29
  53.7 9.5 %copy-start.1 = (f32[1024]{0:T(1024)S(1)}, f32[1024]{0:T(1024)}, u32[]{:S(2)}) copy-start(f32[1024]{0:T(1024)} %param.8) | copy-start | bytes 12292
  57.3 11.2 %all-to-all-start = ((f32[16,1,2048]{2,1,0:T(1,128)}), f32[16,1,2048]{2,1,0:T(1,128)S(1)}, u32[]{:S(2)}, u32[]{:S(2)}) async-start(f32[16,1,2048]{2,1,0:T(1,128)} %copy.15), calls=%async_computation | async-start | bytes 262144 | tf_op jit(solution)/shard_map/all_to_all | solution.py:200
  68.5 13.6 %copy-start = (bf16[1024,768]{1,0:T(8,128)(2,1)S(1)}, bf16[1024,768]{1,0:T(8,128)(2,1)}, u32[]{:S(2)}) copy-start(bf16[1024,768]{1,0:T(8,128)(2,1)} %param.5) | copy-start | bytes 4718596
  76.3 13.4 %all-to-all-start.1 = ((f32[8,1,128]{2,1,0:T(1,128)}), f32[8,1,128]{2,1,0:T(1,128)S(1)}, u32[]{:S(2)}, u32[]{:S(2)}) async-start(f32[8,1,128]{2,1,0:T(1,128)} %bitcast.8), calls=%async_computation.1 | async-start | bytes 8192 | tf_op jit(solution)/shard_map/all_to_all | solution.py:205
  89.8 4.8 %collective-permute-start.10 = (f32[64]{0:T(128)S(1)}, f32[64]{0:T(128)S(1)}, u32[]{:S(2)}, u32[]{:S(2)}) collective-permute-start(f32[64]{0:T(128)S(1)} %slice_bitcast_fusion), channel_id=1, source_target_pairs={{0,34},{34,0},{2,32},{32,2},{1,35},{35,1},{3,33},{33,3},{4,38},{38... | collective-permute-start | bytes 776 | tf_op jit(solution)/shard_map/ppermute | solution.py:37

commit v2 on v0

v2 whole, which is shorter than its diff:
```python
import math

import jax
import jax.numpy as jnp
from jax import lax
from jax.experimental import pallas as pl
from jax.experimental.pallas import tpu as pltpu
from jax.sharding import Mesh, PartitionSpec as P

EPSILON = 0.05
LOG2E = math.log2(math.e)
SCALE = 2.0 / EPSILON * LOG2E
BACK = EPSILON * math.log(2.0)

D = 768
PAD = 128
OWN = 64
UNIT = 2 * OWN
UNITS = 8
ROWS = UNIT * UNITS
HALF = 1024
BLOCK = 256
PARTS = HALF // BLOCK
LANES = 128
PEERS = 16
STEPS = 5
VMEM = 12 * 1024 * 1024
NEAR = 640
IN_VMEM = pl.BlockSpec(memory_space=pltpu.VMEM)
IN_HBM = pl.BlockSpec(memory_space=pl.ANY)
IN_SMEM = pl.BlockSpec(memory_space=pltpu.SMEM)


def whole(*shape):
    return pl.BlockSpec(shape, lambda i: (0,) * len(shape))


def onward(value):
    count = lax.axis_size("z")
    up = [(2 * i, 2 * ((i + 1) % count)) for i in range(count)]
    down = [(2 * i + 1, 2 * ((i - 1) % count) + 1) for i in range(count)]
    return lax.ppermute(value, ("z", "core"), up + down)


def onward_across(value):
    count = lax.axis_size("z")
    up = [(2 * i + 1, 2 * ((i + 1) % count)) for i in range(count)]
    down = [(2 * i, 2 * ((i - 1) % count) + 1) for i in range(count)]
    return lax.ppermute(value, ("z", "core"), up + down)


def other_core(value):
    return lax.ppermute(value, "core", [(0, 1), (1, 0)])


def facing(value):
    return lax.ppermute(value, ("x_lo", "x_hi"), [(0, 3), (3, 0), (1, 2), (2, 1)])


def log_sum2(values):
    peak = jnp.max(values, axis=0, keepdims=True)
    return peak + jnp.log2(jnp.sum(jnp.exp2(values - peak), axis=0, keepdims=True))


def pack_kernel(tgt_ref, pot_ref, logw_ref, own_ref, sq_ref):
    tgt = tgt_ref[...]
    wide = tgt.astype(jnp.float32)
    sq = jnp.sum(wide * wide, axis=1, keepdims=True)
    diagonal = lax.broadcasted_iota(jnp.int32, (OWN, OWN), 0) == lax.broadcasted_iota(
        jnp.int32, (OWN, OWN), 1
    )

    def upright(row):
        return jnp.sum(jnp.where(diagonal, row, 0.0), axis=1, keepdims=True)

    sq_ref[...] = jnp.sum(jnp.where(diagonal, sq, 0.0), axis=0, keepdims=True)
    bias = (upright(logw_ref[...]) + (upright(pot_ref[...]) - sq) / EPSILON) * LOG2E
    high = bias.astype(jnp.bfloat16)
    rest = bias - high.astype(jnp.float32)
    middle = rest.astype(jnp.bfloat16)
    low = rest - middle.astype(jnp.float32)
    lane = lax.broadcasted_iota(jnp.int32, (OWN, PAD), 1)
    pieces = jnp.where(lane == 0, high.astype(jnp.float32), 0.0)
    pieces = jnp.where(lane == 1, middle.astype(jnp.float32), pieces)
    pieces = jnp.where(lane == 2, low, pieces)
    own_ref[:, :D] = tgt
    own_ref[:, D:] = pieces.astype(jnp.bfloat16)


def pack(targets, potential, logw):
    return pl.pallas_call(
        pack_kernel,
        grid=(1,),
        in_specs=[whole(OWN, D), whole(1, OWN), whole(1, OWN)],
        out_specs=[whole(OWN, D + PAD), whole(1, OWN)],
        out_shape=[
            jax.ShapeDtypeStruct((OWN, D + PAD), jnp.bfloat16),
            jax.ShapeDtypeStruct((1, OWN), jnp.float32),
        ],
        compiler_params=pltpu.CompilerParams(vmem_limit_bytes=VMEM),
        name="pack",
    )(targets, potential.reshape(1, OWN), logw.reshape(1, OWN))


def score_rows(group_refs, src_ref, cross_ref, lse_ref, kept_ref, sems):
    group = jnp.concatenate([ref[...] for ref in group_refs], axis=0)
    pieces = group[:, D:].astype(jnp.float32)
    bias = pieces[:, 0:1] + pieces[:, 1:2] + pieces[:, 2:3]
    group = group[:, :D]
    copies = []
    for at in range(PARTS):
        part = slice(at * BLOCK, (at + 1) * BLOCK)
        cross = SCALE * lax.dot_general(
            group,
            src_ref[part, :],
            (((1,), (1,)), ((), ())),
            preferred_element_type=jnp.float32,
        )
        cross_ref[:, part] = cross
        if kept_ref is not None:
            copy = pltpu.make_async_copy(cross_ref.at[:, part], kept_ref.at[:, part], sems.at[at])
            copy.start()
            copies.append(copy)
        lse_ref[:, part] = log_sum2(cross + bias)
    return copies


def row_pass(groups, sources):
    count = len(groups)
    rows = sum(group.shape[0] for group in groups)

    def body(*refs):
        group_refs, (src_ref, kept_ref, lse_ref, cross_ref, sems) = refs[:count], refs[count:]
        for copy in score_rows(group_refs, src_ref, cross_ref, lse_ref, kept_ref, sems):
            copy.wait()

    return pl.pallas_call(
        body,
        in_specs=[IN_VMEM] * (count + 1),
        out_specs=[IN_HBM, IN_VMEM],
        out_shape=[
            pltpu.HBM((rows, HALF), jnp.float32),
            jax.ShapeDtypeStruct((1, HALF), jnp.float32),
        ],
        scratch_shapes=[
            pltpu.VMEM((rows, HALF), jnp.float32),
            pltpu.SemaphoreType.DMA((PARTS,)),
        ],
        compiler_params=pltpu.CompilerParams(vmem_limit_bytes=VMEM),
        cost_estimate=pl.CostEstimate(
            flops=2 * rows * HALF * D,
            bytes_accessed=HALF * D * 2 + rows * HALF * 4,
            transcendentals=rows * HALF,
        ),
        name="rows",
    )(*groups, sources)


def last_kernel(count, earlier_count, *refs):
    x_ref, refs = refs[0], refs[1:]
    group_refs, (src_ref, faced_ref, logw_ref) = refs[:count], refs[count : count + 3]
    refs = refs[count + 3 :]
    earlier, refs = refs[:earlier_count], refs[earlier_count:]
    kept_ref, far_kept_ref, near_ref, lse_ref, cross_ref, far_ref, own_row, faced_row, sems = refs
    copies = score_rows(group_refs[-1:], src_ref, cross_ref, own_row, kept_ref, sems.at[0])
    top = 0
    for at in range(0, count, 2):
        groups = group_refs[at : at + 2]
        rows = sum(ref.shape[0] for ref in groups)
        faced_part = faced_row.at[at // 2 : at // 2 + 1, :]
        if top < NEAR:
            held = near_ref.at[top : top + rows, :]
            score_rows(groups, faced_ref, held, faced_part, None, None)
        else:
            here = slice(top - NEAR, top - NEAR + rows)
            copies += score_rows(
                groups,
                faced_ref,
                far_ref.at[here, :],
                faced_part,
                far_kept_ref.at[here, :],
                sems.at[1 + at // 2],
            )
        top += rows
    own = log_sum2(jnp.concatenate([own_row[...], *[ref[...] for ref in earlier]], axis=0))
    faced = log_sum2(faced_row[...])
    mine = pl.multiple_of(x_ref[0] * HALF, HALF)
    other = pl.multiple_of((1 - x_ref[0]) * HALF, HALF)
    logw = logw_ref[...]
    for peer in range(PEERS):
        lse_ref[peer, :, pl.ds(mine, HALF)] = own
        lse_ref[peer, :, pl.ds(other, HALF)] = faced
        lse_ref[peer, :, 2 * HALF :] = logw
    for copy in copies:
        copy.wait()


def last_pass(x_hi, groups, sources, faced, logw, earlier):
    count = len(groups)
    rows = groups[-1].shape[0]
    passes = (count + 1) // 2

    def body(*refs):
        last_kernel(count, len(earlier), *refs)

    return pl.pallas_call(
        body,
        in_specs=[IN_SMEM] + [IN_VMEM] * (count + 3 + len(earlier)),
        out_specs=[IN_HBM, IN_HBM, IN_VMEM, IN_VMEM],
        out_shape=[
            pltpu.HBM((rows, HALF), jnp.float32),
            pltpu.HBM((ROWS - NEAR, HALF), jnp.float32),
            pltpu.VMEM((NEAR, HALF), jnp.float32),
            pltpu.VMEM((PEERS, 1, 3 * HALF), jnp.float32),
        ],
        scratch_shapes=[
            pltpu.VMEM((rows, HALF), jnp.float32),
            pltpu.VMEM((ROWS - NEAR, HALF), jnp.float32),
            pltpu.VMEM((1, HALF), jnp.float32),
            pltpu.VMEM((passes, HALF), jnp.float32),
            pltpu.SemaphoreType.DMA((1 + passes, PARTS)),
        ],
        compiler_params=pltpu.CompilerParams(vmem_limit_bytes=VMEM),
        cost_estimate=pl.CostEstimate(
            flops=2 * (rows + ROWS) * HALF * D,
            bytes_accessed=HALF * D * 2 + (rows + ROWS) * HALF * 4,
            transcendentals=(rows + ROWS) * HALF,
        ),
        name="last_rows",
    )(x_hi, *groups, sources, faced, logw, *earlier)


def column_kernel(place_ref, *refs):
    own_refs, refs = refs[:STEPS], refs[STEPS:]
    far_ref, near_ref, partial_ref, sq_ref, out_ref, pot_ref, own_held, far_held, sems = refs
    copies, top = [], 0
    for own_ref in own_refs:
        for at in range(0, own_ref.shape[0], UNIT):
            here = slice(top, top + UNIT)
            unit = len(copies)
            fetches = [
                pltpu.make_async_copy(
                    own_ref.at[at : at + UNIT, :], own_held.at[here, :], sems.at[0, unit]
                )
            ]
            if top >= NEAR:
                here = slice(top - NEAR, top - NEAR + UNIT)
                fetches.append(
                    pltpu.make_async_copy(
                        far_ref.at[here, :], far_held.at[here, :], sems.at[1, unit]
                    )
                )
            for fetch in fetches:
                fetch.start()
            copies.append(fetches)
            top += UNIT
    x_hi, z, core = place_ref[0], place_ref[1], place_ref[2]
    mine = pl.multiple_of(x_hi * HALF, HALF)
    other = pl.multiple_of((1 - x_hi) * HALF, HALF)

    def bias(start, peer):
        row = log_sum2(partial_ref[:, 0, pl.ds(start, HALF)])
        logw = partial_ref[pl.ds(peer, 1), 0, 2 * HALF :]
        return row, jnp.broadcast_to(logw * LOG2E - row, (8, HALF))

    row, own_bias = bias(mine, x_hi)
    _, faced_bias = bias(other, 1 - x_hi)
    pot_ref[...] = sq_ref[...] - BACK * row
    side = 2 * core - 1
    top = 0
    for step, own_ref in enumerate(own_refs):
        for at in range(0, own_ref.shape[0], UNIT):
            peaks, totals = [], []
            for copy in copies[top // UNIT]:
                copy.wait()
            for row_at in range(top, top + UNIT, 8):
                scores = own_held[row_at : row_at + 8, :] + own_bias
                pieces = [scores[:, k : k + LANES] for k in range(0, HALF, LANES)]
                if top < NEAR:
                    scores = near_ref[row_at : row_at + 8, :] + faced_bias
                else:
                    scores = far_held[row_at - NEAR : row_at - NEAR + 8, :] + faced_bias
                pieces += [scores[:, k : k + LANES] for k in range(0, HALF, LANES)]
                peak = pieces[0]
                for piece in pieces[1:]:
                    peak = jnp.maximum(peak, piece)
                total = jnp.exp2(pieces[0] - peak)
                for piece in pieces[1:]:
                    total = total + jnp.exp2(piece - peak)
                peaks.append(peak)
                totals.append(total)
            peak = jnp.concatenate(peaks, axis=0).T
            total = jnp.concatenate(totals, axis=0).T
            highest = jnp.max(peak, axis=0, keepdims=True)
            total = jnp.sum(total * jnp.exp2(peak - highest), axis=0, keepdims=True)
            lse = highest + jnp.log2(total)
            top += UNIT
            if step == 0:
                first, second = 2 * z + core, 2 * z + 1 - core
            else:
                chip = lax.rem(z + UNITS + (side if at == 0 else -side) * step, UNITS)
                first, second = 2 * chip, 2 * chip + 1
            out_ref[pl.ds(first, 1)] = lse[:, :OWN].reshape(1, 1, OWN)
            out_ref[pl.ds(second, 1)] = lse[:, OWN:].reshape(1, 1, OWN)


def column_pass(place, own_crosses, far, near, partial, src_sq):
    return pl.pallas_call(
        column_kernel,
        in_specs=[IN_SMEM] + [IN_HBM] * (STEPS + 1) + [IN_VMEM] * 3,
        out_specs=[IN_VMEM] * 2,
        out_shape=[
            jax.ShapeDtypeStruct((PEERS, 1, OWN), jnp.float32),
            jax.ShapeDtypeStruct((1, HALF), jnp.float32),
        ],
        scratch_shapes=[
            pltpu.VMEM((ROWS, HALF), jnp.float32),
            pltpu.VMEM((ROWS - NEAR, HALF), jnp.float32),
            pltpu.SemaphoreType.DMA((2, UNITS)),
        ],
        compiler_params=pltpu.CompilerParams(vmem_limit_bytes=VMEM),
        cost_estimate=pl.CostEstimate(
            flops=12 * ROWS * HALF, bytes_accessed=ROWS * HALF * 8, transcendentals=2 * ROWS * HALF
        ),
        name="columns",
    )(
        place,
        *[pltpu.with_memory_space_constraint(cross, pltpu.HBM) for cross in (*own_crosses, far)],
        pltpu.with_memory_space_constraint(near, pltpu.VMEM),
        partial,
        src_sq,
    )


def on_device(sources, targets, potential_in, source_logw, target_logw):
    place = jnp.stack([lax.axis_index(axis) for axis in ("x_hi", "z", "core")]).astype(jnp.int32)
    faced_sources = facing(sources)
    own, tgt_sq = pack(targets, potential_in, target_logw)
    same, cross_core = onward(own), onward_across(own)
    beside = other_core(own)

    src_sq = jnp.sum(jnp.square(sources.astype(jnp.float32)), axis=1)
    first = lax.axis_index("core") == 0
    unit = jnp.concatenate(
        [jnp.where(first, same, cross_core), jnp.where(first, cross_core, same)], axis=0
    )
    groups, crosses, lses = [], [], []
    pending = [own, beside]
    for step in (1, 2, 3):
        following = onward(unit)
        beside = other_core(unit)
        cross, lse = row_pass(pending, sources)
        groups += pending
        crosses.append(cross)
        lses.append(lse)
        following, lses[-1], src_sq = lax.optimization_barrier((following, lses[-1], src_sq))
        pending = [unit, beside]
        unit = following
    cross, lse = row_pass(pending, sources)
    groups += [*pending, unit]
    crosses.append(cross)
    lses.append(lse)
    cross, far, near, shared = last_pass(
        place, groups, sources, faced_sources, source_logw.reshape(1, HALF), lses
    )
    crosses.append(cross)

    partial = lax.all_to_all(shared, ("y", "x_lo", "x_hi"), 0, 0, tiled=True)
    columns, source_potential = column_pass(
        place, crosses, far, near, partial, src_sq.reshape(1, HALF)
    )
    gathered = lax.all_to_all(columns, ("z", "core"), 0, 0, tiled=True)
    final = log_sum2(gathered.reshape(PEERS, OWN)).reshape(OWN)
    potential_out = tgt_sq.reshape(OWN) - BACK * final
    return (source_potential.reshape(HALF), potential_out)


def solution(mesh):
    every = ("y", "x_lo", "z", "x_hi", "core")
    blk = ("z", "x_hi", "core")
    fine = Mesh(mesh.devices.reshape(4, 2, 8, 2, 2), every)
    in_specs = (P(blk, None), P(every, None), P(every), P(blk), P(every))
    out_specs = (P(blk), P(every))
    return jax.shard_map(
        on_device, mesh=fine, in_specs=in_specs, out_specs=out_specs, check_vma=False
    )
```

time: 599 us -> 81.2 us (0.14)
  starting transfers between devices: 383 us -> 21.8 us
  waiting for transfers between devices: 110 us -> 4.69 us
  matrix products: 42.4 us -> 0 us
  other arithmetic: 23 us -> 2.5 us
  Pallas kernels: 0 us -> 16.5 us
    ppermute x188 -> x10, starting transfers between devices: 383 us -> 21.8 us  [the longest x4 13.4 us: onward(): return lax.ppermute(value, ('z', 'core'), up + down)]
    ppermute x188 -> x10, waiting for transfers between devices: 110 us -> 4.69 us  [the longest x4 3.45 us: onward(): return lax.ppermute(value, ('z', 'core'), up + down)]
    dot_general x64 -> x0, matrix products: 42.4 us -> none  [the longest x32 22.6 us: column_terms(): lax.dot_general(group, sources, (((1,), (1,)), ((), ())), preferred_eleme...]
    all_to_all x0 -> x2, blocking collectives: none -> 32.6 us  [the longest x1 18.3 us: on_device(): gathered = lax.all_to_all(columns, ('z', 'core'), 0, 0, tiled=True)]
    reduce_sum x127 -> x1, other arithmetic: 19.1 us -> 0.03 us  [log_sum2(): jnp.sum(jnp.exp2(values - peak), axis=0, keepdims=True)]
    pallas_call x0 -> x7, Pallas kernels: none -> 16.5 us  [the longest x4 5.97 us: row_pass(): pl.pallas_call(body, in_specs=[IN_VMEM] * (count + 1), out_specs=[IN_HBM,...]
    pmax x1 -> x0, blocking collectives: 15.3 us -> none  [on_device(): highest = lax.pmax(peak, 'grp')]
    psum x1 -> x0, blocking collectives: 12.6 us -> none  [on_device(): total = lax.psum(total * jnp.exp(peak - highest), 'grp')]
  transfers between devices with their start and end apart: 188 -> 10, of which waited for: 60 -> 3; matrix products, arithmetic and copies ran while one was open for 6% -> 2% of each run, Pallas kernels for 0% -> 8%
where the time goes in v2:
time: 81.2 us; the launch traced here: 81 us
  blocking collectives  32.6 us (40%)
  starting transfers between devices  21.8 us (27%)
  Pallas kernels  16.5 us (20%)
  waiting for transfers between devices  4.69 us (6%)
  other arithmetic  2.5 us (3%)
  local copies, waits for them, and re-layouts  2.21 us (3%)
    all_to_all x1, blocking collectives, on_device(): gathered = lax.all_to_all(columns, ('z', 'core'), 0, 0, tiled=True)  18.3 us
    all_to_all x1, blocking collectives, on_device(): partial = lax.all_to_all(shared, ('y', 'x_lo', 'x_hi'), 0, 0, tiled=True)  14.3 us
    ppermute x4, starting transfers between devices, onward(): return lax.ppermute(value, ('z', 'core'), up + down)  13.4 us
    pallas_call x4, Pallas kernels, row_pass(): pl.pallas_call(body, in_specs=[IN_VMEM] * (count + 1), out_specs=[IN_HBM,...  5.97 us
    pallas_call x1, Pallas kernels, last_pass(): pl.pallas_call(body, in_specs=[IN_SMEM] + [IN_VMEM] * (count + 3 + len(ea...  5.45 us
    pallas_call x1, Pallas kernels, column_pass(): pl.pallas_call(column_kernel, in_specs=[IN_SMEM] + [IN_HBM] * (STEPS + 1)...  4.9 us
    ppermute x4, waiting for transfers between devices, onward(): return lax.ppermute(value, ('z', 'core'), up + down)  3.45 us
    ppermute x1, starting transfers between devices, facing(): lax.ppermute(value, ('x_lo', 'x_hi'), [(0, 3), (3, 0), (1, 2), (2, 1)])  3.39 us
  transfers between devices with their start and end apart: 10, of which 3 were waited for; matrix products, arithmetic and copies ran while one was open for 2% of the time, Pallas kernels for 8%

profile of v2, /device:TPU:1, one launch (start us, length us, event | category | flops | bytes accessed | tf_op | source)
XLA Modules:
  0.0 81.0 jit_solution(3932361326769674980)
XLA Ops:
  0.6 0.0 copy-start
  0.6 3.4 %collective-permute-start.9 = (bf16[1024,768]{1,0:T(8,128)(2,1)}, bf16[1024,768]{1,0:T(8,128)(2,1)}, u32[]{:S(2)}, u32[]{:S(2)}) collective-permute-start(bf16[1024,768]{1,0:T(8,128)(2,1)} %refs_10_.1), channel_id=1, source_target_pairs={{0,34},{34,0},{2,32},{32,2},{1,35},{35,1},{3,33},{33,3},{4,38},{38... | collective-permute-start | bytes 4718600 | tf_op jit(solution)/shard_map/ppermute | solution.py:57
  4.0 0.0 copy-start.1
  4.0 0.9 %copy-done.1 = bf16[64,768]{1,0:T(8,128)(2,1)S(1)} copy-done((bf16[64,768]{1,0:T(8,128)(2,1)S(1)}, bf16[64,768]{1,0:T(8,128)(2,1)}, u32[]{:S(2)}) %copy-start.1) | copy-done | bytes 98328
  4.9 0.0 copy-start.2
  4.9 0.7 copy-done.2
  5.6 0.0 copy-start.3
  5.6 0.7 copy-done.3
  6.2 0.1 pack.1
  6.4 2.6 %collective-permute-start.2 = (bf16[64,896]{1,0:T(8,128)(2,1)S(1)}, bf16[64,896]{1,0:T(8,128)(2,1)S(1)}, u32[]{:S(2)}, u32[]{:S(2)}) collective-permute-start(bf16[64,896]{1,0:T(8,128)(2,1)S(1)} %get-tuple-element.27.refs_0_.refs_1_), channel_id=1, source_target_pairs={{1,4},{5,8},{9,12},{13,16},{17,20},{21,24},{25,28},{29,0},{0,29},{... | collective-permute-start | bytes 344072 | tf_op jit(solution)/shard_map/ppermute | solution.py:49
  8.9 3.2 %collective-permute-start.1 = (bf16[64,896]{1,0:T(8,128)(2,1)S(1)}, bf16[64,896]{1,0:T(8,128)(2,1)S(1)}, u32[]{:S(2)}, u32[]{:S(2)}) collective-permute-start(bf16[64,896]{1,0:T(8,128)(2,1)S(1)} %get-tuple-element.27.refs_0_.refs_1_), channel_id=1, source_target_pairs={{0,4},{4,8},{8,12},{12,16},{16,20},{20,24},{24,28},{28,0},{1,29},{... | collective-permute-start | bytes 344072 | tf_op jit(solution)/shard_map/ppermute | solution.py:42
  12.1 0.0 collective-permute-done.2
  12.1 2.6 %collective-permute-done.1 = bf16[64,896]{1,0:T(8,128)(2,1)S(1)} collective-permute-done((bf16[64,896]{1,0:T(8,128)(2,1)S(1)}, bf16[64,896]{1,0:T(8,128)(2,1)S(1)}, u32[]{:S(2)}, u32[]{:S(2)}) %collective-permute-start.1) | collective-permute-done | bytes 114720 | tf_op jit(solution)/shard_map/ppermute | solution.py:42
  14.7 4.0 %collective-permute-start.4 = (bf16[128,896]{1,0:T(8,128)(2,1)S(1)}, bf16[128,896]{1,0:T(8,128)(2,1)S(1)}, u32[]{:S(2)}, u32[]{:S(2)}) collective-permute-start(bf16[128,896]{1,0:T(8,128)(2,1)S(1)} %pad_maximum_fusion.refs_0_.refs_3_), channel_id=1, source_target_pairs={{0,4},{4,8},{8,12},{12,16},{16,20},{20,24},{24,28},{28,0},{1,29},{... | collective-permute-start | bytes 688136 | tf_op jit(solution)/shard_map/ppermute | solution.py:42
  18.7 0.0 collective-permute-start
  18.7 0.5 collective-permute-start.3
  19.3 1.8 %multiply_reduce_fusion = f32[1024]{0:T(1024)S(1)} fusion(bf16[1024,768]{1,0:T(8,128)(2,1)} %refs_10_.1), kind=kLoop, calls=%fused_computation | loop fusion | flops 2358272 | bytes 1576960 | tf_op jit(solution)/shard_map/reduce_sum | solution.py:342
  21.0 0.0 collective-permute-done.refs_1_.refs_2_
  21.1 0.0 copy-done
  21.1 1.4 %rows.4 = (f32[128,1024]{1,0:T(8,128)}, f32[1,1024]{1,0:T(1,128)S(1)}) custom-call(bf16[64,896]{1,0:T(8,128)(2,1)S(1)} %get-tuple-element.27.refs_0_.refs_1_, bf16[64,896]{1,0:T(8,128)(2,1)S(1)} %collective-permute-done.refs_1_.refs_2_, bf16[1024,768]{1,0:T(8,128)(2,1)S(1)} %copy-done), custom_call_target="tpu_custom_call" | custom-call | flops 201326592 | bytes 2097152 | tf_op jit(solution)/shard_map/rows/pallas_call | solution.py:137
  22.5 0.0 collective-permute-done.4.refs_0_.refs_5_
  22.5 2.7 %collective-permute-start.6 = (bf16[128,896]{1,0:T(8,128)(2,1)S(1)}, bf16[128,896]{1,0:T(8,128)(2,1)S(1)}, u32[]{:S(2)}, u32[]{:S(2)}) collective-permute-start(bf16[128,896]{1,0:T(8,128)(2,1)S(1)} %collective-permute-done.4.refs_0_.refs_5_), channel_id=1, source_target_pairs={{0,4},{4,8},{8,12},{12,16},{16,20},{20,24},{24,28},{28,0},{1,29},{... | collective-permute-start | bytes 688136 | tf_op jit(solution)/shard_map/ppermute | solution.py:42
  25.2 0.6 collective-permute-start.5
  25.8 0.0 collective-permute-done.3.refs_1_.refs_4_
  25.8 1.5 %rows.5 = (f32[256,1024]{1,0:T(8,128)}, f32[1,1024]{1,0:T(1,128)S(1)}) custom-call(bf16[128,896]{1,0:T(8,128)(2,1)S(1)} %pad_maximum_fusion.refs_0_.refs_3_, bf16[128,896]{1,0:T(8,128)(2,1)S(1)} %collective-permute-done.3.refs_1_.refs_4_, bf16[1024,768]{1,0:T(8,128)(2,1)S(1)} %copy-done), custom_call_target="tpu_custom_call" | custom-call | flops 402653184 | bytes 2621440 | tf_op jit(solution)/shard_map/rows/pallas_call | solution.py:137
  27.3 0.8 %collective-permute-done.6.refs_0_.refs_7_ = bf16[128,896]{1,0:T(8,128)(2,1)S(1)} collective-permute-done((bf16[128,896]{1,0:T(8,128)(2,1)S(1)}, bf16[128,896]{1,0:T(8,128)(2,1)S(1)}, u32[]{:S(2)}, u32[]{:S(2)}) %collective-permute-start.6) | collective-permute-done | bytes 229408 | tf_op jit(solution)/shard_map/ppermute | solution.py:42
  28.2 3.5 %collective-permute-start.8 = (bf16[128,896]{1,0:T(8,128)(2,1)S(1)}, bf16[128,896]{1,0:T(8,128)(2,1)S(1)}, u32[]{:S(2)}, u32[]{:S(2)}) collective-permute-start(bf16[128,896]{1,0:T(8,128)(2,1)S(1)} %collective-permute-done.6.refs_0_.refs_7_), channel_id=1, source_target_pairs={{0,4},{4,8},{8,12},{12,16},{16,20},{20,24},{24,28},{28,0},{1,29},{... | collective-permute-start | bytes 688136 | tf_op jit(solution)/shard_map/ppermute | solution.py:42
  31.7 1.3 %collective-permute-start.7 = (bf16[128,896]{1,0:T(8,128)(2,1)S(1)}, bf16[128,896]{1,0:T(8,128)(2,1)S(1)}, u32[]{:S(2)}, u32[]{:S(2)}) collective-permute-start(bf16[128,896]{1,0:T(8,128)(2,1)S(1)} %collective-permute-done.6.refs_0_.refs_7_), channel_id=1, source_target_pairs={{0,1},{1,0},{2,3},{3,2},{4,5},{5,4},{6,7},{7,6},{8,9},{9,8},{10,11... | collective-permute-start | bytes 688136 | tf_op jit(solution)/shard_map/ppermute | solution.py:53
  33.0 0.1 pad_add_fusion.refs_0_.place_ref
  33.1 0.0 copy-start.4
  33.1 0.0 collective-permute-done.5.refs_1_.refs_6_
  33.1 1.5 %rows.6 = (f32[256,1024]{1,0:T(8,128)}, f32[1,1024]{1,0:T(1,128)S(1)}) custom-call(bf16[128,896]{1,0:T(8,128)(2,1)S(1)} %collective-permute-done.4.refs_0_.refs_5_, bf16[128,896]{1,0:T(8,128)(2,1)S(1)} %collective-permute-done.5.refs_1_.refs_6_, bf16[1024,768]{1,0:T(8,128)(2,1)S(1)} %copy-done), custom_call_target="tpu_custom_call" | custom-call | flops 402653184 | bytes 2621440 | tf_op jit(solution)/shard_map/rows/pallas_call | solution.py:137
  34.6 0.0 collective-permute-done.8.refs_9_
  34.7 0.0 collective-permute-done.7.refs_1_.refs_8_
  34.7 1.5 %rows.7 = (f32[256,1024]{1,0:T(8,128)}, f32[1,1024]{1,0:T(1,128)S(1)}) custom-call(bf16[128,896]{1,0:T(8,128)(2,1)S(1)} %collective-permute-done.6.refs_0_.refs_7_, bf16[128,896]{1,0:T(8,128)(2,1)S(1)} %collective-permute-done.7.refs_1_.refs_8_, bf16[1024,768]{1,0:T(8,128)(2,1)S(1)} %copy-done), custom_call_target="tpu_custom_call" | custom-call | flops 402653184 | bytes 2621440 | tf_op jit(solution)/shard_map/rows/pallas_call | solution.py:137
  36.2 1.2 %collective-permute-done.9.refs_11_ = bf16[1024,768]{1,0:T(8,128)(2,1)} collective-permute-done((bf16[1024,768]{1,0:T(8,128)(2,1)}, bf16[1024,768]{1,0:T(8,128)(2,1)}, u32[]{:S(2)}, u32[]{:S(2)}) %collective-permute-start.9) | collective-permute-done | bytes 1572896 | tf_op jit(solution)/shard_map/ppermute | solution.py:57
  37.4 0.0 copy-done.4
  37.4 5.5 %last_rows.1 = (f32[128,1024]{1,0:T(8,128)}, f32[384,1024]{1,0:T(8,128)}, f32[640,1024]{1,0:T(8,128)S(1)}, f32[16,1,3072]{2,1,0:T(1,128)S(1)}) custom-call(s32[3]{0:T(128)S(1)} %pad_add_fusion.refs_0_.place_ref, bf16[64,896]{1,0:T(8,128)(2,1)S(1)} %get-tuple-element.27.refs_0_.refs_1_, bf16[64,896]{1,0:T(8,128)(2,1)S(1)} %collective-permute-done.refs_1_.refs_2_, ...), custom_call_target="tpu_custom_call" | custom-call | flops 1811939328 | bytes 6291456 | tf_op jit(solution)/shard_map/last_rows/pallas_call | solution.py:206
  42.9 14.3 %all_to_all.10.refs_7_ = f32[16,1,3072]{2,1,0:T(1,128)S(1)} all-to-all(f32[16,1,3072]{2,1,0:T(1,128)S(1)} %get-tuple-element.47), channel_id=1, replica_groups=mesh['y'=4,'x_lo'=2,'z'=8,'x_hi'=2,'core'=2] {'y','x_lo','x_hi'}, dimensions={0} | all-to-all | bytes 393216 | tf_op jit(solution)/shard_map/all_to_all | solution.py:368
  57.2 4.9 %columns.1 = (f32[16,1,64]{2,1,0:T(1,128)S(1)}, f32[1,1024]{1,0:T(1,128)}) custom-call(s32[3]{0:T(128)S(1)} %pad_add_fusion.refs_0_.place_ref, f32[128,1024]{1,0:T(8,128)} %get-tuple-element.28.refs_0_, f32[256,1024]{1,0:T(8,128)} %get-tuple-element.29.refs_1_, f32[256,1024]{1,0:T(8,128)} %get-tuple-element.32.refs_2_, ...), custom_call_target="tpu_custom_call" | custom-call | flops 12582912 | bytes 8388608 | tf_op jit(solution)/shard_map/columns/pallas_call | solution.py:308
  62.1 18.3 %all_to_all.11 = f32[16,1,64]{2,1,0:T(1,128)S(1)} all-to-all(f32[16,1,64]{2,1,0:T(1,128)S(1)} %get-tuple-element.51), channel_id=1, replica_groups=mesh['y'=4,'x_lo'=2,'z'=8,'x_hi'=2,'core'=2] {'z','core'}, dimensions={0} | all-to-all | bytes 8192 | tf_op jit(solution)/shard_map/all_to_all | solution.py:372
  80.4 0.5 bitcast_subtract_fusion
  (4 shorter events, 0.1 us)
Async XLA Ops:
  0.6 20.4 %copy-start = (bf16[1024,768]{1,0:T(8,128)(2,1)S(1)}, bf16[1024,768]{1,0:T(8,128)(2,1)}, u32[]{:S(2)}) copy-start(bf16[1024,768]{1,0:T(8,128)(2,1)} %refs_10_.1) | copy-start | bytes 4718596
  0.6 36.8 %collective-permute-start.9 = (bf16[1024,768]{1,0:T(8,128)(2,1)}, bf16[1024,768]{1,0:T(8,128)(2,1)}, u32[]{:S(2)}, u32[]{:S(2)}) collective-permute-start(bf16[1024,768]{1,0:T(8,128)(2,1)} %refs_10_.1), channel_id=1, source_target_pairs={{0,34},{34,0},{2,32},{32,2},{1,35},{35,1},{3,33},{33,3},{4,38},{38... | collective-permute-start | bytes 4718600 | tf_op jit(solution)/shard_map/ppermute | solution.py:57
  4.0 0.9 %copy-start.1 = (bf16[64,768]{1,0:T(8,128)(2,1)S(1)}, bf16[64,768]{1,0:T(8,128)(2,1)}, u32[]{:S(2)}) copy-start(bf16[64,768]{1,0:T(8,128)(2,1)} %tgt_ref.1) | copy-start | bytes 294916
  4.9 0.7 copy-start.2
  5.6 0.7 copy-start.3
  6.4 5.8 %collective-permute-start.2 = (bf16[64,896]{1,0:T(8,128)(2,1)S(1)}, bf16[64,896]{1,0:T(8,128)(2,1)S(1)}, u32[]{:S(2)}, u32[]{:S(2)}) collective-permute-start(bf16[64,896]{1,0:T(8,128)(2,1)S(1)} %get-tuple-element.27.refs_0_.refs_1_), channel_id=1, source_target_pairs={{1,4},{5,8},{9,12},{13,16},{17,20},{21,24},{25,28},{29,0},{0,29},{... | collective-permute-start | bytes 344072 | tf_op jit(solution)/shard_map/ppermute | solution.py:49
  8.9 5.7 %collective-permute-start.1 = (bf16[64,896]{1,0:T(8,128)(2,1)S(1)}, bf16[64,896]{1,0:T(8,128)(2,1)S(1)}, u32[]{:S(2)}, u32[]{:S(2)}) collective-permute-start(bf16[64,896]{1,0:T(8,128)(2,1)S(1)} %get-tuple-element.27.refs_0_.refs_1_), channel_id=1, source_target_pairs={{0,4},{4,8},{8,12},{12,16},{16,20},{20,24},{24,28},{28,0},{1,29},{... | collective-permute-start | bytes 344072 | tf_op jit(solution)/shard_map/ppermute | solution.py:42
  14.7 7.8 %collective-permute-start.4 = (bf16[128,896]{1,0:T(8,128)(2,1)S(1)}, bf16[128,896]{1,0:T(8,128)(2,1)S(1)}, u32[]{:S(2)}, u32[]{:S(2)}) collective-permute-start(bf16[128,896]{1,0:T(8,128)(2,1)S(1)} %pad_maximum_fusion.refs_0_.refs_3_), channel_id=1, source_target_pairs={{0,4},{4,8},{8,12},{12,16},{16,20},{20,24},{24,28},{28,0},{1,29},{... | collective-permute-start | bytes 688136 | tf_op jit(solution)/shard_map/ppermute | solution.py:42
  18.7 2.3 %collective-permute-start = (bf16[64,896]{1,0:T(8,128)(2,1)S(1)}, bf16[64,896]{1,0:T(8,128)(2,1)S(1)}, u32[]{:S(2)}, u32[]{:S(2)}) collective-permute-start(bf16[64,896]{1,0:T(8,128)(2,1)S(1)} %get-tuple-element.27.refs_0_.refs_1_), channel_id=1, source_target_pairs={{0,1},{1,0},{2,3},{3,2},{4,5},{5,4},{6,7},{7,6},{8,9},{9,8},{10,11... | collective-permute-start | bytes 344072 | tf_op jit(solution)/shard_map/ppermute | solution.py:53
  18.7 7.1 %collective-permute-start.3 = (bf16[128,896]{1,0:T(8,128)(2,1)S(1)}, bf16[128,896]{1,0:T(8,128)(2,1)S(1)}, u32[]{:S(2)}, u32[]{:S(2)}) collective-permute-start(bf16[128,896]{1,0:T(8,128)(2,1)S(1)} %pad_maximum_fusion.refs_0_.refs_3_), channel_id=1, source_target_pairs={{0,1},{1,0},{2,3},{3,2},{4,5},{5,4},{6,7},{7,6},{8,9},{9,8},{10,11... | collective-permute-start | bytes 688136 | tf_op jit(solution)/shard_map/ppermute | solution.py:53
  22.5 5.7 %collective-permute-start.6 = (bf16[128,896]{1,0:T(8,128)(2,1)S(1)}, bf16[128,896]{1,0:T(8,128)(2,1)S(1)}, u32[]{:S(2)}, u32[]{:S(2)}) collective-permute-start(bf16[128,896]{1,0:T(8,128)(2,1)S(1)} %collective-permute-done.4.refs_0_.refs_5_), channel_id=1, source_target_pairs={{0,4},{4,8},{8,12},{12,16},{16,20},{20,24},{24,28},{28,0},{1,29},{... | collective-permute-start | bytes 688136 | tf_op jit(solution)/shard_map/ppermute | solution.py:42
  25.2 7.9 %collective-permute-start.5 = (bf16[128,896]{1,0:T(8,128)(2,1)S(1)}, bf16[128,896]{1,0:T(8,128)(2,1)S(1)}, u32[]{:S(2)}, u32[]{:S(2)}) collective-permute-start(bf16[128,896]{1,0:T(8,128)(2,1)S(1)} %collective-permute-done.4.refs_0_.refs_5_), channel_id=1, source_target_pairs={{0,1},{1,0},{2,3},{3,2},{4,5},{5,4},{6,7},{7,6},{8,9},{9,8},{10,11... | collective-permute-start | bytes 688136 | tf_op jit(solution)/shard_map/ppermute | solution.py:53
  28.2 6.5 %collective-permute-start.8 = (bf16[128,896]{1,0:T(8,128)(2,1)S(1)}, bf16[128,896]{1,0:T(8,128)(2,1)S(1)}, u32[]{:S(2)}, u32[]{:S(2)}) collective-permute-start(bf16[128,896]{1,0:T(8,128)(2,1)S(1)} %collective-permute-done.6.refs_0_.refs_7_), channel_id=1, source_target_pairs={{0,4},{4,8},{8,12},{12,16},{16,20},{20,24},{24,28},{28,0},{1,29},{... | collective-permute-start | bytes 688136 | tf_op jit(solution)/shard_map/ppermute | solution.py:42
  31.7 3.0 %collective-permute-start.7 = (bf16[128,896]{1,0:T(8,128)(2,1)S(1)}, bf16[128,896]{1,0:T(8,128)(2,1)S(1)}, u32[]{:S(2)}, u32[]{:S(2)}) collective-permute-start(bf16[128,896]{1,0:T(8,128)(2,1)S(1)} %collective-permute-done.6.refs_0_.refs_7_), channel_id=1, source_target_pairs={{0,1},{1,0},{2,3},{3,2},{4,5},{5,4},{6,7},{7,6},{8,9},{9,8},{10,11... | collective-permute-start | bytes 688136 | tf_op jit(solution)/shard_map/ppermute | solution.py:53
  33.1 4.3 %copy-start.4 = (f32[1024]{0:T(1024)S(1)}, f32[1024]{0:T(1024)}, u32[]{:S(2)}) copy-start(f32[1024]{0:T(1024)} %param.8) | copy-start | bytes 12292

commit v3 on v2

v3 whole, which is shorter than its diff:
```python
import math

import jax
import jax.numpy as jnp
from jax import lax
from jax.experimental import pallas as pl
from jax.experimental.pallas import tpu as pltpu
from jax.sharding import Mesh, PartitionSpec as P

EPSILON = 0.05
LOG2E = math.log2(math.e)
SCALE = 2.0 / EPSILON * LOG2E
BACK = EPSILON * math.log(2.0)

D = 768
PAD = 128
OWN = 64
UNIT = 2 * OWN
UNITS = 8
ROWS = UNIT * UNITS
HALF = 1024
BLOCK = 512
LANES = 128
PEERS = 16
X_HI, Z, CORE, ODD = range(4)
STEPS = 5
VMEM = 12 * 1024 * 1024
EDGE = HALF // 4
EXTRA = 16
REST = ROWS - UNIT
IN_VMEM = pl.BlockSpec(memory_space=pltpu.VMEM)
IN_HBM = pl.BlockSpec(memory_space=pl.ANY)
IN_SMEM = pl.BlockSpec(memory_space=pltpu.SMEM)


def whole(*shape):
    return pl.BlockSpec(shape, lambda i: (0,) * len(shape))


def onward(value):
    count = lax.axis_size("z")
    up = [(2 * i, 2 * ((i + 1) % count)) for i in range(count)]
    down = [(2 * i + 1, 2 * ((i - 1) % count) + 1) for i in range(count)]
    return lax.ppermute(value, ("z", "core"), up + down)


def onward_across(value):
    count = lax.axis_size("z")
    up = [(2 * i + 1, 2 * ((i + 1) % count)) for i in range(count)]
    down = [(2 * i, 2 * ((i - 1) % count) + 1) for i in range(count)]
    return lax.ppermute(value, ("z", "core"), up + down)


def other_core(value):
    return lax.ppermute(value, "core", [(0, 1), (1, 0)])


def facing(value):
    return lax.ppermute(value, ("x_lo", "x_hi"), [(0, 3), (3, 0), (1, 2), (2, 1)])


def beside_y(value):
    return lax.ppermute(value, "y", [(0, 1), (1, 0), (2, 3), (3, 2)])


def log_sum2(values):
    peak = jnp.max(values, axis=0, keepdims=True)
    return peak + jnp.log2(jnp.sum(jnp.exp2(values - peak), axis=0, keepdims=True))


def split(values):
    high = values.astype(jnp.bfloat16).astype(jnp.float32)
    rest = values - high
    middle = rest.astype(jnp.bfloat16).astype(jnp.float32)
    return high, middle, rest - middle


def pack_kernel(place_ref, src_hbm, tgt_hbm, pot_hbm, logw_hbm, *refs):
    src_logw_hbm, own_ref, sq_ref, edge_ref, tgt_ref, pot_ref, logw_ref, src_logw_ref, sems = refs
    copies = [
        pltpu.make_async_copy(source, target, sems.at[at])
        for at, (source, target) in enumerate(
            (
                (tgt_hbm, tgt_ref),
                (pot_hbm, pot_ref),
                (logw_hbm, logw_ref),
                (src_logw_hbm, src_logw_ref),
            )
        )
    ]
    for copy in copies:
        copy.start()
    start = pl.multiple_of(place_ref[ODD] * (HALF - EDGE), EDGE)
    edge = pltpu.make_async_copy(
        src_hbm.at[pl.ds(start, EDGE), :], edge_ref.at[:EDGE, :], sems.at[4]
    )
    edge.start()
    for copy in copies:
        copy.wait()
    tgt = tgt_ref[...]
    wide = tgt.astype(jnp.float32)
    sq = jnp.sum(wide * wide, axis=1, keepdims=True)
    diagonal = lax.broadcasted_iota(jnp.int32, (OWN, OWN), 0) == lax.broadcasted_iota(
        jnp.int32, (OWN, OWN), 1
    )

    def upright(row):
        return jnp.sum(jnp.where(diagonal, row, 0.0), axis=1, keepdims=True)

    sq_ref[...] = jnp.sum(jnp.where(diagonal, sq, 0.0), axis=0, keepdims=True)
    bias = (upright(logw_ref[...]) + (upright(pot_ref[...]) - sq) / EPSILON) * LOG2E
    high, middle, low = split(bias)
    lane = lax.broadcasted_iota(jnp.int32, (OWN, PAD), 1)
    pieces = jnp.where(lane == 0, high, 0.0)
    pieces = jnp.where(lane == 1, middle, pieces)
    pieces = jnp.where(lane == 2, low, pieces)
    own_ref[:, :D] = tgt
    own_ref[:, D:] = pieces.astype(jnp.bfloat16)
    line = lax.broadcasted_iota(jnp.int32, (EXTRA, D), 0)
    extra = jnp.zeros((EXTRA, D), jnp.float32)
    for quarter in range(HALF // EDGE):
        part = src_logw_ref[:, quarter * EDGE : (quarter + 1) * EDGE]
        row = jnp.concatenate(split(part), axis=1)
        extra = jnp.where(line == quarter, row, extra)
    edge_ref[EDGE:, :] = extra.astype(jnp.bfloat16)
    edge.wait()


def in_hbm(*values):
    return [pltpu.with_memory_space_constraint(value, pltpu.HBM) for value in values]


def pack(place, sources, targets, potential, logw, src_logw):
    return pl.pallas_call(
        pack_kernel,
        in_specs=[IN_SMEM] + [IN_HBM] * 5,
        out_specs=[IN_VMEM] * 3,
        out_shape=[
            jax.ShapeDtypeStruct((OWN, D + PAD), jnp.bfloat16),
            jax.ShapeDtypeStruct((1, OWN), jnp.float32),
            jax.ShapeDtypeStruct((EDGE + EXTRA, D), jnp.bfloat16),
        ],
        scratch_shapes=[
            pltpu.VMEM((OWN, D), jnp.bfloat16),
            pltpu.VMEM((1, OWN), jnp.float32),
            pltpu.VMEM((1, OWN), jnp.float32),
            pltpu.VMEM((1, HALF), jnp.float32),
            pltpu.SemaphoreType.DMA((5,)),
        ],
        compiler_params=pltpu.CompilerParams(vmem_limit_bytes=VMEM),
        name="pack",
    )(
        place,
        *in_hbm(
            sources,
            targets,
            potential.reshape(1, OWN),
            logw.reshape(1, OWN),
            src_logw.reshape(1, HALF),
        ),
    )


def score_rows(group_refs, src_refs, cross_ref, lse_ref):
    group = jnp.concatenate([ref[...] for ref in group_refs], axis=0)
    pieces = group[:, D:].astype(jnp.float32)
    bias = pieces[:, 0:1] + pieces[:, 1:2] + pieces[:, 2:3]
    group = group[:, :D]
    place = 0
    for src_ref in src_refs:
        height = src_ref.shape[0] // EDGE * EDGE
        rows = min(BLOCK, height)
        for start in range(0, height, rows):
            cross = SCALE * lax.dot_general(
                group,
                src_ref[start : start + rows, :],
                (((1,), (1,)), ((), ())),
                preferred_element_type=jnp.float32,
            )
            cross_ref[:, place : place + rows] = cross
            lse_ref[:, place : place + rows] = log_sum2(cross + bias)
            place += rows


def row_pass(groups, sources):
    count, parts = len(groups), len(sources)
    small = 2 if parts > 1 else 1
    rows = sum(group.shape[0] for group in groups)
    passes = (count + 1) // 2

    def body(*refs):
        group_refs, src_refs, refs = (
            refs[:count],
            refs[count : count + parts],
            refs[count + parts :],
        )
        kept_ref, lse_ref, *logw_refs, cross_ref, row_ref, sems = refs
        for logw_ref in logw_refs:
            extra = src_refs[0][EDGE:, :].astype(jnp.float32)
            sums = extra[:, :EDGE] + extra[:, EDGE : 2 * EDGE] + extra[:, 2 * EDGE :]
            for quarter in range(HALF // EDGE):
                here = slice(quarter * EDGE, (quarter + 1) * EDGE)
                logw_ref[:, here] = sums[quarter : quarter + 1, :]
        copies, top = [], 0
        for at in range(passes):
            pair = group_refs[2 * at : 2 * at + 2]
            here = slice(top, top + sum(ref.shape[0] for ref in pair))
            score_rows(pair, src_refs, cross_ref.at[here, :], row_ref.at[at : at + 1, :])
            copies.append(
                pltpu.make_async_copy(cross_ref.at[here, :], kept_ref.at[here, :], sems.at[at])
            )
            copies[-1].start()
            top = here.stop
        lse_ref[...] = log_sum2(row_ref[...])
        for copy in copies:
            copy.wait()

    return pl.pallas_call(
        body,
        in_specs=[IN_VMEM] * (count + parts),
        out_specs=[IN_HBM] + [IN_VMEM] * small,
        out_shape=[pltpu.HBM((rows, HALF), jnp.float32)]
        + [jax.ShapeDtypeStruct((1, HALF), jnp.float32)] * small,
        scratch_shapes=[
            pltpu.VMEM((rows, HALF), jnp.float32),
            pltpu.VMEM((passes, HALF), jnp.float32),
            pltpu.SemaphoreType.DMA((passes,)),
        ],
        compiler_params=pltpu.CompilerParams(vmem_limit_bytes=VMEM),
        cost_estimate=pl.CostEstimate(flops=1, bytes_accessed=1, transcendentals=0),
        name="rows",
    )(*groups, *sources)


def edge_places(place_ref):
    straight = pl.multiple_of(place_ref[ODD] * (HALF - EDGE), EDGE)
    return straight, pl.multiple_of((1 - place_ref[ODD]) * (HALF - EDGE), EDGE)


def last_kernel(place_ref, group_ref, *refs):
    own_refs, faced_refs, (faced_earlier, *earlier), refs = (
        refs[:1],
        refs[1:4],
        refs[4 : 4 + STEPS],
        refs[4 + STEPS :],
    )
    cross_ref, lse_ref, own_row, faced_row = refs
    score_rows([group_ref], own_refs, cross_ref.at[:, :HALF], own_row)
    score_rows([group_ref], faced_refs, cross_ref.at[:, HALF:], faced_row)
    own = log_sum2(jnp.concatenate([own_row[...], *[ref[...] for ref in earlier]], axis=0))
    faced = log_sum2(jnp.concatenate([faced_row[...], faced_earlier[...]], axis=0))
    mine = pl.multiple_of(place_ref[X_HI] * HALF, HALF)
    other = pl.multiple_of((1 - place_ref[X_HI]) * HALF, HALF)
    straight, around = edge_places(place_ref)
    for peer in range(PEERS):
        lse_ref[peer, :, pl.ds(mine, HALF)] = own
        lse_ref[peer, :, pl.ds(other + straight, EDGE)] = faced[:, :EDGE]
        lse_ref[peer, :, pl.ds(other + EDGE, HALF - 2 * EDGE)] = faced[:, EDGE : HALF - EDGE]
        lse_ref[peer, :, pl.ds(other + around, EDGE)] = faced[:, HALF - EDGE :]


def last_pass(place, group, sources, faced, faced_earlier, earlier):
    work = 2 * UNIT * HALF
    return pl.pallas_call(
        last_kernel,
        in_specs=[IN_SMEM] + [IN_VMEM] * (6 + len(earlier)),
        out_specs=[IN_VMEM] * 2,
        out_shape=[
            pltpu.VMEM((UNIT, 2 * HALF), jnp.float32),
            pltpu.VMEM((PEERS, 1, 2 * HALF), jnp.float32),
        ],
        scratch_shapes=[
            pltpu.VMEM((1, HALF), jnp.float32),
            pltpu.VMEM((1, HALF), jnp.float32),
        ],
        compiler_params=pltpu.CompilerParams(vmem_limit_bytes=VMEM),
        cost_estimate=pl.CostEstimate(
            flops=2 * work * D, bytes_accessed=HALF * D * 4 + work * 4, transcendentals=work
        ),
        name="last_rows",
    )(place, group, sources, *faced, faced_earlier, *earlier)


def column_kernel(heights, place_ref, *refs):
    own_kept, refs = refs[: len(heights)], refs[len(heights) :]
    faced_kept, near_ref, partial_ref, sq_ref, logw_ref, faced_logw_ref = refs[:6]
    out_ref, pot_ref, own_held, faced_held, sems = refs[6:]
    copies, top = [], 0
    for height, own_ref in zip(heights, own_kept):
        for start in range(0, height, UNIT):
            here = slice(top, top + UNIT)
            at = len(copies)
            copies.append(
                (
                    pltpu.make_async_copy(
                        own_ref.at[start : start + UNIT, :], own_held.at[here, :], sems.at[0, at]
                    ),
                    pltpu.make_async_copy(
                        faced_kept.at[here, :], faced_held.at[here, :], sems.at[1, at]
                    ),
                )
            )
            top += UNIT
    for pair in copies:
        for copy in pair:
            copy.start()
    z, core = place_ref[Z], place_ref[CORE]
    mine = pl.multiple_of(place_ref[X_HI] * HALF, HALF)
    other = pl.multiple_of((1 - place_ref[X_HI]) * HALF, HALF)
    straight, around = edge_places(place_ref)

    row = log_sum2(partial_ref[:, 0, pl.ds(mine, HALF)])
    own_bias = logw_ref[...] * LOG2E - row
    pot_ref[...] = sq_ref[...] - BACK * row
    own_bias = jnp.broadcast_to(own_bias, (8, HALF))
    faced_bias = [
        faced_logw_ref[:, pl.ds(start, width)] * LOG2E
        - log_sum2(partial_ref[:, 0, pl.ds(other + start, width)])
        for start, width in ((straight, EDGE), (EDGE, HALF - 2 * EDGE), (around, EDGE))
    ]
    faced_bias = jnp.broadcast_to(jnp.concatenate(faced_bias, axis=1), (8, HALF))
    side = 2 * core - 1
    for unit in (UNITS - 1, *range(UNITS - 1)):
        if unit < len(copies):
            for copy in copies[unit]:
                copy.wait()
            own_ref, faced_ref, top = own_held, faced_held, unit * UNIT
        else:
            own_ref, faced_ref, top = near_ref.at[:, :HALF], near_ref.at[:, HALF:], 0
        peaks, totals = [], []
        for at in range(top, top + UNIT, 8):
            pieces = []
            for ref, added in ((own_ref, own_bias), (faced_ref, faced_bias)):
                scores = ref[at : at + 8, :] + added
                pieces += [scores[:, k : k + LANES] for k in range(0, HALF, LANES)]
            peak = pieces[0]
            for piece in pieces[1:]:
                peak = jnp.maximum(peak, piece)
            total = jnp.exp2(pieces[0] - peak)
            for piece in pieces[1:]:
                total = total + jnp.exp2(piece - peak)
            peaks.append(peak)
            totals.append(total)
        peak = jnp.concatenate(peaks, axis=0).T
        total = jnp.concatenate(totals, axis=0).T
        highest = jnp.max(peak, axis=0, keepdims=True)
        total = jnp.sum(total * jnp.exp2(peak - highest), axis=0, keepdims=True)
        lse = highest + jnp.log2(total)
        if unit == 0:
            first, second = 2 * z + core, 2 * z + 1 - core
        else:
            step = (unit + 1) // 2
            chip = lax.rem(z + UNITS + (side if unit % 2 else -side) * step, UNITS)
            first, second = 2 * chip, 2 * chip + 1
        out_ref[pl.ds(first, 1)] = lse[:, :OWN].reshape(1, 1, OWN)
        out_ref[pl.ds(second, 1)] = lse[:, OWN:].reshape(1, 1, OWN)


def column_pass(place, own_crosses, faced_cross, near, partial, *rows):
    heights = [cross.shape[0] for cross in own_crosses]

    def body(*refs):
        column_kernel(heights, *refs)

    return pl.pallas_call(
        body,
        in_specs=[IN_SMEM] + [IN_HBM] * (len(own_crosses) + 1) + [IN_VMEM] * 5,
        out_specs=[IN_VMEM] * 2,
        out_shape=[
            jax.ShapeDtypeStruct((PEERS, 1, OWN), jnp.float32),
            jax.ShapeDtypeStruct((1, HALF), jnp.float32),
        ],
        scratch_shapes=[
            pltpu.VMEM((REST, HALF), jnp.float32),
            pltpu.VMEM((REST, HALF), jnp.float32),
            pltpu.SemaphoreType.DMA((2, UNITS - 1)),
        ],
        compiler_params=pltpu.CompilerParams(vmem_limit_bytes=VMEM),
        cost_estimate=pl.CostEstimate(
            flops=12 * ROWS * HALF, bytes_accessed=ROWS * HALF * 8, transcendentals=2 * ROWS * HALF
        ),
        name="columns",
    )(
        place,
        *in_hbm(*own_crosses, faced_cross),
        pltpu.with_memory_space_constraint(near, pltpu.VMEM),
        partial,
        *[row.reshape(1, HALF) for row in rows],
    )


def on_device(sources, targets, potential_in, source_logw, target_logw):
    place = jnp.stack(
        [
            lax.axis_index("x_hi"),
            lax.axis_index("z"),
            lax.axis_index("core"),
            lax.axis_index("y") % 2,
        ]
    ).astype(jnp.int32)
    own, tgt_sq, edge = pack(
        place, sources, targets, potential_in, target_logw, source_logw
    )
    straight = facing(edge)
    same, cross_core = onward(own), onward_across(own)
    middle = facing(sources[EDGE : HALF - EDGE])
    beside = other_core(own)

    first = lax.axis_index("core") == 0
    unit = jnp.concatenate(
        [jnp.where(first, same, cross_core), jnp.where(first, cross_core, same)], axis=0
    )
    src_sq = jnp.sum(jnp.square(sources.astype(jnp.float32)), axis=1)
    groups, crosses, lses = [], [], []
    pending = [own, beside]
    for step in (1, 2, 3):
        following = onward(unit)
        beside = other_core(unit)
        if step == 1:
            around = beside_y(straight)
        cross, lse = row_pass(pending, [sources])
        groups += pending
        crosses.append(cross)
        if step == 1:
            following, lse, src_sq = lax.optimization_barrier((following, lse, src_sq))
        else:
            following, lse = lax.optimization_barrier((following, lse))
        lses.append(lse)
        pending = [unit, beside]
        unit = following
    cross, lse = row_pass(pending, [sources])
    groups += pending
    crosses.append(cross)
    faced = [straight, middle, around]
    faced_cross, faced_lse, faced_logw = row_pass(groups, faced)
    unit, lse, faced_lse = lax.optimization_barrier((unit, lse, faced_lse))
    lses.append(lse)
    near, shared = last_pass(place, unit, sources, faced, faced_lse, lses)

    partial = lax.all_to_all(shared, ("y", "x_lo", "x_hi"), 0, 0, tiled=True)
    columns, source_potential = column_pass(
        place, crosses, faced_cross, near, partial, src_sq, source_logw, faced_logw
    )
    gathered = lax.all_to_all(columns, ("z", "core"), 0, 0, tiled=True)
    final = log_sum2(gathered.reshape(PEERS, OWN)).reshape(OWN)
    potential_out = tgt_sq.reshape(OWN) - BACK * final
    return (source_potential.reshape(HALF), potential_out)


def solution(mesh):
    every = ("y", "x_lo", "z", "x_hi", "core")
    blk = ("z", "x_hi", "core")
    fine = Mesh(mesh.devices.reshape(4, 2, 8, 2, 2), every)
    in_specs = (P(blk, None), P(every, None), P(every), P(blk), P(every))
    out_specs = (P(blk), P(every))
    return jax.shard_map(
        on_device, mesh=fine, in_specs=in_specs, out_specs=out_specs, check_vma=False
    )
```

time: 81.2 us -> 76 us (0.936)
  blocking collectives: 32.6 us -> 28.3 us
  other arithmetic: 2.5 us -> 1.09 us
  Pallas kernels: 16.5 us -> 17.9 us
    ppermute x4, starting transfers between devices: 2.41 us -> 6.26 us  [other_core(): return lax.ppermute(value, 'core', [(0, 1), (1, 0)])]
    all_to_all x1, blocking collectives: 18.3 us -> 15.2 us  [on_device(): gathered = lax.all_to_all(columns, ('z', 'core'), 0, 0, tiled=True)]
    ppermute x1, starting transfers between devices: 2.56 us -> 0.01 us  [onward_across(): return lax.ppermute(value, ('z', 'core'), up + down)]
    ppermute x4, starting transfers between devices: 13.4 us -> 11.1 us  [onward(): return lax.ppermute(value, ('z', 'core'), up + down)]
    unnamed x10 -> x4, local copies, waits for them, and re-layouts: 2.21 us -> 0.01 us
    slice x0 -> x1, local copies, waits for them, and re-layouts: none -> 2.09 us  [on_device(): middle = facing(sources[EDGE:HALF - EDGE])]
    ppermute x4, waiting for transfers between devices: 3.45 us -> 1.87 us  [onward(): return lax.ppermute(value, ('z', 'core'), up + down)]
    pallas_call x7 -> x8, Pallas kernels: 16.5 us -> 17.9 us  [the longest x5 9.49 us: row_pass(): pl.pallas_call(body, in_specs=[IN_VMEM] * (count + parts), out_specs=[IN_...]
  transfers between devices with their start and end apart: 10 -> 12, of which waited for: 3 -> 3; matrix products, arithmetic and copies ran while one was open for 2% -> 3% of each run, Pallas kernels for 8% -> 8%
where the time goes in v3:
time: 76 us; the launch traced here: 75.8 us
  blocking collectives  28.3 us (37%)
  starting transfers between devices  21.3 us (28%)
  Pallas kernels  17.9 us (24%)
  waiting for transfers between devices  4.21 us (6%)
  local copies, waits for them, and re-layouts  2.1 us (3%)
  other arithmetic  1.09 us (1%)
  between operations  0.77 us (1%)
    all_to_all x1, blocking collectives, on_device(): gathered = lax.all_to_all(columns, ('z', 'core'), 0, 0, tiled=True)  15.2 us
    all_to_all x1, blocking collectives, on_device(): partial = lax.all_to_all(shared, ('y', 'x_lo', 'x_hi'), 0, 0, tiled=True)  13.2 us
    ppermute x4, starting transfers between devices, onward(): return lax.ppermute(value, ('z', 'core'), up + down)  11.1 us
    pallas_call x5, Pallas kernels, row_pass(): pl.pallas_call(body, in_specs=[IN_VMEM] * (count + parts), out_specs=[IN_...  9.49 us
    ppermute x4, starting transfers between devices, other_core(): return lax.ppermute(value, 'core', [(0, 1), (1, 0)])  6.26 us
    pallas_call x1, Pallas kernels, column_pass(): pl.pallas_call(body, in_specs=[IN_SMEM] + [IN_HBM] * (len(own_crosses) +...  4.84 us
    ppermute x2, starting transfers between devices, facing(): lax.ppermute(value, ('x_lo', 'x_hi'), [(0, 3), (3, 0), (1, 2), (2, 1)])  2.68 us
    slice x1, local copies, waits for them, and re-layouts, on_device(): middle = facing(sources[EDGE:HALF - EDGE])  2.09 us
  transfers between devices with their start and end apart: 12, of which 3 were waited for; matrix products, arithmetic and copies ran while one was open for 3% of the time, Pallas kernels for 8%

profile of v3, /device:TPU:1, one launch (start us, length us, event | category | flops | bytes accessed | tf_op | source)
XLA Modules:
  0.0 75.8 jit_solution(8872673877657312248)
XLA Ops:
  0.6 0.0 copy-start
  0.7 0.1 pad_add_fusion.place_ref.refs_0_
  0.7 1.7 %pack.1 = (bf16[64,896]{1,0:T(8,128)(2,1)S(1)}, f32[1,64]{1,0:T(1,128)S(1)}, bf16[272,768]{1,0:T(8,128)(2,1)S(1)}) custom-call(s32[4]{0:T(128)S(1)} %pad_add_fusion.place_ref.refs_0_, bf16[1024,768]{1,0:T(8,128)(2,1)} %refs_0_.1, bf16[64,768]{1,0:T(8,128)(2,1)} %tgt_hbm.1, f32[1,64]{1,0:T(1,128)} %bitcast.16, f32[1,64]{1,0:T(1,128)} %bitcast.17, ...), custom_call_target="tpu_custom_call" | custom-call | tf_op jit(solution)/shard_map/pack/pallas_call | solution.py:134
  2.4 6.5 %collective-permute-start.1 = (bf16[64,896]{1,0:T(8,128)(2,1)S(1)}, bf16[64,896]{1,0:T(8,128)(2,1)S(1)}, u32[]{:S(2)}, u32[]{:S(2)}) collective-permute-start(bf16[64,896]{1,0:T(8,128)(2,1)S(1)} %get-tuple-element.30.refs_0_), channel_id=1, source_target_pairs={{0,4},{4,8},{8,12},{12,16},{16,20},{20,24},{24,28},{28,0},{1,29},{... | collective-permute-start | bytes 344072 | tf_op jit(solution)/shard_map/ppermute | solution.py:44
  8.9 0.0 collective-permute-start.2
  8.9 2.5 %collective-permute-start.8 = (bf16[272,768]{1,0:T(8,128)(2,1)S(1)}, bf16[272,768]{1,0:T(8,128)(2,1)S(1)}, u32[]{:S(2)}, u32[]{:S(2)}) collective-permute-start(bf16[272,768]{1,0:T(8,128)(2,1)S(1)} %get-tuple-element.39), channel_id=1, source_target_pairs={{0,34},{34,0},{2,32},{32,2},{1,35},{35,1},{3,33},{33,3},{4,38},{38... | collective-permute-start | bytes 1253384 | tf_op jit(solution)/shard_map/ppermute | solution.py:59
  11.4 2.1 %slice.3 = bf16[512,768]{1,0:T(8,128)(2,1)} slice(bf16[1024,768]{1,0:T(8,128)(2,1)} %refs_0_.1), slice={[256:768], [0:768]} | slice | bytes 1572864 | tf_op jit(solution)/shard_map/slice | solution.py:406
  13.5 0.2 collective-permute-start.9
  13.7 0.0 collective-permute-done.1
  13.7 0.0 collective-permute-done.2
  13.8 1.7 %collective-permute-start.4 = (bf16[128,896]{1,0:T(8,128)(2,1)S(1)}, bf16[128,896]{1,0:T(8,128)(2,1)S(1)}, u32[]{:S(2)}, u32[]{:S(2)}) collective-permute-start(bf16[128,896]{1,0:T(8,128)(2,1)S(1)} %pad_maximum_fusion.refs_0_.refs_2_), channel_id=1, source_target_pairs={{0,4},{4,8},{8,12},{12,16},{16,20},{20,24},{24,28},{28,0},{1,29},{... | collective-permute-start | bytes 688136 | tf_op jit(solution)/shard_map/ppermute | solution.py:44
  15.5 1.0 %collective-permute-start = (bf16[64,896]{1,0:T(8,128)(2,1)S(1)}, bf16[64,896]{1,0:T(8,128)(2,1)S(1)}, u32[]{:S(2)}, u32[]{:S(2)}) collective-permute-start(bf16[64,896]{1,0:T(8,128)(2,1)S(1)} %get-tuple-element.30.refs_0_), channel_id=1, source_target_pairs={{0,1},{1,0},{2,3},{3,2},{4,5},{5,4},{6,7},{7,6},{8,9},{9,8},{10,11... | collective-permute-start | bytes 344072 | tf_op jit(solution)/shard_map/ppermute | solution.py:55
  16.5 0.0 copy-done
  16.5 0.4 multiply_reduce_fusion
  16.9 0.1 collective-permute-start.3
  17.0 0.5 collective-permute-done.refs_1_
  17.5 1.5 %rows.5 = (f32[128,1024]{1,0:T(8,128)}, f32[1,1024]{1,0:T(1,128)S(1)}) custom-call(bf16[64,896]{1,0:T(8,128)(2,1)S(1)} %get-tuple-element.30.refs_0_, bf16[64,896]{1,0:T(8,128)(2,1)S(1)} %collective-permute-done.refs_1_, bf16[1024,768]{1,0:T(8,128)(2,1)S(1)} %copy-done), custom_call_target="tpu_custom_call" | custom-call | flops 1 | bytes 1 | tf_op jit(solution)/shard_map/rows/pallas_call | solution.py:218
  19.0 0.0 collective-permute-done.4.refs_0_.refs_4_
  19.0 2.9 %collective-permute-start.6 = (bf16[128,896]{1,0:T(8,128)(2,1)S(1)}, bf16[128,896]{1,0:T(8,128)(2,1)S(1)}, u32[]{:S(2)}, u32[]{:S(2)}) collective-permute-start(bf16[128,896]{1,0:T(8,128)(2,1)S(1)} %collective-permute-done.4.refs_0_.refs_4_), channel_id=1, source_target_pairs={{0,4},{4,8},{8,12},{12,16},{16,20},{20,24},{24,28},{28,0},{1,29},{... | collective-permute-start | bytes 688136 | tf_op jit(solution)/shard_map/ppermute | solution.py:44
  21.9 0.0 collective-permute-done.8.refs_8_.refs_1_
  21.9 1.3 %collective-permute-start.10 = (bf16[272,768]{1,0:T(8,128)(2,1)S(1)}, bf16[272,768]{1,0:T(8,128)(2,1)S(1)}, u32[]{:S(2)}, u32[]{:S(2)}) collective-permute-start(bf16[272,768]{1,0:T(8,128)(2,1)S(1)} %collective-permute-done.8.refs_8_.refs_1_), channel_id=1, source_target_pairs={{0,64},{64,0},{128,192},{192,128},{1,65},{65,1},{129,193},{193,129... | collective-permute-start | bytes 1253384 | tf_op jit(solution)/shard_map/ppermute | solution.py:63
  23.2 2.2 %collective-permute-start.5 = (bf16[128,896]{1,0:T(8,128)(2,1)S(1)}, bf16[128,896]{1,0:T(8,128)(2,1)S(1)}, u32[]{:S(2)}, u32[]{:S(2)}) collective-permute-start(bf16[128,896]{1,0:T(8,128)(2,1)S(1)} %collective-permute-done.4.refs_0_.refs_4_), channel_id=1, source_target_pairs={{0,1},{1,0},{2,3},{3,2},{4,5},{5,4},{6,7},{7,6},{8,9},{9,8},{10,11... | collective-permute-start | bytes 688136 | tf_op jit(solution)/shard_map/ppermute | solution.py:55
  25.4 0.0 collective-permute-done.3.refs_1_.refs_3_
  25.4 1.6 %rows.6 = (f32[256,1024]{1,0:T(8,128)}, f32[1,1024]{1,0:T(1,128)S(1)}) custom-call(bf16[128,896]{1,0:T(8,128)(2,1)S(1)} %pad_maximum_fusion.refs_0_.refs_2_, bf16[128,896]{1,0:T(8,128)(2,1)S(1)} %collective-permute-done.3.refs_1_.refs_3_, bf16[1024,768]{1,0:T(8,128)(2,1)S(1)} %copy-done), custom_call_target="tpu_custom_call" | custom-call | flops 1 | bytes 1 | tf_op jit(solution)/shard_map/rows/pallas_call | solution.py:218
  27.1 0.0 collective-permute-done.6.refs_0_.refs_6_
  27.1 2.9 %collective-permute-start.7 = (bf16[128,896]{1,0:T(8,128)(2,1)S(1)}, bf16[128,896]{1,0:T(8,128)(2,1)S(1)}, u32[]{:S(2)}, u32[]{:S(2)}) collective-permute-start(bf16[128,896]{1,0:T(8,128)(2,1)S(1)} %collective-permute-done.6.refs_0_.refs_6_), channel_id=1, source_target_pairs={{0,1},{1,0},{2,3},{3,2},{4,5},{5,4},{6,7},{7,6},{8,9},{9,8},{10,11... | collective-permute-start | bytes 688136 | tf_op jit(solution)/shard_map/ppermute | solution.py:55
  30.0 0.0 collective-permute-start.11
  30.0 0.0 collective-permute-done.5.refs_1_.refs_5_
  30.0 1.7 %rows.7 = (f32[256,1024]{1,0:T(8,128)}, f32[1,1024]{1,0:T(1,128)S(1)}) custom-call(bf16[128,896]{1,0:T(8,128)(2,1)S(1)} %collective-permute-done.4.refs_0_.refs_4_, bf16[128,896]{1,0:T(8,128)(2,1)S(1)} %collective-permute-done.5.refs_1_.refs_5_, bf16[1024,768]{1,0:T(8,128)(2,1)S(1)} %copy-done), custom_call_target="tpu_custom_call" | custom-call | flops 1 | bytes 1 | tf_op jit(solution)/shard_map/rows/pallas_call | solution.py:218
  31.7 0.0 collective-permute-done.7.refs_1_.refs_7_
  31.7 1.6 %rows.8 = (f32[256,1024]{1,0:T(8,128)}, f32[1,1024]{1,0:T(1,128)S(1)}) custom-call(bf16[128,896]{1,0:T(8,128)(2,1)S(1)} %collective-permute-done.6.refs_0_.refs_6_, bf16[128,896]{1,0:T(8,128)(2,1)S(1)} %collective-permute-done.7.refs_1_.refs_7_, bf16[1024,768]{1,0:T(8,128)(2,1)S(1)} %copy-done), custom_call_target="tpu_custom_call" | custom-call | flops 1 | bytes 1 | tf_op jit(solution)/shard_map/rows/pallas_call | solution.py:218
  33.3 1.8 %collective-permute-done.11.group_ref = bf16[128,896]{1,0:T(8,128)(2,1)S(1)} collective-permute-done((bf16[128,896]{1,0:T(8,128)(2,1)S(1)}, bf16[128,896]{1,0:T(8,128)(2,1)S(1)}, u32[]{:S(2)}, u32[]{:S(2)}) %collective-permute-start.11) | collective-permute-done | bytes 229408 | tf_op jit(solution)/shard_map/ppermute | solution.py:44
  35.1 0.0 copy-start.1
  35.1 1.8 %collective-permute-done.9.refs_9_.refs_2_ = bf16[512,768]{1,0:T(8,128)(2,1)S(1)} collective-permute-done((bf16[512,768]{1,0:T(8,128)(2,1)}, bf16[512,768]{1,0:T(8,128)(2,1)S(1)}, u32[]{:S(2)}, u32[]{:S(2)}) %collective-permute-start.9) | collective-permute-done | bytes 786464 | tf_op jit(solution)/shard_map/ppermute | solution.py:59
  37.0 0.0 collective-permute-done.10.refs_10_.refs_3_
  37.0 3.1 %rows.9 = (f32[896,1024]{1,0:T(8,128)}, f32[1,1024]{1,0:T(1,128)S(1)}, f32[1,1024]{1,0:T(1,128)S(1)}) custom-call(bf16[64,896]{1,0:T(8,128)(2,1)S(1)} %get-tuple-element.30.refs_0_, bf16[64,896]{1,0:T(8,128)(2,1)S(1)} %collective-permute-done.refs_1_, bf16[128,896]{1,0:T(8,128)(2,1)S(1)} %pad_maximum_fusion.refs_0_.refs_2_, ...), custom_call_target="tpu_custom_call" | custom-call | flops 1 | bytes 1 | tf_op jit(solution)/shard_map/rows/pallas_call | solution.py:218
  40.1 1.9 %last_rows.1 = (f32[128,2048]{1,0:T(8,128)S(1)}, f32[16,1,2048]{2,1,0:T(1,128)S(1)}) custom-call(s32[4]{0:T(128)S(1)} %pad_add_fusion.place_ref.refs_0_, bf16[128,896]{1,0:T(8,128)(2,1)S(1)} %collective-permute-done.11.group_ref, bf16[1024,768]{1,0:T(8,128)(2,1)S(1)} %copy-done, bf16[272,768]{1,0:T(8,128)(2,1)S(1)} %collective-permute-done.8.refs_8_.refs_1_, ...), custom_call_target="tpu_custom_call" | custom-call | flops 402653184 | bytes 4194304 | tf_op jit(solution)/shard_map/last_rows/pallas_call | solution.py:264
  42.0 13.2 %all_to_all.10.refs_7_ = f32[16,1,2048]{2,1,0:T(1,128)S(1)} all-to-all(f32[16,1,2048]{2,1,0:T(1,128)S(1)} %get-tuple-element.52), channel_id=1, replica_groups=mesh['y'=4,'x_lo'=2,'z'=8,'x_hi'=2,'core'=2] {'y','x_lo','x_hi'}, dimensions={0} | all-to-all | bytes 262144 | tf_op jit(solution)/shard_map/all_to_all | solution.py:440
  55.1 0.0 copy-done.1
  55.1 4.8 %columns.1 = (f32[16,1,64]{2,1,0:T(1,128)S(1)}, f32[1,1024]{1,0:T(1,128)}) custom-call(s32[4]{0:T(128)S(1)} %pad_add_fusion.place_ref.refs_0_, f32[128,1024]{1,0:T(8,128)} %get-tuple-element.31.refs_1_, f32[256,1024]{1,0:T(8,128)} %get-tuple-element.32.refs_2_, f32[256,1024]{1,0:T(8,128)} %get-tuple-element.35.refs_3_, ...), custom_call_target="tpu_custom_call" | custom-call | flops 12582912 | bytes 8388608 | tf_op jit(solution)/shard_map/columns/pallas_call | solution.py:365
  60.0 15.2 %all_to_all.11 = f32[16,1,64]{2,1,0:T(1,128)S(1)} all-to-all(f32[16,1,64]{2,1,0:T(1,128)S(1)} %get-tuple-element.57), channel_id=1, replica_groups=mesh['y'=4,'x_lo'=2,'z'=8,'x_hi'=2,'core'=2] {'z','core'}, dimensions={0} | all-to-all | bytes 8192 | tf_op jit(solution)/shard_map/all_to_all | solution.py:444
  75.2 0.5 bitcast_subtract_fusion
  (4 shorter events, 0.1 us)
Async XLA Ops:
  0.6 15.9 %copy-start = (bf16[1024,768]{1,0:T(8,128)(2,1)S(1)}, bf16[1024,768]{1,0:T(8,128)(2,1)}, u32[]{:S(2)}) copy-start(bf16[1024,768]{1,0:T(8,128)(2,1)} %refs_0_.1) | copy-start | bytes 4718596
  2.4 11.3 %collective-permute-start.1 = (bf16[64,896]{1,0:T(8,128)(2,1)S(1)}, bf16[64,896]{1,0:T(8,128)(2,1)S(1)}, u32[]{:S(2)}, u32[]{:S(2)}) collective-permute-start(bf16[64,896]{1,0:T(8,128)(2,1)S(1)} %get-tuple-element.30.refs_0_), channel_id=1, source_target_pairs={{0,4},{4,8},{8,12},{12,16},{16,20},{20,24},{24,28},{28,0},{1,29},{... | collective-permute-start | bytes 344072 | tf_op jit(solution)/shard_map/ppermute | solution.py:44
  8.9 4.8 %collective-permute-start.2 = (bf16[64,896]{1,0:T(8,128)(2,1)S(1)}, bf16[64,896]{1,0:T(8,128)(2,1)S(1)}, u32[]{:S(2)}, u32[]{:S(2)}) collective-permute-start(bf16[64,896]{1,0:T(8,128)(2,1)S(1)} %get-tuple-element.30.refs_0_), channel_id=1, source_target_pairs={{1,4},{5,8},{9,12},{13,16},{17,20},{21,24},{25,28},{29,0},{0,29},{... | collective-permute-start | bytes 344072 | tf_op jit(solution)/shard_map/ppermute | solution.py:51
  8.9 13.0 %collective-permute-start.8 = (bf16[272,768]{1,0:T(8,128)(2,1)S(1)}, bf16[272,768]{1,0:T(8,128)(2,1)S(1)}, u32[]{:S(2)}, u32[]{:S(2)}) collective-permute-start(bf16[272,768]{1,0:T(8,128)(2,1)S(1)} %get-tuple-element.39), channel_id=1, source_target_pairs={{0,34},{34,0},{2,32},{32,2},{1,35},{35,1},{3,33},{33,3},{4,38},{38... | collective-permute-start | bytes 1253384 | tf_op jit(solution)/shard_map/ppermute | solution.py:59
  13.5 23.5 %collective-permute-start.9 = (bf16[512,768]{1,0:T(8,128)(2,1)}, bf16[512,768]{1,0:T(8,128)(2,1)S(1)}, u32[]{:S(2)}, u32[]{:S(2)}) collective-permute-start(bf16[512,768]{1,0:T(8,128)(2,1)} %slice.3), channel_id=1, source_target_pairs={{0,34},{34,0},{2,32},{32,2},{1,35},{35,1},{3,33},{33,3},{4,38},{38... | collective-permute-start | bytes 2359304 | tf_op jit(solution)/shard_map/ppermute | solution.py:59
  13.8 5.2 %collective-permute-start.4 = (bf16[128,896]{1,0:T(8,128)(2,1)S(1)}, bf16[128,896]{1,0:T(8,128)(2,1)S(1)}, u32[]{:S(2)}, u32[]{:S(2)}) collective-permute-start(bf16[128,896]{1,0:T(8,128)(2,1)S(1)} %pad_maximum_fusion.refs_0_.refs_2_), channel_id=1, source_target_pairs={{0,4},{4,8},{8,12},{12,16},{16,20},{20,24},{24,28},{28,0},{1,29},{... | collective-permute-start | bytes 688136 | tf_op jit(solution)/shard_map/ppermute | solution.py:44
  15.5 2.0 %collective-permute-start = (bf16[64,896]{1,0:T(8,128)(2,1)S(1)}, bf16[64,896]{1,0:T(8,128)(2,1)S(1)}, u32[]{:S(2)}, u32[]{:S(2)}) collective-permute-start(bf16[64,896]{1,0:T(8,128)(2,1)S(1)} %get-tuple-element.30.refs_0_), channel_id=1, source_target_pairs={{0,1},{1,0},{2,3},{3,2},{4,5},{5,4},{6,7},{7,6},{8,9},{9,8},{10,11... | collective-permute-start | bytes 344072 | tf_op jit(solution)/shard_map/ppermute | solution.py:55
  16.9 8.5 %collective-permute-start.3 = (bf16[128,896]{1,0:T(8,128)(2,1)S(1)}, bf16[128,896]{1,0:T(8,128)(2,1)S(1)}, u32[]{:S(2)}, u32[]{:S(2)}) collective-permute-start(bf16[128,896]{1,0:T(8,128)(2,1)S(1)} %pad_maximum_fusion.refs_0_.refs_2_), channel_id=1, source_target_pairs={{0,1},{1,0},{2,3},{3,2},{4,5},{5,4},{6,7},{7,6},{8,9},{9,8},{10,11... | collective-permute-start | bytes 688136 | tf_op jit(solution)/shard_map/ppermute | solution.py:55
  19.0 8.1 %collective-permute-start.6 = (bf16[128,896]{1,0:T(8,128)(2,1)S(1)}, bf16[128,896]{1,0:T(8,128)(2,1)S(1)}, u32[]{:S(2)}, u32[]{:S(2)}) collective-permute-start(bf16[128,896]{1,0:T(8,128)(2,1)S(1)} %collective-permute-done.4.refs_0_.refs_4_), channel_id=1, source_target_pairs={{0,4},{4,8},{8,12},{12,16},{16,20},{20,24},{24,28},{28,0},{1,29},{... | collective-permute-start | bytes 688136 | tf_op jit(solution)/shard_map/ppermute | solution.py:44
  21.9 15.1 %collective-permute-start.10 = (bf16[272,768]{1,0:T(8,128)(2,1)S(1)}, bf16[272,768]{1,0:T(8,128)(2,1)S(1)}, u32[]{:S(2)}, u32[]{:S(2)}) collective-permute-start(bf16[272,768]{1,0:T(8,128)(2,1)S(1)} %collective-permute-done.8.refs_8_.refs_1_), channel_id=1, source_target_pairs={{0,64},{64,0},{128,192},{192,128},{1,65},{65,1},{129,193},{193,129... | collective-permute-start | bytes 1253384 | tf_op jit(solution)/shard_map/ppermute | solution.py:63
  23.2 6.8 %collective-permute-start.5 = (bf16[128,896]{1,0:T(8,128)(2,1)S(1)}, bf16[128,896]{1,0:T(8,128)(2,1)S(1)}, u32[]{:S(2)}, u32[]{:S(2)}) collective-permute-start(bf16[128,896]{1,0:T(8,128)(2,1)S(1)} %collective-permute-done.4.refs_0_.refs_4_), channel_id=1, source_target_pairs={{0,1},{1,0},{2,3},{3,2},{4,5},{5,4},{6,7},{7,6},{8,9},{9,8},{10,11... | collective-permute-start | bytes 688136 | tf_op jit(solution)/shard_map/ppermute | solution.py:55
  27.1 4.6 %collective-permute-start.7 = (bf16[128,896]{1,0:T(8,128)(2,1)S(1)}, bf16[128,896]{1,0:T(8,128)(2,1)S(1)}, u32[]{:S(2)}, u32[]{:S(2)}) collective-permute-start(bf16[128,896]{1,0:T(8,128)(2,1)S(1)} %collective-permute-done.6.refs_0_.refs_6_), channel_id=1, source_target_pairs={{0,1},{1,0},{2,3},{3,2},{4,5},{5,4},{6,7},{7,6},{8,9},{9,8},{10,11... | collective-permute-start | bytes 688136 | tf_op jit(solution)/shard_map/ppermute | solution.py:55
  30.0 5.2 %collective-permute-start.11 = (bf16[128,896]{1,0:T(8,128)(2,1)S(1)}, bf16[128,896]{1,0:T(8,128)(2,1)S(1)}, u32[]{:S(2)}, u32[]{:S(2)}) collective-permute-start(bf16[128,896]{1,0:T(8,128)(2,1)S(1)} %collective-permute-done.6.refs_0_.refs_6_), channel_id=1, source_target_pairs={{0,4},{4,8},{8,12},{12,16},{16,20},{20,24},{24,28},{28,0},{1,29},{... | collective-permute-start | bytes 688136 | tf_op jit(solution)/shard_map/ppermute | solution.py:44
  35.1 20.0 %copy-start.1 = (f32[1024]{0:T(1024)S(1)}, f32[1024]{0:T(1024)}, u32[]{:S(2)}) copy-start(f32[1024]{0:T(1024)} %param.8) | copy-start | bytes 12292

commit v4 on v3

--- a/solution.py
+++ b/solution.py
@@ -22,7 +22,8 @@
 BLOCK = 512
 LANES = 128
 PEERS = 16
-X_HI, Z, CORE, ODD = range(4)
+X_HI, Z, CORE, QUARTERS, SENT = 0, 1, 2, 3, 7
+PART = HALF // 2
 STEPS = 5
 VMEM = 12 * 1024 * 1024
 EDGE = HALF // 4
@@ -57,6 +58,10 @@
 
 def facing(value):
     return lax.ppermute(value, ("x_lo", "x_hi"), [(0, 3), (3, 0), (1, 2), (2, 1)])
+
+
+def beside_x(value):
+    return lax.ppermute(value, "x_lo", [(0, 1), (1, 0)])
 
 
 def beside_y(value):
@@ -90,7 +95,7 @@
     ]
     for copy in copies:
         copy.start()
-    start = pl.multiple_of(place_ref[ODD] * (HALF - EDGE), EDGE)
+    start = pl.multiple_of(place_ref[SENT] * EDGE, EDGE)
     edge = pltpu.make_async_copy(
         src_hbm.at[pl.ds(start, EDGE), :], edge_ref.at[:EDGE, :], sems.at[4]
     )
@@ -182,10 +187,21 @@
             place += rows
 
 
-def row_pass(groups, sources):
+def score_units(group_refs, src_refs, cross_ref, row_ref, done=None):
+    top = 0
+    for at in range((len(group_refs) + 1) // 2):
+        pair = group_refs[2 * at : 2 * at + 2]
+        here = slice(top, top + sum(ref.shape[0] for ref in pair))
+        score_rows(pair, src_refs, cross_ref.at[here, :], row_ref.at[at : at + 1, :])
+        if done is not None:
+            done(at, here)
+        top = here.stop
+
+
+def row_pass(groups, sources, with_logw=False):
     count, parts = len(groups), len(sources)
-    small = 2 if parts > 1 else 1
     rows = sum(group.shape[0] for group in groups)
+    width = sum(part.shape[0] // EDGE * EDGE for part in sources)
     passes = (count + 1) // 2
 
     def body(*refs):
@@ -201,29 +217,30 @@
             for quarter in range(HALF // EDGE):
                 here = slice(quarter * EDGE, (quarter + 1) * EDGE)
                 logw_ref[:, here] = sums[quarter : quarter + 1, :]
-        copies, top = [], 0
-        for at in range(passes):
-            pair = group_refs[2 * at : 2 * at + 2]
-            here = slice(top, top + sum(ref.shape[0] for ref in pair))
-            score_rows(pair, src_refs, cross_ref.at[here, :], row_ref.at[at : at + 1, :])
+        copies = []
+
+        def keep(at, here):
             copies.append(
                 pltpu.make_async_copy(cross_ref.at[here, :], kept_ref.at[here, :], sems.at[at])
             )
             copies[-1].start()
-            top = here.stop
+
+        score_units(group_refs, src_refs, cross_ref, row_ref, keep)
         lse_ref[...] = log_sum2(row_ref[...])
         for copy in copies:
             copy.wait()
 
+    small = [jax.ShapeDtypeStruct((1, width), jnp.float32)]
+    if with_logw:
+        small.append(jax.ShapeDtypeStruct((1, HALF), jnp.float32))
     return pl.pallas_call(
         body,
         in_specs=[IN_VMEM] * (count + parts),
-        out_specs=[IN_HBM] + [IN_VMEM] * small,
-        out_shape=[pltpu.HBM((rows, HALF), jnp.float32)]
-        + [jax.ShapeDtypeStruct((1, HALF), jnp.float32)] * small,
+        out_specs=[IN_HBM] + [IN_VMEM] * len(small),
+        out_shape=[pltpu.HBM((rows, width), jnp.float32), *small],
         scratch_shapes=[
-            pltpu.VMEM((rows, HALF), jnp.float32),
-            pltpu.VMEM((passes, HALF), jnp.float32),
+            pltpu.VMEM((rows, width), jnp.float32),
+            pltpu.VMEM((passes, width), jnp.float32),
             pltpu.SemaphoreType.DMA((passes,)),
         ],
         compiler_params=pltpu.CompilerParams(vmem_limit_bytes=VMEM),
@@ -232,59 +249,70 @@
     )(*groups, *sources)
 
 
-def edge_places(place_ref):
-    straight = pl.multiple_of(place_ref[ODD] * (HALF - EDGE), EDGE)
-    return straight, pl.multiple_of((1 - place_ref[ODD]) * (HALF - EDGE), EDGE)
-
-
-def last_kernel(place_ref, group_ref, *refs):
-    own_refs, faced_refs, (faced_earlier, *earlier), refs = (
-        refs[:1],
-        refs[1:4],
-        refs[4 : 4 + STEPS],
-        refs[4 + STEPS :],
-    )
-    cross_ref, lse_ref, own_row, faced_row = refs
-    score_rows([group_ref], own_refs, cross_ref.at[:, :HALF], own_row)
-    score_rows([group_ref], faced_refs, cross_ref.at[:, HALF:], faced_row)
+def quarter_places(place_ref):
+    return [pl.multiple_of(place_ref[QUARTERS + k] * EDGE, EDGE) for k in range(HALF // EDGE)]
+
+
+def last_kernel(count, place_ref, *refs):
+    group_refs, own_refs, first_refs, round_refs = (
+        refs[:count],
+        refs[count : count + 1],
+        refs[count + 1 : count + 3],
+        refs[count + 3 : count + 5],
+    )
+    first_earlier, *earlier = refs[count + 5 : count + 5 + STEPS]
+    near_ref, round_ref, lse_ref, own_row, first_row, round_row = refs[count + 5 + STEPS :]
+    score_rows(group_refs[-1:], own_refs, near_ref.at[:, :HALF], own_row)
+    score_rows(group_refs[-1:], first_refs, near_ref.at[:, HALF:], first_row)
+    score_units(group_refs, round_refs, round_ref, round_row)
     own = log_sum2(jnp.concatenate([own_row[...], *[ref[...] for ref in earlier]], axis=0))
-    faced = log_sum2(jnp.concatenate([faced_row[...], faced_earlier[...]], axis=0))
+    faced = [
+        log_sum2(jnp.concatenate([first_row[...], first_earlier[...]], axis=0)),
+        log_sum2(round_row[...]),
+    ]
     mine = pl.multiple_of(place_ref[X_HI] * HALF, HALF)
     other = pl.multiple_of((1 - place_ref[X_HI]) * HALF, HALF)
-    straight, around = edge_places(place_ref)
+    places = quarter_places(place_ref)
     for peer in range(PEERS):
         lse_ref[peer, :, pl.ds(mine, HALF)] = own
-        lse_ref[peer, :, pl.ds(other + straight, EDGE)] = faced[:, :EDGE]
-        lse_ref[peer, :, pl.ds(other + EDGE, HALF - 2 * EDGE)] = faced[:, EDGE : HALF - EDGE]
-        lse_ref[peer, :, pl.ds(other + around, EDGE)] = faced[:, HALF - EDGE :]
-
-
-def last_pass(place, group, sources, faced, faced_earlier, earlier):
-    work = 2 * UNIT * HALF
+        for at, start in enumerate(places):
+            part = faced[at // 2][:, at % 2 * EDGE : (at % 2 + 1) * EDGE]
+            lse_ref[peer, :, pl.ds(other + start, EDGE)] = part
+
+
+def last_pass(place, groups, sources, faced, first_earlier, earlier):
+    count = len(groups)
+    work = UNIT * (HALF + PART) + ROWS * PART
+
+    def body(*refs):
+        last_kernel(count, *refs)
+
     return pl.pallas_call(
-        last_kernel,
-        in_specs=[IN_SMEM] + [IN_VMEM] * (6 + len(earlier)),
-        out_specs=[IN_VMEM] * 2,
+        body,
+        in_specs=[IN_SMEM] + [IN_VMEM] * (count + 6 + len(earlier)),
+        out_specs=[IN_VMEM] * 3,
         out_shape=[
-            pltpu.VMEM((UNIT, 2 * HALF), jnp.float32),
+            pltpu.VMEM((UNIT, HALF + PART), jnp.float32),
+            pltpu.VMEM((ROWS, PART), jnp.float32),
             pltpu.VMEM((PEERS, 1, 2 * HALF), jnp.float32),
         ],
         scratch_shapes=[
             pltpu.VMEM((1, HALF), jnp.float32),
-            pltpu.VMEM((1, HALF), jnp.float32),
+            pltpu.VMEM((1, PART), jnp.float32),
+            pltpu.VMEM(((count + 1) // 2, PART), jnp.float32),
         ],
         compiler_params=pltpu.CompilerParams(vmem_limit_bytes=VMEM),
         cost_estimate=pl.CostEstimate(
             flops=2 * work * D, bytes_accessed=HALF * D * 4 + work * 4, transcendentals=work
         ),
         name="last_rows",
-    )(place, group, sources, *faced, faced_earlier, *earlier)
+    )(place, *groups, sources, *faced, first_earlier, *earlier)
 
 
 def column_kernel(heights, place_ref, *refs):
     own_kept, refs = refs[: len(heights)], refs[len(heights) :]
-    faced_kept, near_ref, partial_ref, sq_ref, logw_ref, faced_logw_ref = refs[:6]
-    out_ref, pot_ref, own_held, faced_held, sems = refs[6:]
+    first_kept, near_ref, round_ref, partial_ref, sq_ref, logw_ref, faced_logw_ref = refs[:7]
+    out_ref, pot_ref, own_held, first_held, peak_ref, total_ref, sems = refs[7:]
     copies, top = [], 0
     for height, own_ref in zip(heights, own_kept):
         for start in range(0, height, UNIT):
@@ -296,7 +324,7 @@
                         own_ref.at[start : start + UNIT, :], own_held.at[here, :], sems.at[0, at]
                     ),
                     pltpu.make_async_copy(
-                        faced_kept.at[here, :], faced_held.at[here, :], sems.at[1, at]
+                        first_kept.at[here, :], first_held.at[here, :], sems.at[1, at]
                     ),
                 )
             )
@@ -307,42 +335,54 @@
     z, core = place_ref[Z], place_ref[CORE]
     mine = pl.multiple_of(place_ref[X_HI] * HALF, HALF)
     other = pl.multiple_of((1 - place_ref[X_HI]) * HALF, HALF)
-    straight, around = edge_places(place_ref)
-
     row = log_sum2(partial_ref[:, 0, pl.ds(mine, HALF)])
     own_bias = logw_ref[...] * LOG2E - row
     pot_ref[...] = sq_ref[...] - BACK * row
     own_bias = jnp.broadcast_to(own_bias, (8, HALF))
     faced_bias = [
-        faced_logw_ref[:, pl.ds(start, width)] * LOG2E
-        - log_sum2(partial_ref[:, 0, pl.ds(other + start, width)])
-        for start, width in ((straight, EDGE), (EDGE, HALF - 2 * EDGE), (around, EDGE))
+        faced_logw_ref[:, pl.ds(start, EDGE)] * LOG2E
+        - log_sum2(partial_ref[:, 0, pl.ds(other + start, EDGE)])
+        for start in quarter_places(place_ref)
     ]
-    faced_bias = jnp.broadcast_to(jnp.concatenate(faced_bias, axis=1), (8, HALF))
-    side = 2 * core - 1
-    for unit in (UNITS - 1, *range(UNITS - 1)):
-        if unit < len(copies):
+    first_bias = jnp.broadcast_to(jnp.concatenate(faced_bias[:2], axis=1), (8, PART))
+    round_bias = jnp.broadcast_to(jnp.concatenate(faced_bias[2:], axis=1), (8, PART))
+
+    def lanes(values):
+        return [values[:, k : k + LANES] for k in range(0, values.shape[1], LANES)]
+
+    def sums(pieces, before=None):
+        peak = pieces[0] if before is None else jnp.maximum(before[0], pieces[0])
+        for piece in pieces[1:]:
+            peak = jnp.maximum(peak, piece)
+        total = jnp.exp2(pieces[0] - peak)
+        for piece in pieces[1:]:
+            total = total + jnp.exp2(piece - peak)
+        if before is not None:
+            total = total + before[1] * jnp.exp2(before[0] - peak)
+        return peak, total
+
+    last = REST
+    for at in range(0, ROWS, 8):
+        rows = slice(at, at + 8)
+        pieces = lanes(round_ref[rows, :] + round_bias)
+        if at >= last:
+            near = near_ref[at - last : at - last + 8, :]
+            pieces += lanes(near[:, :HALF] + own_bias) + lanes(near[:, HALF:] + first_bias)
+        peak_ref[rows, :], total_ref[rows, :] = sums(pieces)
+    for units in (range(2), range(2, 4), range(4, UNITS - 1)):
+        for unit in units:
             for copy in copies[unit]:
                 copy.wait()
-            own_ref, faced_ref, top = own_held, faced_held, unit * UNIT
-        else:
-            own_ref, faced_ref, top = near_ref.at[:, :HALF], near_ref.at[:, HALF:], 0
-        peaks, totals = [], []
-        for at in range(top, top + UNIT, 8):
-            pieces = []
-            for ref, added in ((own_ref, own_bias), (faced_ref, faced_bias)):
-                scores = ref[at : at + 8, :] + added
-                pieces += [scores[:, k : k + LANES] for k in range(0, HALF, LANES)]
-            peak = pieces[0]
-            for piece in pieces[1:]:
-                peak = jnp.maximum(peak, piece)
-            total = jnp.exp2(pieces[0] - peak)
-            for piece in pieces[1:]:
-                total = total + jnp.exp2(piece - peak)
-            peaks.append(peak)
-            totals.append(total)
-        peak = jnp.concatenate(peaks, axis=0).T
-        total = jnp.concatenate(totals, axis=0).T
+        for at in range(units.start * UNIT, units.stop * UNIT, 8):
+            rows = slice(at, at + 8)
+            pieces = lanes(own_held[rows, :] + own_bias)
+            pieces += lanes(first_held[rows, :] + first_bias)
+            before = peak_ref[rows, :], total_ref[rows, :]
+            peak_ref[rows, :], total_ref[rows, :] = sums(pieces, before)
+    side = 2 * core - 1
+    for unit in range(UNITS):
+        rows = slice(unit * UNIT, (unit + 1) * UNIT)
+        peak, total = peak_ref[rows, :].T, total_ref[rows, :].T
         highest = jnp.max(peak, axis=0, keepdims=True)
         total = jnp.sum(total * jnp.exp2(peak - highest), axis=0, keepdims=True)
         lse = highest + jnp.log2(total)
@@ -356,7 +396,7 @@
         out_ref[pl.ds(second, 1)] = lse[:, OWN:].reshape(1, 1, OWN)
 
 
-def column_pass(place, own_crosses, faced_cross, near, partial, *rows):
+def column_pass(place, own_crosses, first_cross, near, round_cross, partial, *rows):
     heights = [cross.shape[0] for cross in own_crosses]
 
     def body(*refs):
@@ -364,7 +404,7 @@
 
     return pl.pallas_call(
         body,
-        in_specs=[IN_SMEM] + [IN_HBM] * (len(own_crosses) + 1) + [IN_VMEM] * 5,
+        in_specs=[IN_SMEM] + [IN_HBM] * (len(own_crosses) + 1) + [IN_VMEM] * 6,
         out_specs=[IN_VMEM] * 2,
         out_shape=[
             jax.ShapeDtypeStruct((PEERS, 1, OWN), jnp.float32),
@@ -372,7 +412,9 @@
         ],
         scratch_shapes=[
             pltpu.VMEM((REST, HALF), jnp.float32),
-            pltpu.VMEM((REST, HALF), jnp.float32),
+            pltpu.VMEM((REST, PART), jnp.float32),
+            pltpu.VMEM((ROWS, LANES), jnp.float32),
+            pltpu.VMEM((ROWS, LANES), jnp.float32),
             pltpu.SemaphoreType.DMA((2, UNITS - 1)),
         ],
         compiler_params=pltpu.CompilerParams(vmem_limit_bytes=VMEM),
@@ -382,28 +424,32 @@
         name="columns",
     )(
         place,
-        *in_hbm(*own_crosses, faced_cross),
+        *in_hbm(*own_crosses, first_cross),
         pltpu.with_memory_space_constraint(near, pltpu.VMEM),
+        pltpu.with_memory_space_constraint(round_cross, pltpu.VMEM),
         partial,
         *[row.reshape(1, HALF) for row in rows],
     )
 
 
 def on_device(sources, targets, potential_in, source_logw, target_logw):
+    x_lo, x_hi, odd = lax.axis_index("x_lo"), lax.axis_index("x_hi"), lax.axis_index("y") % 2
+    quarters = [
+        2 * odd + x_lo,
+        2 * (1 - odd) + 1 - x_lo,
+        2 * (1 - odd) + x_lo,
+        2 * odd + 1 - x_lo,
+    ]
+    sent, sent_next = 2 * odd + 1 - x_lo, 2 * (1 - odd) + x_lo
     place = jnp.stack(
-        [
-            lax.axis_index("x_hi"),
-            lax.axis_index("z"),
-            lax.axis_index("core"),
-            lax.axis_index("y") % 2,
-        ]
+        [x_hi, lax.axis_index("z"), lax.axis_index("core"), *quarters, sent]
     ).astype(jnp.int32)
     own, tgt_sq, edge = pack(
         place, sources, targets, potential_in, target_logw, source_logw
     )
     straight = facing(edge)
     same, cross_core = onward(own), onward_across(own)
-    middle = facing(sources[EDGE : HALF - EDGE])
+    opposite = facing(lax.dynamic_slice(sources, (sent_next * EDGE, 0), (EDGE, D)))
     beside = other_core(own)
 
     first = lax.axis_index("core") == 0
@@ -417,12 +463,14 @@
         following = onward(unit)
         beside = other_core(unit)
         if step == 1:
-            around = beside_y(straight)
+            by_y, by_x = beside_y(straight), beside_x(straight)
         cross, lse = row_pass(pending, [sources])
         groups += pending
         crosses.append(cross)
         if step == 1:
             following, lse, src_sq = lax.optimization_barrier((following, lse, src_sq))
+        elif step == 2:
+            following, lse, opposite = lax.optimization_barrier((following, lse, opposite))
         else:
             following, lse = lax.optimization_barrier((following, lse))
         lses.append(lse)
@@ -431,15 +479,17 @@
     cross, lse = row_pass(pending, [sources])
     groups += pending
     crosses.append(cross)
-    faced = [straight, middle, around]
-    faced_cross, faced_lse, faced_logw = row_pass(groups, faced)
-    unit, lse, faced_lse = lax.optimization_barrier((unit, lse, faced_lse))
+    first_cross, first_lse, faced_logw = row_pass(groups, [straight, opposite], True)
+    unit, lse, first_lse = lax.optimization_barrier((unit, lse, first_lse))
     lses.append(lse)
-    near, shared = last_pass(place, unit, sources, faced, faced_lse, lses)
+    groups.append(unit)
+    near, round_cross, shared = last_pass(
+        place, groups, sources, [straight, opposite, by_y, by_x], first_lse, lses
+    )
 
     partial = lax.all_to_all(shared, ("y", "x_lo", "x_hi"), 0, 0, tiled=True)
     columns, source_potential = column_pass(
-        place, crosses, faced_cross, near, partial, src_sq, source_logw, faced_logw
+        place, crosses, first_cross, near, round_cross, partial, src_sq, source_logw, faced_logw
     )
     gathered = lax.all_to_all(columns, ("z", "core"), 0, 0, tiled=True)
     final = log_sum2(gathered.reshape(PEERS, OWN)).reshape(OWN)

time: 76 us -> 73.1 us (0.962)
  starting transfers between devices: 21.3 us -> 25.3 us
  blocking collectives: 28.3 us -> 26.1 us
  local copies, waits for them, and re-layouts: 2.1 us -> 0.12 us
  waiting for transfers between devices: 4.21 us -> 2.61 us
  Pallas kernels: 17.9 us -> 16.9 us
    ppermute x4, starting transfers between devices: 6.26 us -> 3.07 us  [other_core(): return lax.ppermute(value, 'core', [(0, 1), (1, 0)])]
    ppermute x1, starting transfers between devices: 0.01 us -> 3.11 us  [onward_across(): return lax.ppermute(value, ('z', 'core'), up + down)]
    all_to_all x1, blocking collectives: 15.2 us -> 12.5 us  [on_device(): gathered = lax.all_to_all(columns, ('z', 'core'), 0, 0, tiled=True)]
    ppermute x2, starting transfers between devices: 2.68 us -> 5.04 us  [facing(): lax.ppermute(value, ('x_lo', 'x_hi'), [(0, 3), (3, 0), (1, 2), (2, 1)])]
    slice x1 -> x0, local copies, waits for them, and re-layouts: 2.09 us -> none  [on_device(): middle = facing(sources[EDGE:HALF - EDGE])]
    ppermute x4, waiting for transfers between devices: 1.87 us -> 0.01 us  [onward(): return lax.ppermute(value, ('z', 'core'), up + down)]
    ppermute x4, starting transfers between devices: 11.1 us -> 12.8 us  [onward(): return lax.ppermute(value, ('z', 'core'), up + down)]
    pallas_call x5, Pallas kernels: 9.49 us -> 8.34 us  [row_pass(): pl.pallas_call(body, in_specs=[IN_VMEM] * (count + parts), out_specs=[IN_...]
  transfers between devices with their start and end apart: 12 -> 13, of which waited for: 3 -> 1; matrix products, arithmetic and copies ran while one was open for 3% -> 1% of each run, Pallas kernels for 8% -> 11%
where the time goes in v4:
time: 73.1 us; the launch traced here: 72.9 us
  blocking collectives  26.1 us (36%)
  starting transfers between devices  25.3 us (35%)
  Pallas kernels  16.9 us (23%)
  waiting for transfers between devices  2.61 us (4%)
  other arithmetic  1.02 us (1%)
  between operations  0.8 us (1%)
    all_to_all x1, blocking collectives, on_device(): partial = lax.all_to_all(shared, ('y', 'x_lo', 'x_hi'), 0, 0, tiled=True)  13.6 us
    ppermute x4, starting transfers between devices, onward(): return lax.ppermute(value, ('z', 'core'), up + down)  12.8 us
    all_to_all x1, blocking collectives, on_device(): gathered = lax.all_to_all(columns, ('z', 'core'), 0, 0, tiled=True)  12.5 us
    pallas_call x5, Pallas kernels, row_pass(): pl.pallas_call(body, in_specs=[IN_VMEM] * (count + parts), out_specs=[IN_...  8.34 us
    ppermute x2, starting transfers between devices, facing(): lax.ppermute(value, ('x_lo', 'x_hi'), [(0, 3), (3, 0), (1, 2), (2, 1)])  5.04 us
    pallas_call x1, Pallas kernels, column_pass(): pl.pallas_call(body, in_specs=[IN_SMEM] + [IN_HBM] * (len(own_crosses) +...  4.01 us
    ppermute x1, starting transfers between devices, onward_across(): return lax.ppermute(value, ('z', 'core'), up + down)  3.11 us
    ppermute x4, starting transfers between devices, other_core(): return lax.ppermute(value, 'core', [(0, 1), (1, 0)])  3.07 us
  transfers between devices with their start and end apart: 13, of which 1 were waited for; matrix products, arithmetic and copies ran while one was open for 1% of the time, Pallas kernels for 11%

profile of v4, /device:TPU:1, one launch (start us, length us, event | category | flops | bytes accessed | tf_op | source)
XLA Modules:
  0.0 72.9 jit_solution(14879559502153635720)
XLA Ops:
  0.6 0.0 copy-start
  0.7 0.1 stack.32.place_ref.refs_0_
  0.7 1.7 %pack.1 = (bf16[64,896]{1,0:T(8,128)(2,1)S(1)}, f32[1,64]{1,0:T(1,128)S(1)}, bf16[272,768]{1,0:T(8,128)(2,1)S(1)}) custom-call(s32[8]{0:T(128)S(1)} %stack.32.place_ref.refs_0_, bf16[1024,768]{1,0:T(8,128)(2,1)} %refs_10_.1, bf16[64,768]{1,0:T(8,128)(2,1)} %tgt_hbm.1, f32[1,64]{1,0:T(1,128)} %bitcast.19, f32[1,64]{1,0:T(1,128)} %bitcast.20, f32[1,1024]{1,0:T(1,128)} %bitcast.15), custom_call_target="tpu_custom_call" | custom-call | tf_op jit(solution)/shard_map/pack/pallas_call | solution.py:139
  2.4 3.1 %collective-permute-start.2 = (bf16[64,896]{1,0:T(8,128)(2,1)S(1)}, bf16[64,896]{1,0:T(8,128)(2,1)S(1)}, u32[]{:S(2)}, u32[]{:S(2)}) collective-permute-start(bf16[64,896]{1,0:T(8,128)(2,1)S(1)} %get-tuple-element.32.refs_0_.refs_1_), channel_id=1, source_target_pairs={{1,4},{5,8},{9,12},{13,16},{17,20},{21,24},{25,28},{29,0},{0,29},{... | collective-permute-start | bytes 344072 | tf_op jit(solution)/shard_map/ppermute | solution.py:52
  5.6 3.5 %collective-permute-start.1 = (bf16[64,896]{1,0:T(8,128)(2,1)S(1)}, bf16[64,896]{1,0:T(8,128)(2,1)S(1)}, u32[]{:S(2)}, u32[]{:S(2)}) collective-permute-start(bf16[64,896]{1,0:T(8,128)(2,1)S(1)} %get-tuple-element.32.refs_0_.refs_1_), channel_id=1, source_target_pairs={{0,4},{4,8},{8,12},{12,16},{16,20},{20,24},{24,28},{28,0},{1,29},{... | collective-permute-start | bytes 344072 | tf_op jit(solution)/shard_map/ppermute | solution.py:45
  9.0 0.3 collective-permute-start
  9.3 2.5 %collective-permute-start.9 = (bf16[272,768]{1,0:T(8,128)(2,1)S(1)}, bf16[272,768]{1,0:T(8,128)(2,1)S(1)}, u32[]{:S(2)}, u32[]{:S(2)}) collective-permute-start(bf16[272,768]{1,0:T(8,128)(2,1)S(1)} %get-tuple-element.41), channel_id=1, source_target_pairs={{0,34},{34,0},{2,32},{32,2},{1,35},{35,1},{3,33},{33,3},{4,38},{38... | collective-permute-start | bytes 1253384 | tf_op jit(solution)/shard_map/ppermute | solution.py:60
  11.8 0.0 collective-permute-done.2
  11.8 0.0 collective-permute-done.1
  11.9 3.4 %collective-permute-start.4 = (bf16[128,896]{1,0:T(8,128)(2,1)S(1)}, bf16[128,896]{1,0:T(8,128)(2,1)S(1)}, u32[]{:S(2)}, u32[]{:S(2)}) collective-permute-start(bf16[128,896]{1,0:T(8,128)(2,1)S(1)} %pad_maximum_fusion.refs_0_.refs_2_.refs_3_), channel_id=1, source_target_pairs={{0,4},{4,8},{8,12},{12,16},{16,20},{20,24},{24,28},{28,0},{1,29},{... | collective-permute-start | bytes 688136 | tf_op jit(solution)/shard_map/ppermute | solution.py:45
  15.2 0.0 copy-done
  15.3 2.6 %collective-permute-start.7 = (bf16[256,768]{1,0:T(8,128)(2,1)S(1)}, bf16[256,768]{1,0:T(8,128)(2,1)S(1)}, u32[]{:S(2)}, u32[]{:S(2)}) collective-permute-start(bf16[256,768]{1,0:T(8,128)(2,1)S(1)} %constant_dynamic-slice_fusion), channel_id=1, source_target_pairs={{0,34},{34,0},{2,32},{32,2},{1,35},{35,1},{3,33},{33,3},{4,38},{38... | collective-permute-start | bytes 1179656 | tf_op jit(solution)/shard_map/ppermute | solution.py:60
  17.8 0.4 multiply_reduce_fusion
  18.2 0.6 collective-permute-start.3
  18.8 0.0 collective-permute-done.refs_1_.refs_2_
  18.9 1.5 %rows.5 = (f32[128,1024]{1,0:T(8,128)}, f32[1,1024]{1,0:T(1,128)S(1)}) custom-call(bf16[64,896]{1,0:T(8,128)(2,1)S(1)} %get-tuple-element.32.refs_0_.refs_1_, bf16[64,896]{1,0:T(8,128)(2,1)S(1)} %collective-permute-done.refs_1_.refs_2_, bf16[1024,768]{1,0:T(8,128)(2,1)S(1)} %copy-done), custom_call_target="tpu_custom_call" | custom-call | flops 1 | bytes 1 | tf_op jit(solution)/shard_map/rows/pallas_call | solution.py:236
  20.3 0.0 collective-permute-done.4.refs_0_.refs_4_.refs_5_
  20.3 3.0 %collective-permute-start.6 = (bf16[128,896]{1,0:T(8,128)(2,1)S(1)}, bf16[128,896]{1,0:T(8,128)(2,1)S(1)}, u32[]{:S(2)}, u32[]{:S(2)}) collective-permute-start(bf16[128,896]{1,0:T(8,128)(2,1)S(1)} %collective-permute-done.4.refs_0_.refs_4_.refs_5_), channel_id=1, source_target_pairs={{0,4},{4,8},{8,12},{12,16},{16,20},{20,24},{24,28},{28,0},{1,29},{... | collective-permute-start | bytes 688136 | tf_op jit(solution)/shard_map/ppermute | solution.py:45
  23.3 0.0 collective-permute-done.9.refs_8_.refs_11_
  23.3 0.0 collective-permute-start.12
  23.3 1.3 %collective-permute-start.11 = (bf16[272,768]{1,0:T(8,128)(2,1)S(1)}, bf16[272,768]{1,0:T(8,128)(2,1)S(1)}, u32[]{:S(2)}, u32[]{:S(2)}) collective-permute-start(bf16[272,768]{1,0:T(8,128)(2,1)S(1)} %collective-permute-done.9.refs_8_.refs_11_), channel_id=1, source_target_pairs={{0,64},{64,0},{128,192},{192,128},{1,65},{65,1},{129,193},{193,129... | collective-permute-start | bytes 1253384 | tf_op jit(solution)/shard_map/ppermute | solution.py:68
  24.6 0.0 collective-permute-done.3.refs_1_.refs_3_.refs_4_
  24.7 1.1 %collective-permute-start.5 = (bf16[128,896]{1,0:T(8,128)(2,1)S(1)}, bf16[128,896]{1,0:T(8,128)(2,1)S(1)}, u32[]{:S(2)}, u32[]{:S(2)}) collective-permute-start(bf16[128,896]{1,0:T(8,128)(2,1)S(1)} %collective-permute-done.4.refs_0_.refs_4_.refs_5_), channel_id=1, source_target_pairs={{0,1},{1,0},{2,3},{3,2},{4,5},{5,4},{6,7},{7,6},{8,9},{9,8},{10,11... | collective-permute-start | bytes 688136 | tf_op jit(solution)/shard_map/ppermute | solution.py:56
  25.8 1.6 %rows.6 = (f32[256,1024]{1,0:T(8,128)}, f32[1,1024]{1,0:T(1,128)S(1)}) custom-call(bf16[128,896]{1,0:T(8,128)(2,1)S(1)} %pad_maximum_fusion.refs_0_.refs_2_.refs_3_, bf16[128,896]{1,0:T(8,128)(2,1)S(1)} %collective-permute-done.3.refs_1_.refs_3_.refs_4_, bf16[1024,768]{1,0:T(8,128)(2,1)S(1)} %copy-done), custom_call_target="tpu_custom_call" | custom-call | flops 1 | bytes 1 | tf_op jit(solution)/shard_map/rows/pallas_call | solution.py:236
  27.4 2.6 %collective-permute-done.7.refs_9_.refs_12_ = bf16[256,768]{1,0:T(8,128)(2,1)S(1)} collective-permute-done((bf16[256,768]{1,0:T(8,128)(2,1)S(1)}, bf16[256,768]{1,0:T(8,128)(2,1)S(1)}, u32[]{:S(2)}, u32[]{:S(2)}) %collective-permute-start.7) | collective-permute-done | bytes 393248 | tf_op jit(solution)/shard_map/ppermute | solution.py:60
  30.0 0.0 collective-permute-done.6.refs_0_.refs_6_.refs_7_
  30.0 1.0 %collective-permute-start.8 = (bf16[128,896]{1,0:T(8,128)(2,1)S(1)}, bf16[128,896]{1,0:T(8,128)(2,1)S(1)}, u32[]{:S(2)}, u32[]{:S(2)}) collective-permute-start(bf16[128,896]{1,0:T(8,128)(2,1)S(1)} %collective-permute-done.6.refs_0_.refs_6_.refs_7_), channel_id=1, source_target_pairs={{0,1},{1,0},{2,3},{3,2},{4,5},{5,4},{6,7},{7,6},{8,9},{9,8},{10,11... | collective-permute-start | bytes 688136 | tf_op jit(solution)/shard_map/ppermute | solution.py:56
  31.0 3.0 %collective-permute-start.10 = (bf16[128,896]{1,0:T(8,128)(2,1)S(1)}, bf16[128,896]{1,0:T(8,128)(2,1)S(1)}, u32[]{:S(2)}, u32[]{:S(2)}) collective-permute-start(bf16[128,896]{1,0:T(8,128)(2,1)S(1)} %collective-permute-done.6.refs_0_.refs_6_.refs_7_), channel_id=1, source_target_pairs={{0,4},{4,8},{8,12},{12,16},{16,20},{20,24},{24,28},{28,0},{1,29},{... | collective-permute-start | bytes 688136 | tf_op jit(solution)/shard_map/ppermute | solution.py:45
  34.0 0.0 collective-permute-done.5.refs_1_.refs_5_.refs_6_
  34.0 1.6 %rows.7 = (f32[256,1024]{1,0:T(8,128)}, f32[1,1024]{1,0:T(1,128)S(1)}) custom-call(bf16[128,896]{1,0:T(8,128)(2,1)S(1)} %collective-permute-done.4.refs_0_.refs_4_.refs_5_, bf16[128,896]{1,0:T(8,128)(2,1)S(1)} %collective-permute-done.5.refs_1_.refs_5_.refs_6_, bf16[1024,768]{1,0:T(8,128)(2,1)S(1)} %copy-done), custom_call_target="tpu_custom_call" | custom-call | flops 1 | bytes 1 | tf_op jit(solution)/shard_map/rows/pallas_call | solution.py:236
  35.6 0.0 collective-permute-done.8.refs_1_.refs_7_.refs_8_
  35.6 1.6 %rows.8 = (f32[256,1024]{1,0:T(8,128)}, f32[1,1024]{1,0:T(1,128)S(1)}) custom-call(bf16[128,896]{1,0:T(8,128)(2,1)S(1)} %collective-permute-done.6.refs_0_.refs_6_.refs_7_, bf16[128,896]{1,0:T(8,128)(2,1)S(1)} %collective-permute-done.8.refs_1_.refs_7_.refs_8_, bf16[1024,768]{1,0:T(8,128)(2,1)S(1)} %copy-done), custom_call_target="tpu_custom_call" | custom-call | flops 1 | bytes 1 | tf_op jit(solution)/shard_map/rows/pallas_call | solution.py:236
  37.3 2.0 %rows.9 = (f32[896,512]{1,0:T(8,128)}, f32[1,512]{1,0:T(1,128)S(1)}, f32[1,1024]{1,0:T(1,128)S(1)}) custom-call(bf16[64,896]{1,0:T(8,128)(2,1)S(1)} %get-tuple-element.32.refs_0_.refs_1_, bf16[64,896]{1,0:T(8,128)(2,1)S(1)} %collective-permute-done.refs_1_.refs_2_, bf16[128,896]{1,0:T(8,128)(2,1)S(1)} %pad_maximum_fusion.refs_0_.refs_2_.refs_3_, ...), custom_call_target="tpu_custom_call" | custom-call | flops 1 | bytes 1 | tf_op jit(solution)/shard_map/rows/pallas_call | solution.py:236
  39.2 0.0 collective-permute-done.10.refs_9_
  39.3 0.0 copy-start.1
  39.3 0.0 collective-permute-done.12.refs_14_
  39.3 0.0 collective-permute-done.11.refs_13_
  39.3 2.9 %last_rows.1 = (f32[128,1536]{1,0:T(8,128)S(1)}, f32[1024,512]{1,0:T(8,128)S(1)}, f32[16,1,2048]{2,1,0:T(1,128)S(1)}) custom-call(s32[8]{0:T(128)S(1)} %stack.32.place_ref.refs_0_, bf16[64,896]{1,0:T(8,128)(2,1)S(1)} %get-tuple-element.32.refs_0_.refs_1_, bf16[64,896]{1,0:T(8,128)(2,1)S(1)} %collective-permute-done.refs_1_.refs_2_, ...), custom_call_target="tpu_custom_call" | custom-call | flops 1107296256 | bytes 6029312 | tf_op jit(solution)/shard_map/last_rows/pallas_call | solution.py:290
  42.1 13.6 %all_to_all.10.refs_8_ = f32[16,1,2048]{2,1,0:T(1,128)S(1)} all-to-all(f32[16,1,2048]{2,1,0:T(1,128)S(1)} %get-tuple-element.56), channel_id=1, replica_groups=mesh['y'=4,'x_lo'=2,'z'=8,'x_hi'=2,'core'=2] {'y','x_lo','x_hi'}, dimensions={0} | all-to-all | bytes 262144 | tf_op jit(solution)/shard_map/all_to_all | solution.py:490
  55.7 0.0 copy-done.1
  55.7 4.0 %columns.1 = (f32[16,1,64]{2,1,0:T(1,128)S(1)}, f32[1,1024]{1,0:T(1,128)}) custom-call(s32[8]{0:T(128)S(1)} %stack.32.place_ref.refs_0_, f32[128,1024]{1,0:T(8,128)} %get-tuple-element.33.refs_1_, f32[256,1024]{1,0:T(8,128)} %get-tuple-element.34.refs_2_, f32[256,1024]{1,0:T(8,128)} %get-tuple-element.37.refs_3_, f32[256,1024]{1,0:T(8,128)} %get-tuple-element.40.refs_4_, ...), custom_call_target="tpu_custom_call" | custom-call | flops 12582912 | bytes 8388608 | tf_op jit(solution)/shard_map/columns/pallas_call | solution.py:405
  59.8 12.5 %all_to_all.11 = f32[16,1,64]{2,1,0:T(1,128)S(1)} all-to-all(f32[16,1,64]{2,1,0:T(1,128)S(1)} %get-tuple-element.61), channel_id=1, replica_groups=mesh['y'=4,'x_lo'=2,'z'=8,'x_hi'=2,'core'=2] {'z','core'}, dimensions={0} | all-to-all | bytes 8192 | tf_op jit(solution)/shard_map/all_to_all | solution.py:494
  72.4 0.5 bitcast_subtract_fusion
  (5 shorter events, 0.1 us)
Async XLA Ops:
  0.6 14.6 %copy-start = (bf16[1024,768]{1,0:T(8,128)(2,1)S(1)}, bf16[1024,768]{1,0:T(8,128)(2,1)}, u32[]{:S(2)}) copy-start(bf16[1024,768]{1,0:T(8,128)(2,1)} %refs_10_.1) | copy-start | bytes 4718596
  2.4 9.4 %collective-permute-start.2 = (bf16[64,896]{1,0:T(8,128)(2,1)S(1)}, bf16[64,896]{1,0:T(8,128)(2,1)S(1)}, u32[]{:S(2)}, u32[]{:S(2)}) collective-permute-start(bf16[64,896]{1,0:T(8,128)(2,1)S(1)} %get-tuple-element.32.refs_0_.refs_1_), channel_id=1, source_target_pairs={{1,4},{5,8},{9,12},{13,16},{17,20},{21,24},{25,28},{29,0},{0,29},{... | collective-permute-start | bytes 344072 | tf_op jit(solution)/shard_map/ppermute | solution.py:52
  5.6 6.3 %collective-permute-start.1 = (bf16[64,896]{1,0:T(8,128)(2,1)S(1)}, bf16[64,896]{1,0:T(8,128)(2,1)S(1)}, u32[]{:S(2)}, u32[]{:S(2)}) collective-permute-start(bf16[64,896]{1,0:T(8,128)(2,1)S(1)} %get-tuple-element.32.refs_0_.refs_1_), channel_id=1, source_target_pairs={{0,4},{4,8},{8,12},{12,16},{16,20},{20,24},{24,28},{28,0},{1,29},{... | collective-permute-start | bytes 344072 | tf_op jit(solution)/shard_map/ppermute | solution.py:45
  9.0 9.8 %collective-permute-start = (bf16[64,896]{1,0:T(8,128)(2,1)S(1)}, bf16[64,896]{1,0:T(8,128)(2,1)S(1)}, u32[]{:S(2)}, u32[]{:S(2)}) collective-permute-start(bf16[64,896]{1,0:T(8,128)(2,1)S(1)} %get-tuple-element.32.refs_0_.refs_1_), channel_id=1, source_target_pairs={{0,1},{1,0},{2,3},{3,2},{4,5},{5,4},{6,7},{7,6},{8,9},{9,8},{10,11... | collective-permute-start | bytes 344072 | tf_op jit(solution)/shard_map/ppermute | solution.py:56
  9.3 14.0 %collective-permute-start.9 = (bf16[272,768]{1,0:T(8,128)(2,1)S(1)}, bf16[272,768]{1,0:T(8,128)(2,1)S(1)}, u32[]{:S(2)}, u32[]{:S(2)}) collective-permute-start(bf16[272,768]{1,0:T(8,128)(2,1)S(1)} %get-tuple-element.41), channel_id=1, source_target_pairs={{0,34},{34,0},{2,32},{32,2},{1,35},{35,1},{3,33},{33,3},{4,38},{38... | collective-permute-start | bytes 1253384 | tf_op jit(solution)/shard_map/ppermute | solution.py:60
  11.9 8.4 %collective-permute-start.4 = (bf16[128,896]{1,0:T(8,128)(2,1)S(1)}, bf16[128,896]{1,0:T(8,128)(2,1)S(1)}, u32[]{:S(2)}, u32[]{:S(2)}) collective-permute-start(bf16[128,896]{1,0:T(8,128)(2,1)S(1)} %pad_maximum_fusion.refs_0_.refs_2_.refs_3_), channel_id=1, source_target_pairs={{0,4},{4,8},{8,12},{12,16},{16,20},{20,24},{24,28},{28,0},{1,29},{... | collective-permute-start | bytes 688136 | tf_op jit(solution)/shard_map/ppermute | solution.py:45
  15.3 14.7 %collective-permute-start.7 = (bf16[256,768]{1,0:T(8,128)(2,1)S(1)}, bf16[256,768]{1,0:T(8,128)(2,1)S(1)}, u32[]{:S(2)}, u32[]{:S(2)}) collective-permute-start(bf16[256,768]{1,0:T(8,128)(2,1)S(1)} %constant_dynamic-slice_fusion), channel_id=1, source_target_pairs={{0,34},{34,0},{2,32},{32,2},{1,35},{35,1},{3,33},{33,3},{4,38},{38... | collective-permute-start | bytes 1179656 | tf_op jit(solution)/shard_map/ppermute | solution.py:60
  18.2 6.4 %collective-permute-start.3 = (bf16[128,896]{1,0:T(8,128)(2,1)S(1)}, bf16[128,896]{1,0:T(8,128)(2,1)S(1)}, u32[]{:S(2)}, u32[]{:S(2)}) collective-permute-start(bf16[128,896]{1,0:T(8,128)(2,1)S(1)} %pad_maximum_fusion.refs_0_.refs_2_.refs_3_), channel_id=1, source_target_pairs={{0,1},{1,0},{2,3},{3,2},{4,5},{5,4},{6,7},{7,6},{8,9},{9,8},{10,11... | collective-permute-start | bytes 688136 | tf_op jit(solution)/shard_map/ppermute | solution.py:56
  20.3 9.7 %collective-permute-start.6 = (bf16[128,896]{1,0:T(8,128)(2,1)S(1)}, bf16[128,896]{1,0:T(8,128)(2,1)S(1)}, u32[]{:S(2)}, u32[]{:S(2)}) collective-permute-start(bf16[128,896]{1,0:T(8,128)(2,1)S(1)} %collective-permute-done.4.refs_0_.refs_4_.refs_5_), channel_id=1, source_target_pairs={{0,4},{4,8},{8,12},{12,16},{16,20},{20,24},{24,28},{28,0},{1,29},{... | collective-permute-start | bytes 688136 | tf_op jit(solution)/shard_map/ppermute | solution.py:45
  23.3 15.9 %collective-permute-start.12 = (bf16[272,768]{1,0:T(8,128)(2,1)S(1)}, bf16[272,768]{1,0:T(8,128)(2,1)S(1)}, u32[]{:S(2)}, u32[]{:S(2)}) collective-permute-start(bf16[272,768]{1,0:T(8,128)(2,1)S(1)} %collective-permute-done.9.refs_8_.refs_11_), channel_id=1, source_target_pairs={{0,32},{32,0},{1,33},{33,1},{2,34},{34,2},{3,35},{35,3},{4,36},{36... | collective-permute-start | bytes 1253384 | tf_op jit(solution)/shard_map/ppermute | solution.py:64
  23.3 15.9 %collective-permute-start.11 = (bf16[272,768]{1,0:T(8,128)(2,1)S(1)}, bf16[272,768]{1,0:T(8,128)(2,1)S(1)}, u32[]{:S(2)}, u32[]{:S(2)}) collective-permute-start(bf16[272,768]{1,0:T(8,128)(2,1)S(1)} %collective-permute-done.9.refs_8_.refs_11_), channel_id=1, source_target_pairs={{0,64},{64,0},{128,192},{192,128},{1,65},{65,1},{129,193},{193,129... | collective-permute-start | bytes 1253384 | tf_op jit(solution)/shard_map/ppermute | solution.py:68
  24.7 9.3 %collective-permute-start.5 = (bf16[128,896]{1,0:T(8,128)(2,1)S(1)}, bf16[128,896]{1,0:T(8,128)(2,1)S(1)}, u32[]{:S(2)}, u32[]{:S(2)}) collective-permute-start(bf16[128,896]{1,0:T(8,128)(2,1)S(1)} %collective-permute-done.4.refs_0_.refs_4_.refs_5_), channel_id=1, source_target_pairs={{0,1},{1,0},{2,3},{3,2},{4,5},{5,4},{6,7},{7,6},{8,9},{9,8},{10,11... | collective-permute-start | bytes 688136 | tf_op jit(solution)/shard_map/ppermute | solution.py:56
  30.0 5.6 %collective-permute-start.8 = (bf16[128,896]{1,0:T(8,128)(2,1)S(1)}, bf16[128,896]{1,0:T(8,128)(2,1)S(1)}, u32[]{:S(2)}, u32[]{:S(2)}) collective-permute-start(bf16[128,896]{1,0:T(8,128)(2,1)S(1)} %collective-permute-done.6.refs_0_.refs_6_.refs_7_), channel_id=1, source_target_pairs={{0,1},{1,0},{2,3},{3,2},{4,5},{5,4},{6,7},{7,6},{8,9},{9,8},{10,11... | collective-permute-start | bytes 688136 | tf_op jit(solution)/shard_map/ppermute | solution.py:56
  31.0 8.2 %collective-permute-start.10 = (bf16[128,896]{1,0:T(8,128)(2,1)S(1)}, bf16[128,896]{1,0:T(8,128)(2,1)S(1)}, u32[]{:S(2)}, u32[]{:S(2)}) collective-permute-start(bf16[128,896]{1,0:T(8,128)(2,1)S(1)} %collective-permute-done.6.refs_0_.refs_6_.refs_7_), channel_id=1, source_target_pairs={{0,4},{4,8},{8,12},{12,16},{16,20},{20,24},{24,28},{28,0},{1,29},{... | collective-permute-start | bytes 688136 | tf_op jit(solution)/shard_map/ppermute | solution.py:45
  39.3 16.5 %copy-start.1 = (f32[1024]{0:T(1024)S(1)}, f32[1024]{0:T(1024)}, u32[]{:S(2)}) copy-start(f32[1024]{0:T(1024)} %param.8) | copy-start | bytes 12292

commit v5 on v4

--- a/solution.py
+++ b/solution.py
@@ -24,7 +24,7 @@
 PEERS = 16
 X_HI, Z, CORE, QUARTERS, SENT = 0, 1, 2, 3, 7
 PART = HALF // 2
-STEPS = 5
+PASSES = 4
 VMEM = 12 * 1024 * 1024
 EDGE = HALF // 4
 EXTRA = 16
@@ -171,7 +171,7 @@
     pieces = group[:, D:].astype(jnp.float32)
     bias = pieces[:, 0:1] + pieces[:, 1:2] + pieces[:, 2:3]
     group = group[:, :D]
-    place = 0
+    place, totals = 0, []
     for src_ref in src_refs:
         height = src_ref.shape[0] // EDGE * EDGE
         rows = min(BLOCK, height)
@@ -183,8 +183,9 @@
                 preferred_element_type=jnp.float32,
             )
             cross_ref[:, place : place + rows] = cross
-            lse_ref[:, place : place + rows] = log_sum2(cross + bias)
+            totals.append(log_sum2(cross + bias))
             place += rows
+    lse_ref[...] = jnp.concatenate(totals, axis=1)
 
 
 def score_units(group_refs, src_refs, cross_ref, row_ref, done=None):
@@ -198,55 +199,78 @@
         top = here.stop
 
 
-def row_pass(groups, sources, with_logw=False):
-    count, parts = len(groups), len(sources)
-    rows = sum(group.shape[0] for group in groups)
-    width = sum(part.shape[0] // EDGE * EDGE for part in sources)
-    passes = (count + 1) // 2
+def row_pass(groups, sources, faced=(), late=0):
+    count, parts = len(groups), len(faced)
+    tops = [sum(group.shape[0] for group in groups[:at]) for at in range(count + 1)]
+    own_from = count - late if parts else 0
+    own_rows, all_rows = tops[-1] - tops[own_from], tops[-1]
+    own_passes, passes = (count - own_from + 1) // 2, (count + 1) // 2
+    width = sum(part.shape[0] // EDGE * EDGE for part in faced)
 
     def body(*refs):
-        group_refs, src_refs, refs = (
-            refs[:count],
-            refs[count : count + parts],
-            refs[count + parts :],
-        )
-        kept_ref, lse_ref, *logw_refs, cross_ref, row_ref, sems = refs
-        for logw_ref in logw_refs:
-            extra = src_refs[0][EDGE:, :].astype(jnp.float32)
+        group_refs, src_ref = refs[:count], refs[count]
+        faced_refs, refs = refs[count + 1 : count + 1 + parts], refs[count + 1 + parts :]
+        if parts:
+            kept_ref, lse_ref, faced_kept, faced_lse, logw_ref, *refs = refs
+            cross_ref, row_ref, sems, faced_cross, faced_row, faced_sems = refs
+            extra = faced_refs[0][EDGE:, :].astype(jnp.float32)
             sums = extra[:, :EDGE] + extra[:, EDGE : 2 * EDGE] + extra[:, 2 * EDGE :]
             for quarter in range(HALF // EDGE):
                 here = slice(quarter * EDGE, (quarter + 1) * EDGE)
                 logw_ref[:, here] = sums[quarter : quarter + 1, :]
+        else:
+            kept_ref, lse_ref, cross_ref, row_ref, sems = refs
         copies = []
 
-        def keep(at, here):
-            copies.append(
-                pltpu.make_async_copy(cross_ref.at[here, :], kept_ref.at[here, :], sems.at[at])
-            )
-            copies[-1].start()
-
-        score_units(group_refs, src_refs, cross_ref, row_ref, keep)
+        def keeper(held_ref, kept_ref, sems):
+            def keep(at, here):
+                copy = pltpu.make_async_copy(held_ref.at[here, :], kept_ref.at[here, :], sems.at[at])
+                copy.start()
+                copies.append(copy)
+
+            return keep
+
+        score_units(
+            group_refs[own_from:], [src_ref], cross_ref, row_ref, keeper(cross_ref, kept_ref, sems)
+        )
+        if parts:
+            keep = keeper(faced_cross, faced_kept, faced_sems)
+            score_units(group_refs, faced_refs, faced_cross, faced_row, keep)
+            faced_lse[...] = log_sum2(faced_row[...])
         lse_ref[...] = log_sum2(row_ref[...])
         for copy in copies:
             copy.wait()
 
-    small = [jax.ShapeDtypeStruct((1, width), jnp.float32)]
-    if with_logw:
-        small.append(jax.ShapeDtypeStruct((1, HALF), jnp.float32))
+    out_shape = [
+        pltpu.HBM((own_rows, HALF), jnp.float32),
+        jax.ShapeDtypeStruct((1, HALF), jnp.float32),
+    ]
+    scratch = [
+        pltpu.VMEM((own_rows, HALF), jnp.float32),
+        pltpu.VMEM((own_passes, HALF), jnp.float32),
+        pltpu.SemaphoreType.DMA((own_passes,)),
+    ]
+    if parts:
+        out_shape += [
+            pltpu.HBM((all_rows, width), jnp.float32),
+            jax.ShapeDtypeStruct((1, width), jnp.float32),
+            jax.ShapeDtypeStruct((1, HALF), jnp.float32),
+        ]
+        scratch += [
+            pltpu.VMEM((all_rows, width), jnp.float32),
+            pltpu.VMEM((passes, width), jnp.float32),
+            pltpu.SemaphoreType.DMA((passes,)),
+        ]
     return pl.pallas_call(
         body,
-        in_specs=[IN_VMEM] * (count + parts),
-        out_specs=[IN_HBM] + [IN_VMEM] * len(small),
-        out_shape=[pltpu.HBM((rows, width), jnp.float32), *small],
-        scratch_shapes=[
-            pltpu.VMEM((rows, width), jnp.float32),
-            pltpu.VMEM((passes, width), jnp.float32),
-            pltpu.SemaphoreType.DMA((passes,)),
-        ],
+        in_specs=[IN_VMEM] * (count + 1 + parts),
+        out_specs=[IN_HBM, IN_VMEM] + [IN_HBM, IN_VMEM, IN_VMEM] * (parts > 0),
+        out_shape=out_shape,
+        scratch_shapes=scratch,
         compiler_params=pltpu.CompilerParams(vmem_limit_bytes=VMEM),
         cost_estimate=pl.CostEstimate(flops=1, bytes_accessed=1, transcendentals=0),
         name="rows",
-    )(*groups, *sources)
+    )(*groups, sources, *faced)
 
 
 def quarter_places(place_ref):
@@ -260,8 +284,8 @@
         refs[count + 1 : count + 3],
         refs[count + 3 : count + 5],
     )
-    first_earlier, *earlier = refs[count + 5 : count + 5 + STEPS]
-    near_ref, round_ref, lse_ref, own_row, first_row, round_row = refs[count + 5 + STEPS :]
+    first_earlier, *earlier = refs[count + 5 : count + 5 + PASSES]
+    near_ref, round_ref, lse_ref, own_row, first_row, round_row = refs[count + 5 + PASSES :]
     score_rows(group_refs[-1:], own_refs, near_ref.at[:, :HALF], own_row)
     score_rows(group_refs[-1:], first_refs, near_ref.at[:, HALF:], first_row)
     score_units(group_refs, round_refs, round_ref, round_row)
@@ -457,30 +481,28 @@
         [jnp.where(first, same, cross_core), jnp.where(first, cross_core, same)], axis=0
     )
     src_sq = jnp.sum(jnp.square(sources.astype(jnp.float32)), axis=1)
-    groups, crosses, lses = [], [], []
-    pending = [own, beside]
-    for step in (1, 2, 3):
+    groups, crosses, lses = [own, beside], [], []
+    for step in (1, 2):
         following = onward(unit)
         beside = other_core(unit)
         if step == 1:
             by_y, by_x = beside_y(straight), beside_x(straight)
-        cross, lse = row_pass(pending, [sources])
-        groups += pending
+        cross, lse = row_pass(groups[-2:], sources)
         crosses.append(cross)
+        lses.append(lse)
+        groups += [unit, beside]
         if step == 1:
-            following, lse, src_sq = lax.optimization_barrier((following, lse, src_sq))
-        elif step == 2:
-            following, lse, opposite = lax.optimization_barrier((following, lse, opposite))
+            unit, lses[0], src_sq = lax.optimization_barrier((following, lse, src_sq))
         else:
-            following, lse = lax.optimization_barrier((following, lse))
-        lses.append(lse)
-        pending = [unit, beside]
-        unit = following
-    cross, lse = row_pass(pending, [sources])
-    groups += pending
+            unit, lses[1] = lax.optimization_barrier((following, lse))
+            groups[-1], opposite = lax.optimization_barrier((groups[-1], opposite))
+    groups += [unit, other_core(unit)]
+    following = onward(unit)
+    cross, lse, first_cross, first_lse, faced_logw = row_pass(
+        groups, sources, [straight, opposite], 4
+    )
     crosses.append(cross)
-    first_cross, first_lse, faced_logw = row_pass(groups, [straight, opposite], True)
-    unit, lse, first_lse = lax.optimization_barrier((unit, lse, first_lse))
+    unit, lse, first_lse = lax.optimization_barrier((following, lse, first_lse))
     lses.append(lse)
     groups.append(unit)
     near, round_cross, shared = last_pass(

time: 73.1 us -> 73.1 us (level)
  blocking collectives: 26.1 us -> 29.2 us
  waiting for transfers between devices: 2.61 us -> 0.11 us
  Pallas kernels: 16.9 us -> 14.6 us
  starting transfers between devices: 25.3 us -> 27 us
    all_to_all x1, blocking collectives: 12.5 us -> 16 us  [on_device(): gathered = lax.all_to_all(columns, ('z', 'core'), 0, 0, tiled=True)]
    ppermute x2, waiting for transfers between devices: 2.58 us -> 0.09 us  [facing(): lax.ppermute(value, ('x_lo', 'x_hi'), [(0, 3), (3, 0), (1, 2), (2, 1)])]
    pallas_call x5 -> x3, Pallas kernels: 8.34 us -> 6.08 us  [row_pass(): pl.pallas_call(body, in_specs=[IN_VMEM] * (count + 1 + parts), out_specs=...]
    ppermute x4, starting transfers between devices: 3.07 us -> 4.57 us  [other_core(): return lax.ppermute(value, 'core', [(0, 1), (1, 0)])]
  transfers between devices with their start and end apart: 13 -> 13, of which waited for: 1 -> 1; matrix products, arithmetic and copies ran while one was open for 1% -> 1% of each run, Pallas kernels for 11% -> 8%
where the time goes in v5:
time: 73.1 us; the launch traced here: 72.9 us
  blocking collectives  29.2 us (40%)
  starting transfers between devices  27 us (37%)
  Pallas kernels  14.6 us (20%)
  other arithmetic  1.02 us (1%)
  between operations  0.79 us (1%)
    all_to_all x1, blocking collectives, on_device(): gathered = lax.all_to_all(columns, ('z', 'core'), 0, 0, tiled=True)  16 us
    all_to_all x1, blocking collectives, on_device(): partial = lax.all_to_all(shared, ('y', 'x_lo', 'x_hi'), 0, 0, tiled=True)  13.2 us
    ppermute x4, starting transfers between devices, onward(): return lax.ppermute(value, ('z', 'core'), up + down)  13 us
    pallas_call x3, Pallas kernels, row_pass(): pl.pallas_call(body, in_specs=[IN_VMEM] * (count + 1 + parts), out_specs=...  6.08 us
    ppermute x2, starting transfers between devices, facing(): lax.ppermute(value, ('x_lo', 'x_hi'), [(0, 3), (3, 0), (1, 2), (2, 1)])  5.04 us
    ppermute x4, starting transfers between devices, other_core(): return lax.ppermute(value, 'core', [(0, 1), (1, 0)])  4.57 us
    pallas_call x1, Pallas kernels, column_pass(): pl.pallas_call(body, in_specs=[IN_SMEM] + [IN_HBM] * (len(own_crosses) +...  4.01 us
    ppermute x1, starting transfers between devices, onward_across(): return lax.ppermute(value, ('z', 'core'), up + down)  3.11 us
  transfers between devices with their start and end apart: 13, of which 1 were waited for; matrix products, arithmetic and copies ran while one was open for 1% of the time, Pallas kernels for 8%

profile of v5, /device:TPU:1, one launch (start us, length us, event | category | flops | bytes accessed | tf_op | source)
XLA Modules:
  0.0 72.9 jit_solution(2500792022468410732)
XLA Ops:
  0.6 0.0 copy-start
  0.7 0.1 stack.32.place_ref.refs_0_
  0.7 1.7 %pack.1 = (bf16[64,896]{1,0:T(8,128)(2,1)S(1)}, f32[1,64]{1,0:T(1,128)S(1)}, bf16[272,768]{1,0:T(8,128)(2,1)S(1)}) custom-call(s32[8]{0:T(128)S(1)} %stack.32.place_ref.refs_0_, bf16[1024,768]{1,0:T(8,128)(2,1)} %refs_10_.1, bf16[64,768]{1,0:T(8,128)(2,1)} %tgt_hbm.1, f32[1,64]{1,0:T(1,128)} %bitcast.19, f32[1,64]{1,0:T(1,128)} %bitcast.20, f32[1,1024]{1,0:T(1,128)} %bitcast.15), custom_call_target="tpu_custom_call" | custom-call | tf_op jit(solution)/shard_map/pack/pallas_call | solution.py:139
  2.4 3.1 %collective-permute-start.2 = (bf16[64,896]{1,0:T(8,128)(2,1)S(1)}, bf16[64,896]{1,0:T(8,128)(2,1)S(1)}, u32[]{:S(2)}, u32[]{:S(2)}) collective-permute-start(bf16[64,896]{1,0:T(8,128)(2,1)S(1)} %get-tuple-element.29.refs_0_.refs_1_), channel_id=1, source_target_pairs={{1,4},{5,8},{9,12},{13,16},{17,20},{21,24},{25,28},{29,0},{0,29},{... | collective-permute-start | bytes 344072 | tf_op jit(solution)/shard_map/ppermute | solution.py:52
  5.6 3.5 %collective-permute-start.1 = (bf16[64,896]{1,0:T(8,128)(2,1)S(1)}, bf16[64,896]{1,0:T(8,128)(2,1)S(1)}, u32[]{:S(2)}, u32[]{:S(2)}) collective-permute-start(bf16[64,896]{1,0:T(8,128)(2,1)S(1)} %get-tuple-element.29.refs_0_.refs_1_), channel_id=1, source_target_pairs={{0,4},{4,8},{8,12},{12,16},{16,20},{20,24},{24,28},{28,0},{1,29},{... | collective-permute-start | bytes 344072 | tf_op jit(solution)/shard_map/ppermute | solution.py:45
  9.0 0.3 collective-permute-start
  9.3 2.5 %collective-permute-start.9 = (bf16[272,768]{1,0:T(8,128)(2,1)S(1)}, bf16[272,768]{1,0:T(8,128)(2,1)S(1)}, u32[]{:S(2)}, u32[]{:S(2)}) collective-permute-start(bf16[272,768]{1,0:T(8,128)(2,1)S(1)} %get-tuple-element.37), channel_id=1, source_target_pairs={{0,34},{34,0},{2,32},{32,2},{1,35},{35,1},{3,33},{33,3},{4,38},{38... | collective-permute-start | bytes 1253384 | tf_op jit(solution)/shard_map/ppermute | solution.py:60
  11.8 0.0 collective-permute-done.2
  11.8 0.0 collective-permute-done.1
  11.9 3.4 %collective-permute-start.4 = (bf16[128,896]{1,0:T(8,128)(2,1)S(1)}, bf16[128,896]{1,0:T(8,128)(2,1)S(1)}, u32[]{:S(2)}, u32[]{:S(2)}) collective-permute-start(bf16[128,896]{1,0:T(8,128)(2,1)S(1)} %pad_maximum_fusion.refs_0_.refs_2_.refs_3_), channel_id=1, source_target_pairs={{0,4},{4,8},{8,12},{12,16},{16,20},{20,24},{24,28},{28,0},{1,29},{... | collective-permute-start | bytes 688136 | tf_op jit(solution)/shard_map/ppermute | solution.py:45
  15.2 0.0 copy-done
  15.3 2.6 %collective-permute-start.6 = (bf16[256,768]{1,0:T(8,128)(2,1)S(1)}, bf16[256,768]{1,0:T(8,128)(2,1)S(1)}, u32[]{:S(2)}, u32[]{:S(2)}) collective-permute-start(bf16[256,768]{1,0:T(8,128)(2,1)S(1)} %constant_dynamic-slice_fusion), channel_id=1, source_target_pairs={{0,34},{34,0},{2,32},{32,2},{1,35},{35,1},{3,33},{33,3},{4,38},{38... | collective-permute-start | bytes 1179656 | tf_op jit(solution)/shard_map/ppermute | solution.py:60
  17.8 0.4 multiply_reduce_fusion
  18.2 0.6 collective-permute-start.3
  18.8 0.0 collective-permute-done.refs_1_.refs_2_
  18.9 1.5 %rows.3 = (f32[128,1024]{1,0:T(8,128)}, f32[1,1024]{1,0:T(1,128)S(1)}) custom-call(bf16[64,896]{1,0:T(8,128)(2,1)S(1)} %get-tuple-element.29.refs_0_.refs_1_, bf16[64,896]{1,0:T(8,128)(2,1)S(1)} %collective-permute-done.refs_1_.refs_2_, bf16[1024,768]{1,0:T(8,128)(2,1)S(1)} %copy-done), custom_call_target="tpu_custom_call" | custom-call | flops 1 | bytes 1 | tf_op jit(solution)/shard_map/rows/pallas_call | solution.py:264
  20.3 0.0 collective-permute-done.4.refs_4_.refs_5_
  20.3 3.0 %collective-permute-start.7 = (bf16[128,896]{1,0:T(8,128)(2,1)S(1)}, bf16[128,896]{1,0:T(8,128)(2,1)S(1)}, u32[]{:S(2)}, u32[]{:S(2)}) collective-permute-start(bf16[128,896]{1,0:T(8,128)(2,1)S(1)} %collective-permute-done.4.refs_4_.refs_5_), channel_id=1, source_target_pairs={{0,4},{4,8},{8,12},{12,16},{16,20},{20,24},{24,28},{28,0},{1,29},{... | collective-permute-start | bytes 688136 | tf_op jit(solution)/shard_map/ppermute | solution.py:45
  23.3 0.0 collective-permute-done.9.refs_9_.refs_11_
  23.3 0.0 collective-permute-start.12
  23.3 1.3 %collective-permute-start.11 = (bf16[272,768]{1,0:T(8,128)(2,1)S(1)}, bf16[272,768]{1,0:T(8,128)(2,1)S(1)}, u32[]{:S(2)}, u32[]{:S(2)}) collective-permute-start(bf16[272,768]{1,0:T(8,128)(2,1)S(1)} %collective-permute-done.9.refs_9_.refs_11_), channel_id=1, source_target_pairs={{0,64},{64,0},{128,192},{192,128},{1,65},{65,1},{129,193},{193,129... | collective-permute-start | bytes 1253384 | tf_op jit(solution)/shard_map/ppermute | solution.py:68
  24.6 0.0 collective-permute-done.3.refs_1_.refs_3_.refs_4_
  24.7 1.1 %collective-permute-start.5 = (bf16[128,896]{1,0:T(8,128)(2,1)S(1)}, bf16[128,896]{1,0:T(8,128)(2,1)S(1)}, u32[]{:S(2)}, u32[]{:S(2)}) collective-permute-start(bf16[128,896]{1,0:T(8,128)(2,1)S(1)} %collective-permute-done.4.refs_4_.refs_5_), channel_id=1, source_target_pairs={{0,1},{1,0},{2,3},{3,2},{4,5},{5,4},{6,7},{7,6},{8,9},{9,8},{10,11... | collective-permute-start | bytes 688136 | tf_op jit(solution)/shard_map/ppermute | solution.py:56
  25.8 1.6 %rows.4 = (f32[256,1024]{1,0:T(8,128)}, f32[1,1024]{1,0:T(1,128)S(1)}) custom-call(bf16[128,896]{1,0:T(8,128)(2,1)S(1)} %pad_maximum_fusion.refs_0_.refs_2_.refs_3_, bf16[128,896]{1,0:T(8,128)(2,1)S(1)} %collective-permute-done.3.refs_1_.refs_3_.refs_4_, bf16[1024,768]{1,0:T(8,128)(2,1)S(1)} %copy-done), custom_call_target="tpu_custom_call" | custom-call | flops 1 | bytes 1 | tf_op jit(solution)/shard_map/rows/pallas_call | solution.py:264
  27.4 0.0 collective-permute-done.7.refs_6_.refs_7_
  27.4 2.5 %collective-permute-start.8 = (bf16[128,896]{1,0:T(8,128)(2,1)S(1)}, bf16[128,896]{1,0:T(8,128)(2,1)S(1)}, u32[]{:S(2)}, u32[]{:S(2)}) collective-permute-start(bf16[128,896]{1,0:T(8,128)(2,1)S(1)} %collective-permute-done.7.refs_6_.refs_7_), channel_id=1, source_target_pairs={{0,1},{1,0},{2,3},{3,2},{4,5},{5,4},{6,7},{7,6},{8,9},{9,8},{10,11... | collective-permute-start | bytes 688136 | tf_op jit(solution)/shard_map/ppermute | solution.py:56
  29.9 0.1 collective-permute-done.6.refs_10_.refs_12_
  30.0 3.2 %collective-permute-start.10 = (bf16[128,896]{1,0:T(8,128)(2,1)S(1)}, bf16[128,896]{1,0:T(8,128)(2,1)S(1)}, u32[]{:S(2)}, u32[]{:S(2)}) collective-permute-start(bf16[128,896]{1,0:T(8,128)(2,1)S(1)} %collective-permute-done.7.refs_6_.refs_7_), channel_id=1, source_target_pairs={{0,4},{4,8},{8,12},{12,16},{16,20},{20,24},{24,28},{28,0},{1,29},{... | collective-permute-start | bytes 688136 | tf_op jit(solution)/shard_map/ppermute | solution.py:45
  33.2 0.0 collective-permute-done.5.refs_5_.refs_6_
  33.2 0.0 collective-permute-done.8.refs_7_.refs_8_
  33.2 3.0 %rows.5 = (f32[512,1024]{1,0:T(8,128)}, f32[1,1024]{1,0:T(1,128)S(1)}, f32[896,512]{1,0:T(8,128)}, f32[1,512]{1,0:T(1,128)S(1)}, f32[1,1024]{1,0:T(1,128)S(1)}) custom-call(bf16[64,896]{1,0:T(8,128)(2,1)S(1)} %get-tuple-element.29.refs_0_.refs_1_, bf16[64,896]{1,0:T(8,128)(2,1)S(1)} %collective-permute-done.refs_1_.refs_2_, ...), custom_call_target="tpu_custom_call" | custom-call | flops 1 | bytes 1 | tf_op jit(solution)/shard_map/rows/pallas_call | solution.py:264
  36.2 0.0 collective-permute-done.10.refs_9_
  36.2 0.0 copy-start.1
  36.2 0.0 collective-permute-done.12.refs_14_
  36.2 0.0 collective-permute-done.11.refs_13_
  36.2 2.8 %last_rows.1 = (f32[128,1536]{1,0:T(8,128)S(1)}, f32[1024,512]{1,0:T(8,128)S(1)}, f32[16,1,2048]{2,1,0:T(1,128)S(1)}) custom-call(s32[8]{0:T(128)S(1)} %stack.32.place_ref.refs_0_, bf16[64,896]{1,0:T(8,128)(2,1)S(1)} %get-tuple-element.29.refs_0_.refs_1_, bf16[64,896]{1,0:T(8,128)(2,1)S(1)} %collective-permute-done.refs_1_.refs_2_, ...), custom_call_target="tpu_custom_call" | custom-call | flops 1107296256 | bytes 6029312 | tf_op jit(solution)/shard_map/last_rows/pallas_call | solution.py:314
  39.1 13.2 %all_to_all.10.refs_7_ = f32[16,1,2048]{2,1,0:T(1,128)S(1)} all-to-all(f32[16,1,2048]{2,1,0:T(1,128)S(1)} %get-tuple-element.50), channel_id=1, replica_groups=mesh['y'=4,'x_lo'=2,'z'=8,'x_hi'=2,'core'=2] {'y','x_lo','x_hi'}, dimensions={0} | all-to-all | bytes 262144 | tf_op jit(solution)/shard_map/all_to_all | solution.py:512
  52.3 0.0 copy-done.1
  52.3 4.0 %columns.1 = (f32[16,1,64]{2,1,0:T(1,128)S(1)}, f32[1,1024]{1,0:T(1,128)}) custom-call(s32[8]{0:T(128)S(1)} %stack.32.place_ref.refs_0_, f32[128,1024]{1,0:T(8,128)} %get-tuple-element.30.refs_1_, f32[256,1024]{1,0:T(8,128)} %get-tuple-element.31.refs_2_, f32[512,1024]{1,0:T(8,128)} %get-tuple-element.39.refs_3_, f32[896,512]{1,0:T(8,128)} %get-tuple-element.40.refs_4_, ...), custom_call_target="tpu_custom_call" | custom-call | flops 12582912 | bytes 8388608 | tf_op jit(solution)/shard_map/columns/pallas_call | solution.py:429
  56.3 16.0 %all_to_all.11 = f32[16,1,64]{2,1,0:T(1,128)S(1)} all-to-all(f32[16,1,64]{2,1,0:T(1,128)S(1)} %get-tuple-element.55), channel_id=1, replica_groups=mesh['y'=4,'x_lo'=2,'z'=8,'x_hi'=2,'core'=2] {'z','core'}, dimensions={0} | all-to-all | bytes 8192 | tf_op jit(solution)/shard_map/all_to_all | solution.py:516
  72.4 0.5 bitcast_subtract_fusion
  (5 shorter events, 0.1 us)
Async XLA Ops:
  0.6 14.6 %copy-start = (bf16[1024,768]{1,0:T(8,128)(2,1)S(1)}, bf16[1024,768]{1,0:T(8,128)(2,1)}, u32[]{:S(2)}) copy-start(bf16[1024,768]{1,0:T(8,128)(2,1)} %refs_10_.1) | copy-start | bytes 4718596
  2.4 9.4 %collective-permute-start.2 = (bf16[64,896]{1,0:T(8,128)(2,1)S(1)}, bf16[64,896]{1,0:T(8,128)(2,1)S(1)}, u32[]{:S(2)}, u32[]{:S(2)}) collective-permute-start(bf16[64,896]{1,0:T(8,128)(2,1)S(1)} %get-tuple-element.29.refs_0_.refs_1_), channel_id=1, source_target_pairs={{1,4},{5,8},{9,12},{13,16},{17,20},{21,24},{25,28},{29,0},{0,29},{... | collective-permute-start | bytes 344072 | tf_op jit(solution)/shard_map/ppermute | solution.py:52
  5.6 6.3 %collective-permute-start.1 = (bf16[64,896]{1,0:T(8,128)(2,1)S(1)}, bf16[64,896]{1,0:T(8,128)(2,1)S(1)}, u32[]{:S(2)}, u32[]{:S(2)}) collective-permute-start(bf16[64,896]{1,0:T(8,128)(2,1)S(1)} %get-tuple-element.29.refs_0_.refs_1_), channel_id=1, source_target_pairs={{0,4},{4,8},{8,12},{12,16},{16,20},{20,24},{24,28},{28,0},{1,29},{... | collective-permute-start | bytes 344072 | tf_op jit(solution)/shard_map/ppermute | solution.py:45
  9.0 9.8 %collective-permute-start = (bf16[64,896]{1,0:T(8,128)(2,1)S(1)}, bf16[64,896]{1,0:T(8,128)(2,1)S(1)}, u32[]{:S(2)}, u32[]{:S(2)}) collective-permute-start(bf16[64,896]{1,0:T(8,128)(2,1)S(1)} %get-tuple-element.29.refs_0_.refs_1_), channel_id=1, source_target_pairs={{0,1},{1,0},{2,3},{3,2},{4,5},{5,4},{6,7},{7,6},{8,9},{9,8},{10,11... | collective-permute-start | bytes 344072 | tf_op jit(solution)/shard_map/ppermute | solution.py:56
  9.3 14.0 %collective-permute-start.9 = (bf16[272,768]{1,0:T(8,128)(2,1)S(1)}, bf16[272,768]{1,0:T(8,128)(2,1)S(1)}, u32[]{:S(2)}, u32[]{:S(2)}) collective-permute-start(bf16[272,768]{1,0:T(8,128)(2,1)S(1)} %get-tuple-element.37), channel_id=1, source_target_pairs={{0,34},{34,0},{2,32},{32,2},{1,35},{35,1},{3,33},{33,3},{4,38},{38... | collective-permute-start | bytes 1253384 | tf_op jit(solution)/shard_map/ppermute | solution.py:60
  11.9 8.4 %collective-permute-start.4 = (bf16[128,896]{1,0:T(8,128)(2,1)S(1)}, bf16[128,896]{1,0:T(8,128)(2,1)S(1)}, u32[]{:S(2)}, u32[]{:S(2)}) collective-permute-start(bf16[128,896]{1,0:T(8,128)(2,1)S(1)} %pad_maximum_fusion.refs_0_.refs_2_.refs_3_), channel_id=1, source_target_pairs={{0,4},{4,8},{8,12},{12,16},{16,20},{20,24},{24,28},{28,0},{1,29},{... | collective-permute-start | bytes 688136 | tf_op jit(solution)/shard_map/ppermute | solution.py:45
  15.3 14.7 %collective-permute-start.6 = (bf16[256,768]{1,0:T(8,128)(2,1)S(1)}, bf16[256,768]{1,0:T(8,128)(2,1)S(1)}, u32[]{:S(2)}, u32[]{:S(2)}) collective-permute-start(bf16[256,768]{1,0:T(8,128)(2,1)S(1)} %constant_dynamic-slice_fusion), channel_id=1, source_target_pairs={{0,34},{34,0},{2,32},{32,2},{1,35},{35,1},{3,33},{33,3},{4,38},{38... | collective-permute-start | bytes 1179656 | tf_op jit(solution)/shard_map/ppermute | solution.py:60
  18.2 6.4 %collective-permute-start.3 = (bf16[128,896]{1,0:T(8,128)(2,1)S(1)}, bf16[128,896]{1,0:T(8,128)(2,1)S(1)}, u32[]{:S(2)}, u32[]{:S(2)}) collective-permute-start(bf16[128,896]{1,0:T(8,128)(2,1)S(1)} %pad_maximum_fusion.refs_0_.refs_2_.refs_3_), channel_id=1, source_target_pairs={{0,1},{1,0},{2,3},{3,2},{4,5},{5,4},{6,7},{7,6},{8,9},{9,8},{10,11... | collective-permute-start | bytes 688136 | tf_op jit(solution)/shard_map/ppermute | solution.py:56
  20.3 7.1 %collective-permute-start.7 = (bf16[128,896]{1,0:T(8,128)(2,1)S(1)}, bf16[128,896]{1,0:T(8,128)(2,1)S(1)}, u32[]{:S(2)}, u32[]{:S(2)}) collective-permute-start(bf16[128,896]{1,0:T(8,128)(2,1)S(1)} %collective-permute-done.4.refs_4_.refs_5_), channel_id=1, source_target_pairs={{0,4},{4,8},{8,12},{12,16},{16,20},{20,24},{24,28},{28,0},{1,29},{... | collective-permute-start | bytes 688136 | tf_op jit(solution)/shard_map/ppermute | solution.py:45
  23.3 12.9 %collective-permute-start.12 = (bf16[272,768]{1,0:T(8,128)(2,1)S(1)}, bf16[272,768]{1,0:T(8,128)(2,1)S(1)}, u32[]{:S(2)}, u32[]{:S(2)}) collective-permute-start(bf16[272,768]{1,0:T(8,128)(2,1)S(1)} %collective-permute-done.9.refs_9_.refs_11_), channel_id=1, source_target_pairs={{0,32},{32,0},{1,33},{33,1},{2,34},{34,2},{3,35},{35,3},{4,36},{36... | collective-permute-start | bytes 1253384 | tf_op jit(solution)/shard_map/ppermute | solution.py:64
  23.3 12.9 %collective-permute-start.11 = (bf16[272,768]{1,0:T(8,128)(2,1)S(1)}, bf16[272,768]{1,0:T(8,128)(2,1)S(1)}, u32[]{:S(2)}, u32[]{:S(2)}) collective-permute-start(bf16[272,768]{1,0:T(8,128)(2,1)S(1)} %collective-permute-done.9.refs_9_.refs_11_), channel_id=1, source_target_pairs={{0,64},{64,0},{128,192},{192,128},{1,65},{65,1},{129,193},{193,129... | collective-permute-start | bytes 1253384 | tf_op jit(solution)/shard_map/ppermute | solution.py:68
  24.7 8.5 %collective-permute-start.5 = (bf16[128,896]{1,0:T(8,128)(2,1)S(1)}, bf16[128,896]{1,0:T(8,128)(2,1)S(1)}, u32[]{:S(2)}, u32[]{:S(2)}) collective-permute-start(bf16[128,896]{1,0:T(8,128)(2,1)S(1)} %collective-permute-done.4.refs_4_.refs_5_), channel_id=1, source_target_pairs={{0,1},{1,0},{2,3},{3,2},{4,5},{5,4},{6,7},{7,6},{8,9},{9,8},{10,11... | collective-permute-start | bytes 688136 | tf_op jit(solution)/shard_map/ppermute | solution.py:56
  27.4 5.8 %collective-permute-start.8 = (bf16[128,896]{1,0:T(8,128)(2,1)S(1)}, bf16[128,896]{1,0:T(8,128)(2,1)S(1)}, u32[]{:S(2)}, u32[]{:S(2)}) collective-permute-start(bf16[128,896]{1,0:T(8,128)(2,1)S(1)} %collective-permute-done.7.refs_6_.refs_7_), channel_id=1, source_target_pairs={{0,1},{1,0},{2,3},{3,2},{4,5},{5,4},{6,7},{7,6},{8,9},{9,8},{10,11... | collective-permute-start | bytes 688136 | tf_op jit(solution)/shard_map/ppermute | solution.py:56
  30.0 6.2 %collective-permute-start.10 = (bf16[128,896]{1,0:T(8,128)(2,1)S(1)}, bf16[128,896]{1,0:T(8,128)(2,1)S(1)}, u32[]{:S(2)}, u32[]{:S(2)}) collective-permute-start(bf16[128,896]{1,0:T(8,128)(2,1)S(1)} %collective-permute-done.7.refs_6_.refs_7_), channel_id=1, source_target_pairs={{0,4},{4,8},{8,12},{12,16},{16,20},{20,24},{24,28},{28,0},{1,29},{... | collective-permute-start | bytes 688136 | tf_op jit(solution)/shard_map/ppermute | solution.py:45
  36.2 16.1 %copy-start.1 = (f32[1024]{0:T(1024)S(1)}, f32[1024]{0:T(1024)}, u32[]{:S(2)}) copy-start(f32[1024]{0:T(1024)} %param.8) | copy-start | bytes 12292

commit v6 on v5

--- a/solution.py
+++ b/solution.py
@@ -40,15 +40,15 @@
 
 def onward(value):
     count = lax.axis_size("z")
-    up = [(2 * i, 2 * ((i + 1) % count)) for i in range(count)]
-    down = [(2 * i + 1, 2 * ((i - 1) % count) + 1) for i in range(count)]
+    up = [(2 * i + 1, 2 * ((i + 1) % count) + 1) for i in range(count)]
+    down = [(2 * i, 2 * ((i - 1) % count)) for i in range(count)]
     return lax.ppermute(value, ("z", "core"), up + down)
 
 
 def onward_across(value):
     count = lax.axis_size("z")
-    up = [(2 * i + 1, 2 * ((i + 1) % count)) for i in range(count)]
-    down = [(2 * i, 2 * ((i - 1) % count) + 1) for i in range(count)]
+    up = [(2 * i, 2 * ((i + 1) % count) + 1) for i in range(count)]
+    down = [(2 * i + 1, 2 * ((i - 1) % count)) for i in range(count)]
     return lax.ppermute(value, ("z", "core"), up + down)
 
 
@@ -403,7 +403,7 @@
             pieces += lanes(first_held[rows, :] + first_bias)
             before = peak_ref[rows, :], total_ref[rows, :]
             peak_ref[rows, :], total_ref[rows, :] = sums(pieces, before)
-    side = 2 * core - 1
+    side = 1 - 2 * core
     for unit in range(UNITS):
         rows = slice(unit * UNIT, (unit + 1) * UNIT)
         peak, total = peak_ref[rows, :].T, total_ref[rows, :].T

time: 73.1 us -> 72 us (0.985)
  waiting for transfers between devices: 0.11 us -> 8.2 us
  starting transfers between devices: 27 us -> 19.6 us
  blocking collectives: 29.2 us -> 27.4 us
    ppermute x4, starting transfers between devices: 13 us -> 0.17 us  [onward(): return lax.ppermute(value, ('z', 'core'), up + down)]
    ppermute x4, waiting for transfers between devices: 0.01 us -> 5.25 us  [onward(): return lax.ppermute(value, ('z', 'core'), up + down)]
    ppermute x1, starting transfers between devices: 3.11 us -> 7.05 us  [onward_across(): return lax.ppermute(value, ('z', 'core'), up + down)]
    ppermute x2, waiting for transfers between devices: 0.09 us -> 2.94 us  [facing(): lax.ppermute(value, ('x_lo', 'x_hi'), [(0, 3), (3, 0), (1, 2), (2, 1)])]
    all_to_all x1, blocking collectives: 16 us -> 14.2 us  [on_device(): gathered = lax.all_to_all(columns, ('z', 'core'), 0, 0, tiled=True)]
    ppermute x4, starting transfers between devices: 4.57 us -> 6.07 us  [other_core(): return lax.ppermute(value, 'core', [(0, 1), (1, 0)])]
  transfers between devices with their start and end apart: 13 -> 13, of which waited for: 1 -> 4; matrix products, arithmetic and copies ran while one was open for 1% -> 1% of each run, Pallas kernels for 8% -> 8%
where the time goes in v6:
time: 72 us; the launch traced here: 71.8 us
  blocking collectives  27.4 us (38%)
  starting transfers between devices  19.6 us (27%)
  Pallas kernels  14.6 us (20%)
  waiting for transfers between devices  8.2 us (11%)
  other arithmetic  1.02 us (1%)
  between operations  0.8 us (1%)
    all_to_all x1, blocking collectives, on_device(): gathered = lax.all_to_all(columns, ('z', 'core'), 0, 0, tiled=True)  14.2 us
    all_to_all x1, blocking collectives, on_device(): partial = lax.all_to_all(shared, ('y', 'x_lo', 'x_hi'), 0, 0, tiled=True)  13.2 us
    ppermute x1, starting transfers between devices, onward_across(): return lax.ppermute(value, ('z', 'core'), up + down)  7.05 us
    pallas_call x3, Pallas kernels, row_pass(): pl.pallas_call(body, in_specs=[IN_VMEM] * (count + 1 + parts), out_specs=...  6.1 us
    ppermute x4, starting transfers between devices, other_core(): return lax.ppermute(value, 'core', [(0, 1), (1, 0)])  6.07 us
    ppermute x4, waiting for transfers between devices, onward(): return lax.ppermute(value, ('z', 'core'), up + down)  5.25 us
    ppermute x2, starting transfers between devices, facing(): lax.ppermute(value, ('x_lo', 'x_hi'), [(0, 3), (3, 0), (1, 2), (2, 1)])  5.04 us
    pallas_call x1, Pallas kernels, column_pass(): pl.pallas_call(body, in_specs=[IN_SMEM] + [IN_HBM] * (len(own_crosses) +...  4.01 us
  transfers between devices with their start and end apart: 13, of which 4 were waited for; matrix products, arithmetic and copies ran while one was open for 1% of the time, Pallas kernels for 8%

profile of v6, /device:TPU:1, one launch (start us, length us, event | category | flops | bytes accessed | tf_op | source)
XLA Modules:
  0.0 71.8 jit_solution(1592550109479713686)
XLA Ops:
  0.6 0.0 copy-start
  0.7 0.1 stack.32.place_ref.refs_0_
  0.7 1.7 %pack.1 = (bf16[64,896]{1,0:T(8,128)(2,1)S(1)}, f32[1,64]{1,0:T(1,128)S(1)}, bf16[272,768]{1,0:T(8,128)(2,1)S(1)}) custom-call(s32[8]{0:T(128)S(1)} %stack.32.place_ref.refs_0_, bf16[1024,768]{1,0:T(8,128)(2,1)} %refs_10_.1, bf16[64,768]{1,0:T(8,128)(2,1)} %tgt_hbm.1, f32[1,64]{1,0:T(1,128)} %bitcast.19, f32[1,64]{1,0:T(1,128)} %bitcast.20, f32[1,1024]{1,0:T(1,128)} %bitcast.15), custom_call_target="tpu_custom_call" | custom-call | tf_op jit(solution)/shard_map/pack/pallas_call | solution.py:139
  2.4 7.1 %collective-permute-start.2 = (bf16[64,896]{1,0:T(8,128)(2,1)S(1)}, bf16[64,896]{1,0:T(8,128)(2,1)S(1)}, u32[]{:S(2)}, u32[]{:S(2)}) collective-permute-start(bf16[64,896]{1,0:T(8,128)(2,1)S(1)} %get-tuple-element.29.refs_0_.refs_1_), channel_id=1, source_target_pairs={{0,5},{4,9},{8,13},{12,17},{16,21},{20,25},{24,29},{28,1},{1,28},{... | collective-permute-start | bytes 344072 | tf_op jit(solution)/shard_map/ppermute | solution.py:52
  9.5 0.0 collective-permute-start.1
  9.5 0.5 collective-permute-start
  10.0 2.5 %collective-permute-start.9 = (bf16[272,768]{1,0:T(8,128)(2,1)S(1)}, bf16[272,768]{1,0:T(8,128)(2,1)S(1)}, u32[]{:S(2)}, u32[]{:S(2)}) collective-permute-start(bf16[272,768]{1,0:T(8,128)(2,1)S(1)} %get-tuple-element.37), channel_id=1, source_target_pairs={{0,34},{34,0},{2,32},{32,2},{1,35},{35,1},{3,33},{33,3},{4,38},{38... | collective-permute-start | bytes 1253384 | tf_op jit(solution)/shard_map/ppermute | solution.py:60
  12.5 0.0 collective-permute-done.2
  12.5 2.2 %collective-permute-done.1 = bf16[64,896]{1,0:T(8,128)(2,1)S(1)} collective-permute-done((bf16[64,896]{1,0:T(8,128)(2,1)S(1)}, bf16[64,896]{1,0:T(8,128)(2,1)S(1)}, u32[]{:S(2)}, u32[]{:S(2)}) %collective-permute-start.1) | collective-permute-done | bytes 114720 | tf_op jit(solution)/shard_map/ppermute | solution.py:45
  14.7 0.1 collective-permute-start.4
  14.8 0.0 copy-done
  14.8 2.6 %collective-permute-start.6 = (bf16[256,768]{1,0:T(8,128)(2,1)S(1)}, bf16[256,768]{1,0:T(8,128)(2,1)S(1)}, u32[]{:S(2)}, u32[]{:S(2)}) collective-permute-start(bf16[256,768]{1,0:T(8,128)(2,1)S(1)} %constant_dynamic-slice_fusion), channel_id=1, source_target_pairs={{0,34},{34,0},{2,32},{32,2},{1,35},{35,1},{3,33},{33,3},{4,38},{38... | collective-permute-start | bytes 1179656 | tf_op jit(solution)/shard_map/ppermute | solution.py:60
  17.4 0.4 multiply_reduce_fusion
  17.8 2.2 %collective-permute-start.3 = (bf16[128,896]{1,0:T(8,128)(2,1)S(1)}, bf16[128,896]{1,0:T(8,128)(2,1)S(1)}, u32[]{:S(2)}, u32[]{:S(2)}) collective-permute-start(bf16[128,896]{1,0:T(8,128)(2,1)S(1)} %pad_maximum_fusion.refs_0_.refs_2_.refs_3_), channel_id=1, source_target_pairs={{0,1},{1,0},{2,3},{3,2},{4,5},{5,4},{6,7},{7,6},{8,9},{9,8},{10,11... | collective-permute-start | bytes 688136 | tf_op jit(solution)/shard_map/ppermute | solution.py:56
  20.0 0.0 collective-permute-done.refs_1_.refs_2_
  20.0 1.5 %rows.3 = (f32[128,1024]{1,0:T(8,128)}, f32[1,1024]{1,0:T(1,128)S(1)}) custom-call(bf16[64,896]{1,0:T(8,128)(2,1)S(1)} %get-tuple-element.29.refs_0_.refs_1_, bf16[64,896]{1,0:T(8,128)(2,1)S(1)} %collective-permute-done.refs_1_.refs_2_, bf16[1024,768]{1,0:T(8,128)(2,1)S(1)} %copy-done), custom_call_target="tpu_custom_call" | custom-call | flops 1 | bytes 1 | tf_op jit(solution)/shard_map/rows/pallas_call | solution.py:264
  21.5 0.0 collective-permute-done.4.refs_4_.refs_5_
  21.5 0.1 collective-permute-start.7
  21.6 0.8 %collective-permute-done.9.refs_9_.refs_11_ = bf16[272,768]{1,0:T(8,128)(2,1)S(1)} collective-permute-done((bf16[272,768]{1,0:T(8,128)(2,1)S(1)}, bf16[272,768]{1,0:T(8,128)(2,1)S(1)}, u32[]{:S(2)}, u32[]{:S(2)}) %collective-permute-start.9) | collective-permute-done | bytes 417824 | tf_op jit(solution)/shard_map/ppermute | solution.py:60
  22.4 0.0 collective-permute-start.12
  22.4 1.3 %collective-permute-start.11 = (bf16[272,768]{1,0:T(8,128)(2,1)S(1)}, bf16[272,768]{1,0:T(8,128)(2,1)S(1)}, u32[]{:S(2)}, u32[]{:S(2)}) collective-permute-start(bf16[272,768]{1,0:T(8,128)(2,1)S(1)} %collective-permute-done.9.refs_9_.refs_11_), channel_id=1, source_target_pairs={{0,64},{64,0},{128,192},{192,128},{1,65},{65,1},{129,193},{193,129... | collective-permute-start | bytes 1253384 | tf_op jit(solution)/shard_map/ppermute | solution.py:68
  23.7 0.0 collective-permute-done.3.refs_1_.refs_3_.refs_4_
  23.7 3.3 %collective-permute-start.5 = (bf16[128,896]{1,0:T(8,128)(2,1)S(1)}, bf16[128,896]{1,0:T(8,128)(2,1)S(1)}, u32[]{:S(2)}, u32[]{:S(2)}) collective-permute-start(bf16[128,896]{1,0:T(8,128)(2,1)S(1)} %collective-permute-done.4.refs_4_.refs_5_), channel_id=1, source_target_pairs={{0,1},{1,0},{2,3},{3,2},{4,5},{5,4},{6,7},{7,6},{8,9},{9,8},{10,11... | collective-permute-start | bytes 688136 | tf_op jit(solution)/shard_map/ppermute | solution.py:56
  27.0 1.6 %rows.4 = (f32[256,1024]{1,0:T(8,128)}, f32[1,1024]{1,0:T(1,128)S(1)}) custom-call(bf16[128,896]{1,0:T(8,128)(2,1)S(1)} %pad_maximum_fusion.refs_0_.refs_2_.refs_3_, bf16[128,896]{1,0:T(8,128)(2,1)S(1)} %collective-permute-done.3.refs_1_.refs_3_.refs_4_, bf16[1024,768]{1,0:T(8,128)(2,1)S(1)} %copy-done), custom_call_target="tpu_custom_call" | custom-call | flops 1 | bytes 1 | tf_op jit(solution)/shard_map/rows/pallas_call | solution.py:264
  28.6 0.0 collective-permute-done.7.refs_6_.refs_7_
  28.6 0.1 collective-permute-start.8
  28.7 2.1 %collective-permute-done.6.refs_10_.refs_12_ = bf16[256,768]{1,0:T(8,128)(2,1)S(1)} collective-permute-done((bf16[256,768]{1,0:T(8,128)(2,1)S(1)}, bf16[256,768]{1,0:T(8,128)(2,1)S(1)}, u32[]{:S(2)}, u32[]{:S(2)}) %collective-permute-start.6) | collective-permute-done | bytes 393248 | tf_op jit(solution)/shard_map/ppermute | solution.py:60
  30.9 0.0 collective-permute-start.10
  30.9 0.0 collective-permute-done.5.refs_5_.refs_6_
  30.9 0.0 collective-permute-done.8.refs_7_.refs_8_
  30.9 3.0 %rows.5 = (f32[512,1024]{1,0:T(8,128)}, f32[1,1024]{1,0:T(1,128)S(1)}, f32[896,512]{1,0:T(8,128)}, f32[1,512]{1,0:T(1,128)S(1)}, f32[1,1024]{1,0:T(1,128)S(1)}) custom-call(bf16[64,896]{1,0:T(8,128)(2,1)S(1)} %get-tuple-element.29.refs_0_.refs_1_, bf16[64,896]{1,0:T(8,128)(2,1)S(1)} %collective-permute-done.refs_1_.refs_2_, ...), custom_call_target="tpu_custom_call" | custom-call | flops 1 | bytes 1 | tf_op jit(solution)/shard_map/rows/pallas_call | solution.py:264
  33.9 3.1 %collective-permute-done.10.refs_9_ = bf16[128,896]{1,0:T(8,128)(2,1)S(1)} collective-permute-done((bf16[128,896]{1,0:T(8,128)(2,1)S(1)}, bf16[128,896]{1,0:T(8,128)(2,1)S(1)}, u32[]{:S(2)}, u32[]{:S(2)}) %collective-permute-start.10) | collective-permute-done | bytes 229408 | tf_op jit(solution)/shard_map/ppermute | solution.py:45
  36.9 0.0 copy-start.1
  36.9 0.0 collective-permute-done.12.refs_14_
  36.9 0.0 collective-permute-done.11.refs_13_
  37.0 2.8 %last_rows.1 = (f32[128,1536]{1,0:T(8,128)S(1)}, f32[1024,512]{1,0:T(8,128)S(1)}, f32[16,1,2048]{2,1,0:T(1,128)S(1)}) custom-call(s32[8]{0:T(128)S(1)} %stack.32.place_ref.refs_0_, bf16[64,896]{1,0:T(8,128)(2,1)S(1)} %get-tuple-element.29.refs_0_.refs_1_, bf16[64,896]{1,0:T(8,128)(2,1)S(1)} %collective-permute-done.refs_1_.refs_2_, ...), custom_call_target="tpu_custom_call" | custom-call | flops 1107296256 | bytes 6029312 | tf_op jit(solution)/shard_map/last_rows/pallas_call | solution.py:314
  39.8 13.2 %all_to_all.10.refs_7_ = f32[16,1,2048]{2,1,0:T(1,128)S(1)} all-to-all(f32[16,1,2048]{2,1,0:T(1,128)S(1)} %get-tuple-element.50), channel_id=1, replica_groups=mesh['y'=4,'x_lo'=2,'z'=8,'x_hi'=2,'core'=2] {'y','x_lo','x_hi'}, dimensions={0} | all-to-all | bytes 262144 | tf_op jit(solution)/shard_map/all_to_all | solution.py:512
  53.0 0.0 copy-done.1
  53.0 4.0 %columns.1 = (f32[16,1,64]{2,1,0:T(1,128)S(1)}, f32[1,1024]{1,0:T(1,128)}) custom-call(s32[8]{0:T(128)S(1)} %stack.32.place_ref.refs_0_, f32[128,1024]{1,0:T(8,128)} %get-tuple-element.30.refs_1_, f32[256,1024]{1,0:T(8,128)} %get-tuple-element.31.refs_2_, f32[512,1024]{1,0:T(8,128)} %get-tuple-element.39.refs_3_, f32[896,512]{1,0:T(8,128)} %get-tuple-element.40.refs_4_, ...), custom_call_target="tpu_custom_call" | custom-call | flops 12582912 | bytes 8388608 | tf_op jit(solution)/shard_map/columns/pallas_call | solution.py:429
  57.0 14.2 %all_to_all.11 = f32[16,1,64]{2,1,0:T(1,128)S(1)} all-to-all(f32[16,1,64]{2,1,0:T(1,128)S(1)} %get-tuple-element.55), channel_id=1, replica_groups=mesh['y'=4,'x_lo'=2,'z'=8,'x_hi'=2,'core'=2] {'z','core'}, dimensions={0} | all-to-all | bytes 8192 | tf_op jit(solution)/shard_map/all_to_all | solution.py:516
  71.3 0.5 bitcast_subtract_fusion
  (5 shorter events, 0.1 us)
Async XLA Ops:
  0.6 14.2 %copy-start = (bf16[1024,768]{1,0:T(8,128)(2,1)S(1)}, bf16[1024,768]{1,0:T(8,128)(2,1)}, u32[]{:S(2)}) copy-start(bf16[1024,768]{1,0:T(8,128)(2,1)} %refs_10_.1) | copy-start | bytes 4718596
  2.4 10.0 %collective-permute-start.2 = (bf16[64,896]{1,0:T(8,128)(2,1)S(1)}, bf16[64,896]{1,0:T(8,128)(2,1)S(1)}, u32[]{:S(2)}, u32[]{:S(2)}) collective-permute-start(bf16[64,896]{1,0:T(8,128)(2,1)S(1)} %get-tuple-element.29.refs_0_.refs_1_), channel_id=1, source_target_pairs={{0,5},{4,9},{8,13},{12,17},{16,21},{20,25},{24,29},{28,1},{1,28},{... | collective-permute-start | bytes 344072 | tf_op jit(solution)/shard_map/ppermute | solution.py:52
  9.5 5.1 %collective-permute-start.1 = (bf16[64,896]{1,0:T(8,128)(2,1)S(1)}, bf16[64,896]{1,0:T(8,128)(2,1)S(1)}, u32[]{:S(2)}, u32[]{:S(2)}) collective-permute-start(bf16[64,896]{1,0:T(8,128)(2,1)S(1)} %get-tuple-element.29.refs_0_.refs_1_), channel_id=1, source_target_pairs={{1,5},{5,9},{9,13},{13,17},{17,21},{21,25},{25,29},{29,1},{0,28},{... | collective-permute-start | bytes 344072 | tf_op jit(solution)/shard_map/ppermute | solution.py:45
  9.5 10.5 %collective-permute-start = (bf16[64,896]{1,0:T(8,128)(2,1)S(1)}, bf16[64,896]{1,0:T(8,128)(2,1)S(1)}, u32[]{:S(2)}, u32[]{:S(2)}) collective-permute-start(bf16[64,896]{1,0:T(8,128)(2,1)S(1)} %get-tuple-element.29.refs_0_.refs_1_), channel_id=1, source_target_pairs={{0,1},{1,0},{2,3},{3,2},{4,5},{5,4},{6,7},{7,6},{8,9},{9,8},{10,11... | collective-permute-start | bytes 344072 | tf_op jit(solution)/shard_map/ppermute | solution.py:56
  10.0 12.4 %collective-permute-start.9 = (bf16[272,768]{1,0:T(8,128)(2,1)S(1)}, bf16[272,768]{1,0:T(8,128)(2,1)S(1)}, u32[]{:S(2)}, u32[]{:S(2)}) collective-permute-start(bf16[272,768]{1,0:T(8,128)(2,1)S(1)} %get-tuple-element.37), channel_id=1, source_target_pairs={{0,34},{34,0},{2,32},{32,2},{1,35},{35,1},{3,33},{33,3},{4,38},{38... | collective-permute-start | bytes 1253384 | tf_op jit(solution)/shard_map/ppermute | solution.py:60
  14.7 6.8 %collective-permute-start.4 = (bf16[128,896]{1,0:T(8,128)(2,1)S(1)}, bf16[128,896]{1,0:T(8,128)(2,1)S(1)}, u32[]{:S(2)}, u32[]{:S(2)}) collective-permute-start(bf16[128,896]{1,0:T(8,128)(2,1)S(1)} %pad_maximum_fusion.refs_0_.refs_2_.refs_3_), channel_id=1, source_target_pairs={{1,5},{5,9},{9,13},{13,17},{17,21},{21,25},{25,29},{29,1},{0,28},{... | collective-permute-start | bytes 688136 | tf_op jit(solution)/shard_map/ppermute | solution.py:45
  14.8 16.0 %collective-permute-start.6 = (bf16[256,768]{1,0:T(8,128)(2,1)S(1)}, bf16[256,768]{1,0:T(8,128)(2,1)S(1)}, u32[]{:S(2)}, u32[]{:S(2)}) collective-permute-start(bf16[256,768]{1,0:T(8,128)(2,1)S(1)} %constant_dynamic-slice_fusion), channel_id=1, source_target_pairs={{0,34},{34,0},{2,32},{32,2},{1,35},{35,1},{3,33},{33,3},{4,38},{38... | collective-permute-start | bytes 1179656 | tf_op jit(solution)/shard_map/ppermute | solution.py:60
  17.8 5.9 %collective-permute-start.3 = (bf16[128,896]{1,0:T(8,128)(2,1)S(1)}, bf16[128,896]{1,0:T(8,128)(2,1)S(1)}, u32[]{:S(2)}, u32[]{:S(2)}) collective-permute-start(bf16[128,896]{1,0:T(8,128)(2,1)S(1)} %pad_maximum_fusion.refs_0_.refs_2_.refs_3_), channel_id=1, source_target_pairs={{0,1},{1,0},{2,3},{3,2},{4,5},{5,4},{6,7},{7,6},{8,9},{9,8},{10,11... | collective-permute-start | bytes 688136 | tf_op jit(solution)/shard_map/ppermute | solution.py:56
  21.5 7.1 %collective-permute-start.7 = (bf16[128,896]{1,0:T(8,128)(2,1)S(1)}, bf16[128,896]{1,0:T(8,128)(2,1)S(1)}, u32[]{:S(2)}, u32[]{:S(2)}) collective-permute-start(bf16[128,896]{1,0:T(8,128)(2,1)S(1)} %collective-permute-done.4.refs_4_.refs_5_), channel_id=1, source_target_pairs={{1,5},{5,9},{9,13},{13,17},{17,21},{21,25},{25,29},{29,1},{0,28},{... | collective-permute-start | bytes 688136 | tf_op jit(solution)/shard_map/ppermute | solution.py:45
  22.4 14.5 %collective-permute-start.12 = (bf16[272,768]{1,0:T(8,128)(2,1)S(1)}, bf16[272,768]{1,0:T(8,128)(2,1)S(1)}, u32[]{:S(2)}, u32[]{:S(2)}) collective-permute-start(bf16[272,768]{1,0:T(8,128)(2,1)S(1)} %collective-permute-done.9.refs_9_.refs_11_), channel_id=1, source_target_pairs={{0,32},{32,0},{1,33},{33,1},{2,34},{34,2},{3,35},{35,3},{4,36},{36... | collective-permute-start | bytes 1253384 | tf_op jit(solution)/shard_map/ppermute | solution.py:64
  22.4 14.5 %collective-permute-start.11 = (bf16[272,768]{1,0:T(8,128)(2,1)S(1)}, bf16[272,768]{1,0:T(8,128)(2,1)S(1)}, u32[]{:S(2)}, u32[]{:S(2)}) collective-permute-start(bf16[272,768]{1,0:T(8,128)(2,1)S(1)} %collective-permute-done.9.refs_9_.refs_11_), channel_id=1, source_target_pairs={{0,64},{64,0},{128,192},{192,128},{1,65},{65,1},{129,193},{193,129... | collective-permute-start | bytes 1253384 | tf_op jit(solution)/shard_map/ppermute | solution.py:68
  23.7 7.1 %collective-permute-start.5 = (bf16[128,896]{1,0:T(8,128)(2,1)S(1)}, bf16[128,896]{1,0:T(8,128)(2,1)S(1)}, u32[]{:S(2)}, u32[]{:S(2)}) collective-permute-start(bf16[128,896]{1,0:T(8,128)(2,1)S(1)} %collective-permute-done.4.refs_4_.refs_5_), channel_id=1, source_target_pairs={{0,1},{1,0},{2,3},{3,2},{4,5},{5,4},{6,7},{7,6},{8,9},{9,8},{10,11... | collective-permute-start | bytes 688136 | tf_op jit(solution)/shard_map/ppermute | solution.py:56
  28.6 2.2 %collective-permute-start.8 = (bf16[128,896]{1,0:T(8,128)(2,1)S(1)}, bf16[128,896]{1,0:T(8,128)(2,1)S(1)}, u32[]{:S(2)}, u32[]{:S(2)}) collective-permute-start(bf16[128,896]{1,0:T(8,128)(2,1)S(1)} %collective-permute-done.7.refs_6_.refs_7_), channel_id=1, source_target_pairs={{0,1},{1,0},{2,3},{3,2},{4,5},{5,4},{6,7},{7,6},{8,9},{9,8},{10,11... | collective-permute-start | bytes 688136 | tf_op jit(solution)/shard_map/ppermute | solution.py:56
  30.9 6.1 %collective-permute-start.10 = (bf16[128,896]{1,0:T(8,128)(2,1)S(1)}, bf16[128,896]{1,0:T(8,128)(2,1)S(1)}, u32[]{:S(2)}, u32[]{:S(2)}) collective-permute-start(bf16[128,896]{1,0:T(8,128)(2,1)S(1)} %collective-permute-done.7.refs_6_.refs_7_), channel_id=1, source_target_pairs={{1,5},{5,9},{9,13},{13,17},{17,21},{21,25},{25,29},{29,1},{0,28},{... | collective-permute-start | bytes 688136 | tf_op jit(solution)/shard_map/ppermute | solution.py:45
  36.9 16.1 %copy-start.1 = (f32[1024]{0:T(1024)S(1)}, f32[1024]{0:T(1024)}, u32[]{:S(2)}) copy-start(f32[1024]{0:T(1024)} %param.8) | copy-start | bytes 12292

commit v7 on v6

--- a/solution.py
+++ b/solution.py
@@ -495,9 +495,10 @@
             unit, lses[0], src_sq = lax.optimization_barrier((following, lse, src_sq))
         else:
             unit, lses[1] = lax.optimization_barrier((following, lse))
-            groups[-1], opposite = lax.optimization_barrier((groups[-1], opposite))
-    groups += [unit, other_core(unit)]
     following = onward(unit)
+    swapped = other_core(unit)
+    swapped, opposite = lax.optimization_barrier((swapped, opposite))
+    groups += [unit, swapped]
     cross, lse, first_cross, first_lse, faced_logw = row_pass(
         groups, sources, [straight, opposite], 4
     )

time: 72 us -> 72 us (level)
  starting transfers between devices: 19.6 us -> 17.1 us
  waiting for transfers between devices: 8.2 us -> 10.7 us
    ppermute x4, waiting for transfers between devices: 5.25 us -> 7.84 us  [onward(): return lax.ppermute(value, ('z', 'core'), up + down)]
    ppermute x4, starting transfers between devices: 6.07 us -> 3.57 us  [other_core(): return lax.ppermute(value, 'core', [(0, 1), (1, 0)])]
  transfers between devices with their start and end apart: 13 -> 13, of which waited for: 4 -> 5; matrix products, arithmetic and copies ran while one was open for 1% -> 1% of each run, Pallas kernels for 8% -> 8%
where the time goes in v7:
time: 72 us; the launch traced here: 71.8 us
  blocking collectives  27.4 us (38%)
  starting transfers between devices  17.1 us (24%)
  Pallas kernels  14.6 us (20%)
  waiting for transfers between devices  10.7 us (15%)
  other arithmetic  1.02 us (1%)
  between operations  0.78 us (1%)
    all_to_all x1, blocking collectives, on_device(): gathered = lax.all_to_all(columns, ('z', 'core'), 0, 0, tiled=True)  14.2 us
    all_to_all x1, blocking collectives, on_device(): partial = lax.all_to_all(shared, ('y', 'x_lo', 'x_hi'), 0, 0, tiled=True)  13.2 us
    ppermute x4, waiting for transfers between devices, onward(): return lax.ppermute(value, ('z', 'core'), up + down)  7.84 us
    ppermute x1, starting transfers between devices, onward_across(): return lax.ppermute(value, ('z', 'core'), up + down)  7.05 us
    pallas_call x3, Pallas kernels, row_pass(): pl.pallas_call(body, in_specs=[IN_VMEM] * (count + 1 + parts), out_specs=...  6.1 us
    ppermute x2, starting transfers between devices, facing(): lax.ppermute(value, ('x_lo', 'x_hi'), [(0, 3), (3, 0), (1, 2), (2, 1)])  5.04 us
    pallas_call x1, Pallas kernels, column_pass(): pl.pallas_call(body, in_specs=[IN_SMEM] + [IN_HBM] * (len(own_crosses) +...  4.01 us
    ppermute x4, starting transfers between devices, other_core(): return lax.ppermute(value, 'core', [(0, 1), (1, 0)])  3.57 us
  transfers between devices with their start and end apart: 13, of which 5 were waited for; matrix products, arithmetic and copies ran while one was open for 1% of the time, Pallas kernels for 8%

profile of v7, /device:TPU:1, one launch (start us, length us, event | category | flops | bytes accessed | tf_op | source)
XLA Modules:
  0.0 71.8 jit_solution(13469050812180526311)
XLA Ops:
  0.6 0.0 copy-start
  0.7 0.1 stack.32.place_ref.refs_0_
  0.7 1.7 %pack.1 = (bf16[64,896]{1,0:T(8,128)(2,1)S(1)}, f32[1,64]{1,0:T(1,128)S(1)}, bf16[272,768]{1,0:T(8,128)(2,1)S(1)}) custom-call(s32[8]{0:T(128)S(1)} %stack.32.place_ref.refs_0_, bf16[1024,768]{1,0:T(8,128)(2,1)} %refs_10_.1, bf16[64,768]{1,0:T(8,128)(2,1)} %tgt_hbm.1, f32[1,64]{1,0:T(1,128)} %bitcast.19, f32[1,64]{1,0:T(1,128)} %bitcast.20, f32[1,1024]{1,0:T(1,128)} %bitcast.15), custom_call_target="tpu_custom_call" | custom-call | tf_op jit(solution)/shard_map/pack/pallas_call | solution.py:139
  2.4 7.1 %collective-permute-start.2 = (bf16[64,896]{1,0:T(8,128)(2,1)S(1)}, bf16[64,896]{1,0:T(8,128)(2,1)S(1)}, u32[]{:S(2)}, u32[]{:S(2)}) collective-permute-start(bf16[64,896]{1,0:T(8,128)(2,1)S(1)} %get-tuple-element.29.refs_0_.refs_1_), channel_id=1, source_target_pairs={{0,5},{4,9},{8,13},{12,17},{16,21},{20,25},{24,29},{28,1},{1,28},{... | collective-permute-start | bytes 344072 | tf_op jit(solution)/shard_map/ppermute | solution.py:52
  9.5 0.0 collective-permute-start.1
  9.5 0.5 collective-permute-start
  10.0 2.5 %collective-permute-start.9 = (bf16[272,768]{1,0:T(8,128)(2,1)S(1)}, bf16[272,768]{1,0:T(8,128)(2,1)S(1)}, u32[]{:S(2)}, u32[]{:S(2)}) collective-permute-start(bf16[272,768]{1,0:T(8,128)(2,1)S(1)} %get-tuple-element.37), channel_id=1, source_target_pairs={{0,34},{34,0},{2,32},{32,2},{1,35},{35,1},{3,33},{33,3},{4,38},{38... | collective-permute-start | bytes 1253384 | tf_op jit(solution)/shard_map/ppermute | solution.py:60
  12.5 0.0 collective-permute-done.2
  12.5 2.2 %collective-permute-done.1 = bf16[64,896]{1,0:T(8,128)(2,1)S(1)} collective-permute-done((bf16[64,896]{1,0:T(8,128)(2,1)S(1)}, bf16[64,896]{1,0:T(8,128)(2,1)S(1)}, u32[]{:S(2)}, u32[]{:S(2)}) %collective-permute-start.1) | collective-permute-done | bytes 114720 | tf_op jit(solution)/shard_map/ppermute | solution.py:45
  14.7 0.1 collective-permute-start.4
  14.8 0.0 copy-done
  14.8 2.6 %collective-permute-start.8 = (bf16[256,768]{1,0:T(8,128)(2,1)S(1)}, bf16[256,768]{1,0:T(8,128)(2,1)S(1)}, u32[]{:S(2)}, u32[]{:S(2)}) collective-permute-start(bf16[256,768]{1,0:T(8,128)(2,1)S(1)} %constant_dynamic-slice_fusion), channel_id=1, source_target_pairs={{0,34},{34,0},{2,32},{32,2},{1,35},{35,1},{3,33},{33,3},{4,38},{38... | collective-permute-start | bytes 1179656 | tf_op jit(solution)/shard_map/ppermute | solution.py:60
  17.4 0.4 multiply_reduce_fusion
  17.8 2.2 %collective-permute-start.3 = (bf16[128,896]{1,0:T(8,128)(2,1)S(1)}, bf16[128,896]{1,0:T(8,128)(2,1)S(1)}, u32[]{:S(2)}, u32[]{:S(2)}) collective-permute-start(bf16[128,896]{1,0:T(8,128)(2,1)S(1)} %pad_maximum_fusion.refs_0_.refs_2_.refs_3_), channel_id=1, source_target_pairs={{0,1},{1,0},{2,3},{3,2},{4,5},{5,4},{6,7},{7,6},{8,9},{9,8},{10,11... | collective-permute-start | bytes 688136 | tf_op jit(solution)/shard_map/ppermute | solution.py:56
  20.0 0.0 collective-permute-done.refs_1_.refs_2_
  20.0 1.5 %rows.3 = (f32[128,1024]{1,0:T(8,128)}, f32[1,1024]{1,0:T(1,128)S(1)}) custom-call(bf16[64,896]{1,0:T(8,128)(2,1)S(1)} %get-tuple-element.29.refs_0_.refs_1_, bf16[64,896]{1,0:T(8,128)(2,1)S(1)} %collective-permute-done.refs_1_.refs_2_, bf16[1024,768]{1,0:T(8,128)(2,1)S(1)} %copy-done), custom_call_target="tpu_custom_call" | custom-call | flops 1 | bytes 1 | tf_op jit(solution)/shard_map/rows/pallas_call | solution.py:264
  21.5 0.0 collective-permute-done.4.refs_4_.refs_5_
  21.5 0.1 collective-permute-start.6
  21.6 0.8 %collective-permute-done.9.refs_9_.refs_11_ = bf16[272,768]{1,0:T(8,128)(2,1)S(1)} collective-permute-done((bf16[272,768]{1,0:T(8,128)(2,1)S(1)}, bf16[272,768]{1,0:T(8,128)(2,1)S(1)}, u32[]{:S(2)}, u32[]{:S(2)}) %collective-permute-start.9) | collective-permute-done | bytes 417824 | tf_op jit(solution)/shard_map/ppermute | solution.py:60
  22.4 0.0 collective-permute-start.12
  22.4 1.3 %collective-permute-start.11 = (bf16[272,768]{1,0:T(8,128)(2,1)S(1)}, bf16[272,768]{1,0:T(8,128)(2,1)S(1)}, u32[]{:S(2)}, u32[]{:S(2)}) collective-permute-start(bf16[272,768]{1,0:T(8,128)(2,1)S(1)} %collective-permute-done.9.refs_9_.refs_11_), channel_id=1, source_target_pairs={{0,64},{64,0},{128,192},{192,128},{1,65},{65,1},{129,193},{193,129... | collective-permute-start | bytes 1253384 | tf_op jit(solution)/shard_map/ppermute | solution.py:68
  23.7 0.0 collective-permute-done.3.refs_1_.refs_3_.refs_4_
  23.7 1.6 %rows.4 = (f32[256,1024]{1,0:T(8,128)}, f32[1,1024]{1,0:T(1,128)S(1)}) custom-call(bf16[128,896]{1,0:T(8,128)(2,1)S(1)} %pad_maximum_fusion.refs_0_.refs_2_.refs_3_, bf16[128,896]{1,0:T(8,128)(2,1)S(1)} %collective-permute-done.3.refs_1_.refs_3_.refs_4_, bf16[1024,768]{1,0:T(8,128)(2,1)S(1)} %copy-done), custom_call_target="tpu_custom_call" | custom-call | flops 1 | bytes 1 | tf_op jit(solution)/shard_map/rows/pallas_call | solution.py:264
  25.4 2.6 %collective-permute-done.6.refs_6_.refs_7_ = bf16[128,896]{1,0:T(8,128)(2,1)S(1)} collective-permute-done((bf16[128,896]{1,0:T(8,128)(2,1)S(1)}, bf16[128,896]{1,0:T(8,128)(2,1)S(1)}, u32[]{:S(2)}, u32[]{:S(2)}) %collective-permute-start.6) | collective-permute-done | bytes 229408 | tf_op jit(solution)/shard_map/ppermute | solution.py:45
  28.0 0.8 %collective-permute-start.7 = (bf16[128,896]{1,0:T(8,128)(2,1)S(1)}, bf16[128,896]{1,0:T(8,128)(2,1)S(1)}, u32[]{:S(2)}, u32[]{:S(2)}) collective-permute-start(bf16[128,896]{1,0:T(8,128)(2,1)S(1)} %collective-permute-done.6.refs_6_.refs_7_), channel_id=1, source_target_pairs={{0,1},{1,0},{2,3},{3,2},{4,5},{5,4},{6,7},{7,6},{8,9},{9,8},{10,11... | collective-permute-start | bytes 688136 | tf_op jit(solution)/shard_map/ppermute | solution.py:56
  28.7 0.1 collective-permute-start.5
  28.8 2.0 %collective-permute-done.8.refs_10_.refs_12_ = bf16[256,768]{1,0:T(8,128)(2,1)S(1)} collective-permute-done((bf16[256,768]{1,0:T(8,128)(2,1)S(1)}, bf16[256,768]{1,0:T(8,128)(2,1)S(1)}, u32[]{:S(2)}, u32[]{:S(2)}) %collective-permute-start.8) | collective-permute-done | bytes 393248 | tf_op jit(solution)/shard_map/ppermute | solution.py:60
  30.9 0.0 collective-permute-start.10
  30.9 0.0 collective-permute-done.7.refs_7_.refs_8_
  30.9 0.0 collective-permute-done.5.refs_5_.refs_6_
  30.9 3.0 %rows.5 = (f32[512,1024]{1,0:T(8,128)}, f32[1,1024]{1,0:T(1,128)S(1)}, f32[896,512]{1,0:T(8,128)}, f32[1,512]{1,0:T(1,128)S(1)}, f32[1,1024]{1,0:T(1,128)S(1)}) custom-call(bf16[64,896]{1,0:T(8,128)(2,1)S(1)} %get-tuple-element.29.refs_0_.refs_1_, bf16[64,896]{1,0:T(8,128)(2,1)S(1)} %collective-permute-done.refs_1_.refs_2_, ...), custom_call_target="tpu_custom_call" | custom-call | flops 1 | bytes 1 | tf_op jit(solution)/shard_map/rows/pallas_call | solution.py:264
  33.9 3.1 %collective-permute-done.10.refs_9_ = bf16[128,896]{1,0:T(8,128)(2,1)S(1)} collective-permute-done((bf16[128,896]{1,0:T(8,128)(2,1)S(1)}, bf16[128,896]{1,0:T(8,128)(2,1)S(1)}, u32[]{:S(2)}, u32[]{:S(2)}) %collective-permute-start.10) | collective-permute-done | bytes 229408 | tf_op jit(solution)/shard_map/ppermute | solution.py:45
  36.9 0.0 copy-start.1
  36.9 0.0 collective-permute-done.12.refs_14_
  36.9 0.0 collective-permute-done.11.refs_13_
  37.0 2.8 %last_rows.1 = (f32[128,1536]{1,0:T(8,128)S(1)}, f32[1024,512]{1,0:T(8,128)S(1)}, f32[16,1,2048]{2,1,0:T(1,128)S(1)}) custom-call(s32[8]{0:T(128)S(1)} %stack.32.place_ref.refs_0_, bf16[64,896]{1,0:T(8,128)(2,1)S(1)} %get-tuple-element.29.refs_0_.refs_1_, bf16[64,896]{1,0:T(8,128)(2,1)S(1)} %collective-permute-done.refs_1_.refs_2_, ...), custom_call_target="tpu_custom_call" | custom-call | flops 1107296256 | bytes 6029312 | tf_op jit(solution)/shard_map/last_rows/pallas_call | solution.py:314
  39.8 13.2 %all_to_all.10.refs_7_ = f32[16,1,2048]{2,1,0:T(1,128)S(1)} all-to-all(f32[16,1,2048]{2,1,0:T(1,128)S(1)} %get-tuple-element.50), channel_id=1, replica_groups=mesh['y'=4,'x_lo'=2,'z'=8,'x_hi'=2,'core'=2] {'y','x_lo','x_hi'}, dimensions={0} | all-to-all | bytes 262144 | tf_op jit(solution)/shard_map/all_to_all | solution.py:513
  53.0 0.0 copy-done.1
  53.0 4.0 %columns.1 = (f32[16,1,64]{2,1,0:T(1,128)S(1)}, f32[1,1024]{1,0:T(1,128)}) custom-call(s32[8]{0:T(128)S(1)} %stack.32.place_ref.refs_0_, f32[128,1024]{1,0:T(8,128)} %get-tuple-element.30.refs_1_, f32[256,1024]{1,0:T(8,128)} %get-tuple-element.31.refs_2_, f32[512,1024]{1,0:T(8,128)} %get-tuple-element.39.refs_3_, f32[896,512]{1,0:T(8,128)} %get-tuple-element.40.refs_4_, ...), custom_call_target="tpu_custom_call" | custom-call | flops 12582912 | bytes 8388608 | tf_op jit(solution)/shard_map/columns/pallas_call | solution.py:429
  57.0 14.2 %all_to_all.11 = f32[16,1,64]{2,1,0:T(1,128)S(1)} all-to-all(f32[16,1,64]{2,1,0:T(1,128)S(1)} %get-tuple-element.55), channel_id=1, replica_groups=mesh['y'=4,'x_lo'=2,'z'=8,'x_hi'=2,'core'=2] {'z','core'}, dimensions={0} | all-to-all | bytes 8192 | tf_op jit(solution)/shard_map/all_to_all | solution.py:517
  71.3 0.5 bitcast_subtract_fusion
  (5 shorter events, 0.1 us)
Async XLA Ops:
  0.6 14.2 %copy-start = (bf16[1024,768]{1,0:T(8,128)(2,1)S(1)}, bf16[1024,768]{1,0:T(8,128)(2,1)}, u32[]{:S(2)}) copy-start(bf16[1024,768]{1,0:T(8,128)(2,1)} %refs_10_.1) | copy-start | bytes 4718596
  2.4 10.0 %collective-permute-start.2 = (bf16[64,896]{1,0:T(8,128)(2,1)S(1)}, bf16[64,896]{1,0:T(8,128)(2,1)S(1)}, u32[]{:S(2)}, u32[]{:S(2)}) collective-permute-start(bf16[64,896]{1,0:T(8,128)(2,1)S(1)} %get-tuple-element.29.refs_0_.refs_1_), channel_id=1, source_target_pairs={{0,5},{4,9},{8,13},{12,17},{16,21},{20,25},{24,29},{28,1},{1,28},{... | collective-permute-start | bytes 344072 | tf_op jit(solution)/shard_map/ppermute | solution.py:52
  9.5 5.1 %collective-permute-start.1 = (bf16[64,896]{1,0:T(8,128)(2,1)S(1)}, bf16[64,896]{1,0:T(8,128)(2,1)S(1)}, u32[]{:S(2)}, u32[]{:S(2)}) collective-permute-start(bf16[64,896]{1,0:T(8,128)(2,1)S(1)} %get-tuple-element.29.refs_0_.refs_1_), channel_id=1, source_target_pairs={{1,5},{5,9},{9,13},{13,17},{17,21},{21,25},{25,29},{29,1},{0,28},{... | collective-permute-start | bytes 344072 | tf_op jit(solution)/shard_map/ppermute | solution.py:45
  9.5 10.5 %collective-permute-start = (bf16[64,896]{1,0:T(8,128)(2,1)S(1)}, bf16[64,896]{1,0:T(8,128)(2,1)S(1)}, u32[]{:S(2)}, u32[]{:S(2)}) collective-permute-start(bf16[64,896]{1,0:T(8,128)(2,1)S(1)} %get-tuple-element.29.refs_0_.refs_1_), channel_id=1, source_target_pairs={{0,1},{1,0},{2,3},{3,2},{4,5},{5,4},{6,7},{7,6},{8,9},{9,8},{10,11... | collective-permute-start | bytes 344072 | tf_op jit(solution)/shard_map/ppermute | solution.py:56
  10.0 12.4 %collective-permute-start.9 = (bf16[272,768]{1,0:T(8,128)(2,1)S(1)}, bf16[272,768]{1,0:T(8,128)(2,1)S(1)}, u32[]{:S(2)}, u32[]{:S(2)}) collective-permute-start(bf16[272,768]{1,0:T(8,128)(2,1)S(1)} %get-tuple-element.37), channel_id=1, source_target_pairs={{0,34},{34,0},{2,32},{32,2},{1,35},{35,1},{3,33},{33,3},{4,38},{38... | collective-permute-start | bytes 1253384 | tf_op jit(solution)/shard_map/ppermute | solution.py:60
  14.7 6.8 %collective-permute-start.4 = (bf16[128,896]{1,0:T(8,128)(2,1)S(1)}, bf16[128,896]{1,0:T(8,128)(2,1)S(1)}, u32[]{:S(2)}, u32[]{:S(2)}) collective-permute-start(bf16[128,896]{1,0:T(8,128)(2,1)S(1)} %pad_maximum_fusion.refs_0_.refs_2_.refs_3_), channel_id=1, source_target_pairs={{1,5},{5,9},{9,13},{13,17},{17,21},{21,25},{25,29},{29,1},{0,28},{... | collective-permute-start | bytes 688136 | tf_op jit(solution)/shard_map/ppermute | solution.py:45
  14.8 16.0 %collective-permute-start.8 = (bf16[256,768]{1,0:T(8,128)(2,1)S(1)}, bf16[256,768]{1,0:T(8,128)(2,1)S(1)}, u32[]{:S(2)}, u32[]{:S(2)}) collective-permute-start(bf16[256,768]{1,0:T(8,128)(2,1)S(1)} %constant_dynamic-slice_fusion), channel_id=1, source_target_pairs={{0,34},{34,0},{2,32},{32,2},{1,35},{35,1},{3,33},{33,3},{4,38},{38... | collective-permute-start | bytes 1179656 | tf_op jit(solution)/shard_map/ppermute | solution.py:60
  17.8 5.9 %collective-permute-start.3 = (bf16[128,896]{1,0:T(8,128)(2,1)S(1)}, bf16[128,896]{1,0:T(8,128)(2,1)S(1)}, u32[]{:S(2)}, u32[]{:S(2)}) collective-permute-start(bf16[128,896]{1,0:T(8,128)(2,1)S(1)} %pad_maximum_fusion.refs_0_.refs_2_.refs_3_), channel_id=1, source_target_pairs={{0,1},{1,0},{2,3},{3,2},{4,5},{5,4},{6,7},{7,6},{8,9},{9,8},{10,11... | collective-permute-start | bytes 688136 | tf_op jit(solution)/shard_map/ppermute | solution.py:56
  21.5 6.5 %collective-permute-start.6 = (bf16[128,896]{1,0:T(8,128)(2,1)S(1)}, bf16[128,896]{1,0:T(8,128)(2,1)S(1)}, u32[]{:S(2)}, u32[]{:S(2)}) collective-permute-start(bf16[128,896]{1,0:T(8,128)(2,1)S(1)} %collective-permute-done.4.refs_4_.refs_5_), channel_id=1, source_target_pairs={{1,5},{5,9},{9,13},{13,17},{17,21},{21,25},{25,29},{29,1},{0,28},{... | collective-permute-start | bytes 688136 | tf_op jit(solution)/shard_map/ppermute | solution.py:45
  22.4 14.5 %collective-permute-start.12 = (bf16[272,768]{1,0:T(8,128)(2,1)S(1)}, bf16[272,768]{1,0:T(8,128)(2,1)S(1)}, u32[]{:S(2)}, u32[]{:S(2)}) collective-permute-start(bf16[272,768]{1,0:T(8,128)(2,1)S(1)} %collective-permute-done.9.refs_9_.refs_11_), channel_id=1, source_target_pairs={{0,32},{32,0},{1,33},{33,1},{2,34},{34,2},{3,35},{35,3},{4,36},{36... | collective-permute-start | bytes 1253384 | tf_op jit(solution)/shard_map/ppermute | solution.py:64
  22.4 14.5 %collective-permute-start.11 = (bf16[272,768]{1,0:T(8,128)(2,1)S(1)}, bf16[272,768]{1,0:T(8,128)(2,1)S(1)}, u32[]{:S(2)}, u32[]{:S(2)}) collective-permute-start(bf16[272,768]{1,0:T(8,128)(2,1)S(1)} %collective-permute-done.9.refs_9_.refs_11_), channel_id=1, source_target_pairs={{0,64},{64,0},{128,192},{192,128},{1,65},{65,1},{129,193},{193,129... | collective-permute-start | bytes 1253384 | tf_op jit(solution)/shard_map/ppermute | solution.py:68
  28.0 2.9 %collective-permute-start.7 = (bf16[128,896]{1,0:T(8,128)(2,1)S(1)}, bf16[128,896]{1,0:T(8,128)(2,1)S(1)}, u32[]{:S(2)}, u32[]{:S(2)}) collective-permute-start(bf16[128,896]{1,0:T(8,128)(2,1)S(1)} %collective-permute-done.6.refs_6_.refs_7_), channel_id=1, source_target_pairs={{0,1},{1,0},{2,3},{3,2},{4,5},{5,4},{6,7},{7,6},{8,9},{9,8},{10,11... | collective-permute-start | bytes 688136 | tf_op jit(solution)/shard_map/ppermute | solution.py:56
  28.7 2.1 %collective-permute-start.5 = (bf16[128,896]{1,0:T(8,128)(2,1)S(1)}, bf16[128,896]{1,0:T(8,128)(2,1)S(1)}, u32[]{:S(2)}, u32[]{:S(2)}) collective-permute-start(bf16[128,896]{1,0:T(8,128)(2,1)S(1)} %collective-permute-done.4.refs_4_.refs_5_), channel_id=1, source_target_pairs={{0,1},{1,0},{2,3},{3,2},{4,5},{5,4},{6,7},{7,6},{8,9},{9,8},{10,11... | collective-permute-start | bytes 688136 | tf_op jit(solution)/shard_map/ppermute | solution.py:56
  30.9 6.1 %collective-permute-start.10 = (bf16[128,896]{1,0:T(8,128)(2,1)S(1)}, bf16[128,896]{1,0:T(8,128)(2,1)S(1)}, u32[]{:S(2)}, u32[]{:S(2)}) collective-permute-start(bf16[128,896]{1,0:T(8,128)(2,1)S(1)} %collective-permute-done.6.refs_6_.refs_7_), channel_id=1, source_target_pairs={{1,5},{5,9},{9,13},{13,17},{17,21},{21,25},{25,29},{29,1},{0,28},{... | collective-permute-start | bytes 688136 | tf_op jit(solution)/shard_map/ppermute | solution.py:45
  36.9 16.1 %copy-start.1 = (f32[1024]{0:T(1024)S(1)}, f32[1024]{0:T(1024)}, u32[]{:S(2)}) copy-start(f32[1024]{0:T(1024)} %param.8) | copy-start | bytes 12292
